TPU v7x, 32 devices: a whole 2x2x4 slice. The times are simulated.
32 devices in a mesh: parts: 2 (over x), ep: 16 (over z, y, core), tp: 1.
Axes of the slice: x: 2, y: 2, z: 4, core: 2. Of those that a mesh axis runs over, the one named last changes fastest.
Arguments:
- resid: bfloat16 [512, 3584], P(('parts', 'ep', 'tp')), parts along dimension 0, may hold values from -40 to 40
- norm_gain: float32 [3584], replicated, may hold values from 0.1 to 1.9
- expert_ids: int32 [512, 8], P(('parts', 'ep')), parts along dimension 0, may hold values from 0 to 15, all different within a row; in each aligned block of 16 rows (0 to 15, 16 to 31, ...) at most 16 rows name the same one
- route_weights: bfloat16 [512, 8], P(('parts', 'ep')), parts along dimension 0, may hold values from 0.099609375 to 0.59765625
- gate_up: bfloat16 [16, 3584, 2, 1024], P('ep', None, None, 'tp'), may hold values from -0.09375 to 0.09375
- down: bfloat16 [16, 1024, 3584], P('ep', 'tp'), may hold values from -0.1875 to 0.1875
Outputs:
- layer_out: bfloat16 [512, 3584], P(('parts', 'ep', 'tp')), parts along dimension 0
There are 2 independent parts, one for each index of `parts`. A program takes and returns all parts, laid end to end along the dimension named above; an argument that names none is the same for every part. Nothing has to cross between parts.
Inputs may be any that keep to these rules, and one draw needn't show every extreme that they name: `expert_ids`: each row names 8 different experts. In each aligned block of 16 rows (the rows of one index of ep) no expert is named by more than 16 rows, and in every draw some expert of some block is named by exactly 16 rows.
All inputs are finite; a program needn't handle non-finite values.
Results may differ from a plain program's by a relative error of at most 0.0045.
Values may be sent and summed in bfloat16 or wider, within the bound.
No kernel may reach another device: no remote copies, remote signals or barrier semaphores. Data moves between devices by JAX's collectives and lax.ppermute only.
A program may use at most 128 MiB of HBM per device.

v0:
```python
import jax
import jax.numpy as jnp
from jax import lax
from jax.sharding import PartitionSpec as P

eps = 1e-06


def expert_rows(rows, weights_gu, weights_down):
    inner = weights_down.shape[0]
    both = jnp.dot(rows, weights_gu, preferred_element_type=jnp.float32)
    hidden = (jax.nn.silu(both[:, :inner]) * both[:, inner:]).astype(jnp.bfloat16)
    return jnp.dot(hidden, weights_down, preferred_element_type=jnp.float32).astype(jnp.bfloat16)


def slot_tables(hits, capacity):
    count = hits.shape[1]
    before = jnp.cumsum(hits, axis=1) - hits
    slots = jnp.arange(capacity, dtype=jnp.int32)
    match = (hits[:, :, None] == 1) & (before[:, :, None] == slots[None, None, :])
    source = jnp.sum(
        match.astype(jnp.int32) * jnp.arange(count, dtype=jnp.int32)[None, :, None], axis=1
    )
    filled = jnp.any(match, axis=1)
    return (before, source, filled)


def shards(resid, norm_gain, expert_ids, route_weights, gate_up, down):
    values = resid.astype(jnp.float32)
    scale = lax.rsqrt(jnp.mean(values * values, axis=-1, keepdims=True) + eps)
    normed = (values * scale * norm_gain).astype(jnp.bfloat16)
    width = resid.shape[1]
    owners = lax.axis_size("ep")
    normed_all = lax.all_gather(normed, "tp", axis=0, tiled=True)
    group = normed_all.shape[0]
    chosen = expert_ids.shape[1]
    capacity = min(group, 2 * group * chosen // owners)
    weights_gu = gate_up[0].reshape(width, -1)
    weights_down = down[0]
    everything, weights_all = (
        lax.all_gather(normed_all, "ep", axis=0, tiled=True),
        lax.all_gather(route_weights, "ep", axis=0, tiled=True),
    )
    ids_all = lax.all_gather(expert_ids, "ep", axis=0, tiled=True)
    owner = lax.axis_index("ep")
    blocks = ids_all.reshape(owners, group, chosen)
    hits = jnp.any(blocks == owner, axis=-1).astype(jnp.int32)
    before, source, filled = slot_tables(hits, capacity)
    offsets = (jnp.arange(owners, dtype=jnp.int32) * group)[:, None]
    buffer = jnp.where(
        filled[:, :, None], everything[source + offsets], jnp.zeros((), jnp.bfloat16)
    )
    done = expert_rows(buffer.reshape(owners * capacity, width), weights_gu, weights_down)
    flat_slot = jnp.arange(owners, dtype=jnp.int32)[:, None] * capacity + jnp.minimum(
        before, capacity - 1
    )
    picked = done[flat_slot].reshape(owners * group, width)
    share = jnp.sum(jnp.where(ids_all == owner, weights_all.astype(jnp.float32), 0.0), axis=-1)
    terms = share[:, None] * picked.astype(jnp.float32)
    mine = lax.psum_scatter(terms, ("ep", "tp"), scatter_dimension=0, tiled=True)
    return (values + mine).astype(jnp.bfloat16)


def solution(mesh):
    return jax.shard_map(
        shards,
        mesh=mesh,
        in_specs=(
            P(("parts", "ep", "tp"), None),
            P(),
            P(("parts", "ep"), None),
            P(("parts", "ep"), None),
            P("ep", None, None, "tp"),
            P("ep", "tp", None),
        ),
        out_specs=P(("parts", "ep", "tp"), None),
        check_vma=False,
    )
```

profile of v0, /device:TPU:0, one launch (start us, length us, event | category | flops | bytes accessed | tf_op | source)
XLA Modules:
  0.0 165.5 jit_solution(7563507417672208540)
XLA Ops:
  6.5 0.0 all-gather.4.cloned.1.call-start
  6.5 1.0 fusion.8
  7.6 1.6 fusion.10
  9.2 0.0 all-gather.4.cloned.1.call-update
  9.3 0.0 reduce-scatter.2.cloned.1.call-start
  9.3 23.6 %all-gather.1 = bf16[16,16,8]{1,2,0:T(8,128)(2,1)S(1)} all-gather(bf16[1,16,8]{1,2,0:T(8,128)(2,1)} %bitcast.31), channel_id=1, replica_groups=mesh['parts'=2,'ep'=16,'tp'=1] {'ep'}, dimensions={0}, use_global_device_ids=true | all-gather | bytes 4352 | tf_op jit(solution)/shard_map/all_gather | solution.py:42
  32.9 18.1 %all-gather = s32[16,16,8]{1,2,0:T(8,128)S(1)} all-gather(s32[1,16,8]{1,2,0:T(8,128)} %bitcast.30), channel_id=1, replica_groups=mesh['parts'=2,'ep'=16,'tp'=1] {'ep'}, dimensions={0}, use_global_device_ids=true | all-gather | bytes 8704 | tf_op jit(solution)/shard_map/all_gather | solution.py:44
  51.0 0.1 reshape.197
  51.1 0.2 reduce_window_sum.13
  51.3 0.1 compare_select_fusion
  51.4 0.1 reshape.176
  51.5 0.2 select_reduce_fusion
  51.6 0.1 compare_select_fusion.1
  51.7 0.1 reshape.168
  51.8 16.1 %copy.7 = bf16[448,8,2,1024]{3,1,2,0:T(8,128)(2,1)} copy(bf16[448,8,2,1024]{3,2,1,0:T(2,128)(2,1)} %bitcast.26) | data formatting | bytes 29360128
  67.9 0.2 fusion.13
  68.1 0.0 all-gather.4.cloned.1.call-done
  68.1 5.3 %gather_fusion = bf16[256,3584]{1,0:T(8,128)(2,1)S(1)} fusion(bf16[256,3584]{1,0:T(8,128)(2,1)} %all-gather.4.cloned.1.call-done, s32[1024]{0:T(1024)S(1)} %pad_clamp_fusion.1), kind=kCustom, calls=%fused_computation | custom fusion | bytes 3671040 | tf_op jit(solution)/shard_map/gather | solution.py:51
  73.4 0.0 slice-start
  73.4 0.2 broadcast_select_fusion
  73.6 0.0 slice-start.1
  73.6 7.4 %fusion.15 = f32[256,2048]{1,0:T(8,128)S(1)} fusion(bf16[256,3584]{1,0:T(8,128)(2,1)S(1)} %bitcast.29, bf16[3584,2048]{1,0:T(8,128)(2,1)} %bitcast.27), kind=kOutput, calls=%fused_computation.34 | convolution fusion | flops 3758096384 | bytes 18612224 | tf_op jit(solution)/shard_map/dot_general | solution.py:11
  81.0 0.0 slice-done
  81.0 0.0 slice-done.1
  81.0 2.1 %fusion.2 = bf16[256,3584]{1,0:T(8,128)(2,1)S(1)} fusion(bf16[1,1024,3584]{2,1,0:T(8,128)(2,1)S(1)} %bitcast.33, f32[256,2048]{1,0:T(8,128)S(1)} %fusion.15), kind=kOutput, calls=%fused_computation.4 | convolution fusion | flops 1881538560 | bytes 11272192 | tf_op jit(solution)/shard_map/dot_general | solution.py:13
  83.1 3.0 %gather_fusion.1 = bf16[256,3584]{1,0:T(8,128)(2,1)} fusion(bf16[256,3584]{1,0:T(8,128)(2,1)S(1)} %fusion.2, s32[1024]{0:T(1024)S(1)} %pad_clamp_fusion), kind=kCustom, calls=%fused_computation.1 | custom fusion | bytes 3671040 | tf_op jit(solution)/shard_map/gather | solution.py:57
  86.1 3.8 %convert_multiply_fusion = f32[256,3584]{1,0:T(8,128)} fusion(bf16[256,3584]{1,0:T(8,128)(2,1)} %gather_fusion.1, f32[256]{0:T(256)S(1)} %reshape.197), kind=kLoop, calls=%fused_computation.5 | loop fusion | flops 1835008 | bytes 5506048 | tf_op jit(solution)/shard_map/mul | solution.py:59
  89.9 0.0 copy-start
  89.9 0.0 reduce-scatter.2.cloned.1.call-update
  89.9 67.2 %reduce-scatter.2.cloned.1.call-done = f32[16,3584]{1,0:T(8,128)} async-done(((f32[256,3584]{1,0:T(8,128)}), f32[16,3584]{1,0:T(8,128)}) %reduce-scatter.2.cloned.1.call-update) | async-done | bytes 229392 | tf_op jit(solution)/shard_map/reduce_scatter | solution.py:60
  157.1 0.0 copy-done
  157.1 1.6 fusion.11
  (8 shorter events, 0.1 us)
Async XLA Ops:
  6.5 61.6 %all-gather.4.cloned.1.call-start = ((), (), s32[]{:S(2)}) async-start(), calls=%async_computation.1 | async-start | bytes 1949696 | tf_op jit(solution)/shard_map/all_gather | solution.py:41
  9.3 147.8 %reduce-scatter.2.cloned.1.call-start = ((), (), s32[]{:S(2)}) async-start(), calls=%async_computation.2 | async-start | bytes 3899392 | tf_op jit(solution)/shard_map/reduce_scatter | solution.py:60
  73.4 7.6 %slice-start = ((s8[7340032]{0:T(1024)(128)(4,1)}), s8[4194304]{0:T(1024)(128)(4,1)S(1)}, s32[]{:S(2)}) async-start(s8[7340032]{0:T(1024)(128)(4,1)} %bitcast.32), calls=%async_computation.3 | async-start | bytes 8388608
  73.6 7.4 %slice-start.1 = ((s8[7340032]{0:T(1024)(128)(4,1)}), s8[3145728]{0:T(1024)(128)(4,1)S(1)}, s32[]{:S(2)}) async-start(s8[7340032]{0:T(1024)(128)(4,1)} %bitcast.32), calls=%async_computation.4 | async-start | bytes 6291456
  89.9 67.2 %copy-start = (bf16[16,3584]{1,0:T(8,128)(2,1)S(1)}, bf16[16,3584]{1,0:T(8,128)(2,1)}, u32[]{:S(2)}) copy-start(bf16[16,3584]{1,0:T(8,128)(2,1)} %param.6) | copy-start | bytes 344068
Sparse Core Ops, SparseCore 0:
  9.6 43.2 all-gather.3
  90.0 66.9 reduce-scatter.1
where the time goes:
time: 166 us
  waiting for transfers between devices  67.2 us (40%)
  blocking collectives  41.7 us (25%)
  local copies, waits for them, and re-layouts  24.6 us (15%)
  between operations  13.5 us (8%)
  matrix products  9.5 us (6%)
  other arithmetic  8.96 us (5%)
    reduce_scatter x1, waiting for transfers between devices, shards(): lax.psum_scatter(terms, ('ep', 'tp'), scatter_dimension=0, tiled=True)  67.2 us
    all_gather x1, blocking collectives, shards(): lax.all_gather(route_weights, 'ep', axis=0, tiled=True)  23.6 us
    all_gather x1, blocking collectives, shards(): ids_all = lax.all_gather(expert_ids, 'ep', axis=0, tiled=True)  18.1 us
    unnamed x7, local copies, waits for them, and re-layouts  16.1 us
    dot_general x1, matrix products, expert_rows(): both = jnp.dot(rows, weights_gu, preferred_element_type=jnp.float32)  7.41 us
    gather x1, local copies, waits for them, and re-layouts, shards(): everything[source + offsets]  5.27 us
    mul x1, other arithmetic, shards(): terms = share[:, None] * picked.astype(jnp.float32)  3.75 us
  transfers between devices with their start and end apart: 2, of which 1 were waited for; matrix products, arithmetic and copies ran while one was open for 10% of the time, Pallas kernels for 0%

commit v1 on v0

v1 whole, which is shorter than its diff:
```python
import jax
import jax.numpy as jnp
from jax import lax
from jax.sharding import PartitionSpec as P

eps = 1e-06


def swap(block, offset):
    count = lax.axis_size("ep")
    return lax.ppermute(block, "ep", [(i, i ^ offset) for i in range(count)])


def gather_blocks(block, far):
    near = {0: block}
    for offset in far:
        near[offset] = swap(block, offset)
    for offset in (0, *far):
        source = block if offset == far[0] else near[offset]
        near[offset ^ 2] = swap(source, offset ^ 2 if offset == far[0] else 2)
    for offset in list(near):
        near[offset ^ 1] = swap(near[offset], 1)
    return near


def shards(resid, norm_gain, expert_ids, route_weights, gate_up, down):
    values = resid.astype(jnp.float32)
    width = resid.shape[1]
    owners = lax.axis_size("ep")
    owner = lax.axis_index("ep")
    far = tuple(range(4, owners, 4))
    scale = lax.rsqrt(jnp.mean(values * values, axis=-1, keepdims=True) + eps)
    normed = (values * scale * norm_gain).astype(jnp.bfloat16)
    normed = lax.all_gather(normed, "tp", axis=0, tiled=True)
    rows = normed.shape[0]
    lanes = jnp.arange(128, dtype=jnp.int32)
    share_all = jnp.sum(
        jnp.where(expert_ids[:, :, None] == lanes, route_weights[:, :, None], 0), axis=1
    ).astype(jnp.bfloat16)
    blocks = gather_blocks(jnp.concatenate([normed, share_all], axis=1), far)
    order = sorted(blocks, key=lambda o: (1 - (o & 1), 1 - (o >> 1 & 1), -o))
    everything = jnp.concatenate([blocks[o] for o in order], axis=0)
    share = jnp.sum(
        jnp.where(lanes == owner, everything[:, width:].astype(jnp.float32), 0.0),
        axis=1,
        keepdims=True,
    )
    weights_gu = gate_up[0].reshape(width, -1)
    inner = down.shape[1]
    both = jnp.dot(everything[:, :width], weights_gu, preferred_element_type=jnp.float32)
    hidden = (jax.nn.silu(both[:, :inner]) * both[:, inner:]).astype(jnp.bfloat16)
    piece = jnp.dot(hidden, down[0], preferred_element_type=jnp.float32).astype(jnp.bfloat16)
    terms = (share * piece.astype(jnp.float32)).astype(jnp.bfloat16)
    place = {o: at for at, o in enumerate(order)}
    half = owners // 2 * rows
    quarter = half // 2
    add = lambda a, b: a.astype(jnp.float32) + b.astype(jnp.float32)
    total = add(swap(terms[:half], 1), terms[half:]).astype(jnp.bfloat16)
    parts = {}
    for at, offset in enumerate(o for o in order if o & 3 == 0):
        away = total[at * rows : (at + 1) * rows]
        here = total[quarter + at * rows : quarter + (at + 1) * rows]
        parts[offset] = add(swap(away, 2), here)
    mine = parts[0]
    for offset in reversed(far):
        mine = mine + swap(parts[offset].astype(jnp.bfloat16), offset).astype(jnp.float32)
    mine = lax.psum_scatter(mine, "tp", scatter_dimension=0, tiled=True)
    return (values + mine).astype(jnp.bfloat16)


def solution(mesh):
    return jax.shard_map(
        shards,
        mesh=mesh,
        in_specs=(
            P(("parts", "ep", "tp"), None),
            P(),
            P(("parts", "ep"), None),
            P(("parts", "ep"), None),
            P("ep", None, None, "tp"),
            P("ep", "tp", None),
        ),
        out_specs=P(("parts", "ep", "tp"), None),
        check_vma=False,
    )
```

time: 166 us -> 82.5 us (0.50)
  blocking collectives: 41.7 us -> 0 us
  waiting for transfers between devices: 67.2 us -> 27.8 us
  starting transfers between devices: 0.04 us -> 23.1 us
  between operations: 13.5 us -> 0.22 us
  local copies, waits for them, and re-layouts: 24.6 us -> 17.9 us
  other arithmetic: 8.96 us -> 3.34 us
    reduce_scatter x1 -> x0, waiting for transfers between devices: 67.2 us -> none  [shards(): lax.psum_scatter(terms, ('ep', 'tp'), scatter_dimension=0, tiled=True)]
    all_gather x2 -> x0, blocking collectives: 41.7 us -> none  [the longest x1 23.6 us: shards(): lax.all_gather(route_weights, 'ep', axis=0, tiled=True)]
    ppermute x0 -> x23, waiting for transfers between devices: none -> 27.8 us  [swap(): return lax.ppermute(block, 'ep', [(i, i ^ offset) for i in range(count)])]
    ppermute x0 -> x23, starting transfers between devices: none -> 23.1 us  [swap(): return lax.ppermute(block, 'ep', [(i, i ^ offset) for i in range(count)])]
    gather x2 -> x0, local copies, waits for them, and re-layouts: 8.24 us -> none  [the longest x1 5.27 us: shards(): everything[source + offsets]]
    mul x2 -> x0, other arithmetic: 3.76 us -> none  [the longest x1 3.75 us: shards(): terms = share[:, None] * picked.astype(jnp.float32)]
    unnamed x7 -> x24, local copies, waits for them, and re-layouts: 16.1 us -> 17.8 us
  transfers between devices with their start and end apart: 2 -> 23, of which waited for: 1 -> 12; matrix products, arithmetic and copies ran while one was open for 10% -> 20% of each run, Pallas kernels for 0% -> 0%
where the time goes in v1:
time: 82.5 us; the launch traced here: 82.2 us
  waiting for transfers between devices  27.8 us (34%)
  starting transfers between devices  23.1 us (28%)
  local copies, waits for them, and re-layouts  17.9 us (22%)
  matrix products  9.75 us (12%)
  other arithmetic  3.34 us (4%)
    ppermute x23, waiting for transfers between devices, swap(): return lax.ppermute(block, 'ep', [(i, i ^ offset) for i in range(count)])  27.8 us
    ppermute x23, starting transfers between devices, swap(): return lax.ppermute(block, 'ep', [(i, i ^ offset) for i in range(count)])  23.1 us
    unnamed x24, local copies, waits for them, and re-layouts  17.8 us
    dot_general x1, matrix products, shards(): jnp.dot(everything[:, :width], weights_gu, preferred_element_type=jnp.flo...  7.58 us
    dot_general x1, matrix products, shards(): jnp.dot(hidden, down[0], preferred_element_type=jnp.float32)  2.16 us
  transfers between devices with their start and end apart: 23, of which 12 were waited for; matrix products, arithmetic and copies ran while one was open for 20% of the time, Pallas kernels for 0%

profile of v1, /device:TPU:0, one launch (start us, length us, event | category | flops | bytes accessed | tf_op | source)
XLA Modules:
  0.0 82.2 jit_solution(3195860082298294089)
XLA Ops:
  0.0 1.0 %fusion.19 = f32[16]{0:T(128)S(1)} fusion(bf16[16,3584]{1,0:T(8,128)(2,1)} %param.6), kind=kLoop, calls=%fused_computation.15 | loop fusion | flops 172016 | bytes 114752 | tf_op jit(solution)/shard_map/reduce_sum | solution.py:32
  1.0 0.8 copy.9
  1.8 0.8 copy.10
  2.6 1.0 %fusion.21 = bf16[16,3584]{1,0:T(8,128)(2,1)S(1)} fusion(bf16[16,3584]{1,0:T(8,128)(2,1)} %param.6, f32[3584]{0:T(1024)} %param.7, f32[16]{0:T(128)S(1)} %add_rsqrt_fusion), kind=kLoop, calls=%fused_computation.17 | loop fusion | flops 229376 | bytes 243776 | tf_op jit(solution)/shard_map/convert_element_type | solution.py:33
  3.7 5.1 %collective-permute-start = (bf16[16,3712]{1,0:T(8,128)(2,1)S(1)}, bf16[16,3712]{1,0:T(8,128)(2,1)S(1)}, u32[]{:S(2)}, u32[]{:S(2)}) collective-permute-start(bf16[16,3712]{1,0:T(8,128)(2,1)S(1)} %pad_maximum_fusion), channel_id=1, source_target_pairs={{0,12},{1,13},{2,14},{3,15},{4,8},{5,9},{6,10},{7,11},{8,4},{9,5},... | collective-permute-start | bytes 356360 | tf_op jit(solution)/shard_map/ppermute | solution.py:11
  8.8 4.2 %collective-permute-done = bf16[16,3712]{1,0:T(8,128)(2,1)S(1)} collective-permute-done((bf16[16,3712]{1,0:T(8,128)(2,1)S(1)}, bf16[16,3712]{1,0:T(8,128)(2,1)S(1)}, u32[]{:S(2)}, u32[]{:S(2)}) %collective-permute-start) | collective-permute-done | bytes 118816 | tf_op jit(solution)/shard_map/ppermute | solution.py:11
  13.0 1.7 %collective-permute-start.1 = (bf16[16,3712]{1,0:T(8,128)(2,1)S(1)}, bf16[16,3712]{1,0:T(8,128)(2,1)S(1)}, u32[]{:S(2)}, u32[]{:S(2)}) collective-permute-start(bf16[16,3712]{1,0:T(8,128)(2,1)S(1)} %collective-permute-done), channel_id=1, source_target_pairs={{0,2},{1,3},{2,0},{3,1},{4,6},{5,7},{6,4},{7,5},{8,10},{9,11},{10,... | collective-permute-start | bytes 356360 | tf_op jit(solution)/shard_map/ppermute | solution.py:11
  14.7 4.1 %collective-permute-done.3 = bf16[16,3712]{1,0:T(8,128)(2,1)S(1)} collective-permute-done((bf16[16,3712]{1,0:T(8,128)(2,1)S(1)}, bf16[16,3712]{1,0:T(8,128)(2,1)S(1)}, u32[]{:S(2)}, u32[]{:S(2)}) %collective-permute-start.3) | collective-permute-done | bytes 118816 | tf_op jit(solution)/shard_map/ppermute | solution.py:11
  18.8 1.5 %collective-permute-start.4 = (bf16[16,3712]{1,0:T(8,128)(2,1)S(1)}, bf16[16,3712]{1,0:T(8,128)(2,1)S(1)}, u32[]{:S(2)}, u32[]{:S(2)}) collective-permute-start(bf16[16,3712]{1,0:T(8,128)(2,1)S(1)} %collective-permute-done.3), channel_id=1, source_target_pairs={{0,2},{1,3},{2,0},{3,1},{4,6},{5,7},{6,4},{7,5},{8,10},{9,11},{10,... | collective-permute-start | bytes 356360 | tf_op jit(solution)/shard_map/ppermute | solution.py:11
  20.4 3.2 %collective-permute-start.6 = (bf16[16,3712]{1,0:T(8,128)(2,1)S(1)}, bf16[16,3712]{1,0:T(8,128)(2,1)S(1)}, u32[]{:S(2)}, u32[]{:S(2)}) collective-permute-start(bf16[16,3712]{1,0:T(8,128)(2,1)S(1)} %pad_maximum_fusion), channel_id=1, source_target_pairs={{0,6},{1,7},{2,4},{3,5},{4,2},{5,3},{6,0},{7,1},{8,14},{9,15},{10,... | collective-permute-start | bytes 356360 | tf_op jit(solution)/shard_map/ppermute | solution.py:11
  23.6 0.5 collective-permute-start.8
  24.2 16.1 %copy.11 = bf16[448,8,2,1024]{3,1,2,0:T(8,128)(2,1)} copy(bf16[448,8,2,1024]{3,2,1,0:T(2,128)(2,1)} %bitcast.15) | data formatting | bytes 29360128
  40.3 0.5 collective-permute-start.5
  41.0 0.8 collective-permute-done.5
  43.8 0.7 collective-permute-done.13
  44.7 7.6 %fusion.14 = f32[256,2048]{1,0:T(8,128)S(1)} fusion(bf16[3584,2048]{1,0:T(8,128)(2,1)} %bitcast.16, bf16[256,3712]{1,0:T(8,128)(2,1)S(1)} %constant_dynamic-update-slice_fusion), kind=kOutput, calls=%fused_computation.6 | convolution fusion | flops 3758096384 | bytes 18612224 | tf_op jit(solution)/shard_map/dot_general | solution.py:50
  52.4 2.2 %fusion.11 = bf16[256,3584]{1,0:T(8,128)(2,1)S(1)} fusion(bf16[1,1024,3584]{2,1,0:T(8,128)(2,1)S(1)} %bitcast.18, f32[256]{0:T(256)S(1)} %select_reduce_fusion, f32[256,2048]{1,0:T(8,128)S(1)} %fusion.14), kind=kOutput, calls=%fused_computation.5 | convolution fusion | flops 1884291072 | bytes 11273216 | tf_op jit(solution)/shard_map/dot_general | solution.py:52
  54.7 0.4 collective-permute-start.15
  55.1 2.1 %collective-permute-done.15 = bf16[128,3584]{1,0:T(8,128)(2,1)S(1)} collective-permute-done((bf16[128,3584]{1,0:T(8,128)(2,1)S(1)}, bf16[128,3584]{1,0:T(8,128)(2,1)S(1)}, u32[]{:S(2)}, u32[]{:S(2)}) %collective-permute-start.15) | collective-permute-done | bytes 917536 | tf_op jit(solution)/shard_map/ppermute | solution.py:11
  57.5 1.5 %collective-permute-start.17 = (bf16[16,3584]{1,0:T(8,128)(2,1)S(1)}, bf16[16,3584]{1,0:T(8,128)(2,1)S(1)}, u32[]{:S(2)}, u32[]{:S(2)}) collective-permute-start(bf16[16,3584]{1,0:T(8,128)(2,1)S(1)} %get-tuple-element.8), channel_id=1, source_target_pairs={{0,2},{1,3},{2,0},{3,1},{4,6},{5,7},{6,4},{7,5},{8,10},{9,11},{10,... | collective-permute-start | bytes 344072 | tf_op jit(solution)/shard_map/ppermute | solution.py:11
  59.0 0.6 collective-permute-start.19
  59.6 1.5 %collective-permute-start.21 = (bf16[16,3584]{1,0:T(8,128)(2,1)S(1)}, bf16[16,3584]{1,0:T(8,128)(2,1)S(1)}, u32[]{:S(2)}, u32[]{:S(2)}) collective-permute-start(bf16[16,3584]{1,0:T(8,128)(2,1)S(1)} %get-tuple-element.6), channel_id=1, source_target_pairs={{0,2},{1,3},{2,0},{3,1},{4,6},{5,7},{6,4},{7,5},{8,10},{9,11},{10,... | collective-permute-start | bytes 344072 | tf_op jit(solution)/shard_map/ppermute | solution.py:11
  61.0 0.6 collective-permute-start.16
  61.6 1.9 %collective-permute-done.17 = bf16[16,3584]{1,0:T(8,128)(2,1)S(1)} collective-permute-done((bf16[16,3584]{1,0:T(8,128)(2,1)S(1)}, bf16[16,3584]{1,0:T(8,128)(2,1)S(1)}, u32[]{:S(2)}, u32[]{:S(2)}) %collective-permute-start.17) | collective-permute-done | bytes 114720 | tf_op jit(solution)/shard_map/ppermute | solution.py:11
  63.5 2.5 %collective-permute-done.19 = bf16[16,3584]{1,0:T(8,128)(2,1)S(1)} collective-permute-done((bf16[16,3584]{1,0:T(8,128)(2,1)S(1)}, bf16[16,3584]{1,0:T(8,128)(2,1)S(1)}, u32[]{:S(2)}, u32[]{:S(2)}) %collective-permute-start.19) | collective-permute-done | bytes 114720 | tf_op jit(solution)/shard_map/ppermute | solution.py:11
  66.0 2.5 %collective-permute-done.21 = bf16[16,3584]{1,0:T(8,128)(2,1)S(1)} collective-permute-done((bf16[16,3584]{1,0:T(8,128)(2,1)S(1)}, bf16[16,3584]{1,0:T(8,128)(2,1)S(1)}, u32[]{:S(2)}, u32[]{:S(2)}) %collective-permute-start.21) | collective-permute-done | bytes 114720 | tf_op jit(solution)/shard_map/ppermute | solution.py:11
  68.5 2.7 %collective-permute-start.18 = (bf16[16,3584]{1,0:T(8,128)(2,1)S(1)}, bf16[16,3584]{1,0:T(8,128)(2,1)S(1)}, u32[]{:S(2)}, u32[]{:S(2)}) collective-permute-start(bf16[16,3584]{1,0:T(8,128)(2,1)S(1)} %get-tuple-element.9), channel_id=1, source_target_pairs={{0,12},{1,13},{2,14},{3,15},{4,8},{5,9},{6,10},{7,11},{8,4},{9,5},... | collective-permute-start | bytes 344072 | tf_op jit(solution)/shard_map/ppermute | solution.py:11
  71.2 0.8 collective-permute-start.20
  72.0 1.0 %collective-permute-start.22 = (bf16[16,3584]{1,0:T(8,128)(2,1)S(1)}, bf16[16,3584]{1,0:T(8,128)(2,1)S(1)}, u32[]{:S(2)}, u32[]{:S(2)}) collective-permute-start(bf16[16,3584]{1,0:T(8,128)(2,1)S(1)} %get-tuple-element.10), channel_id=1, source_target_pairs={{0,4},{1,5},{2,6},{3,7},{4,0},{5,1},{6,2},{7,3},{8,12},{9,13},{10,... | collective-permute-start | bytes 344072 | tf_op jit(solution)/shard_map/ppermute | solution.py:11
  73.0 3.6 %collective-permute-done.18 = bf16[16,3584]{1,0:T(8,128)(2,1)S(1)} collective-permute-done((bf16[16,3584]{1,0:T(8,128)(2,1)S(1)}, bf16[16,3584]{1,0:T(8,128)(2,1)S(1)}, u32[]{:S(2)}, u32[]{:S(2)}) %collective-permute-start.18) | collective-permute-done | bytes 114720 | tf_op jit(solution)/shard_map/ppermute | solution.py:11
  76.6 4.8 %collective-permute-done.20 = bf16[16,3584]{1,0:T(8,128)(2,1)S(1)} collective-permute-done((bf16[16,3584]{1,0:T(8,128)(2,1)S(1)}, bf16[16,3584]{1,0:T(8,128)(2,1)S(1)}, u32[]{:S(2)}, u32[]{:S(2)}) %collective-permute-start.20) | collective-permute-done | bytes 114720 | tf_op jit(solution)/shard_map/ppermute | solution.py:11
  81.4 0.8 fusion.22
  (54 shorter events, 3.1 us)
Async XLA Ops:
  3.7 9.3 %collective-permute-start = (bf16[16,3712]{1,0:T(8,128)(2,1)S(1)}, bf16[16,3712]{1,0:T(8,128)(2,1)S(1)}, u32[]{:S(2)}, u32[]{:S(2)}) collective-permute-start(bf16[16,3712]{1,0:T(8,128)(2,1)S(1)} %pad_maximum_fusion), channel_id=1, source_target_pairs={{0,12},{1,13},{2,14},{3,15},{4,8},{5,9},{6,10},{7,11},{8,4},{9,5},... | collective-permute-start | bytes 356360 | tf_op jit(solution)/shard_map/ppermute | solution.py:11
  8.8 10.0 %collective-permute-start.3 = (bf16[16,3712]{1,0:T(8,128)(2,1)S(1)}, bf16[16,3712]{1,0:T(8,128)(2,1)S(1)}, u32[]{:S(2)}, u32[]{:S(2)}) collective-permute-start(bf16[16,3712]{1,0:T(8,128)(2,1)S(1)} %pad_maximum_fusion), channel_id=1, source_target_pairs={{0,8},{1,9},{2,10},{3,11},{4,12},{5,13},{6,14},{7,15},{8,0},{9,1},... | collective-permute-start | bytes 356360 | tf_op jit(solution)/shard_map/ppermute | solution.py:11
  13.0 7.4 %collective-permute-start.1 = (bf16[16,3712]{1,0:T(8,128)(2,1)S(1)}, bf16[16,3712]{1,0:T(8,128)(2,1)S(1)}, u32[]{:S(2)}, u32[]{:S(2)}) collective-permute-start(bf16[16,3712]{1,0:T(8,128)(2,1)S(1)} %collective-permute-done), channel_id=1, source_target_pairs={{0,2},{1,3},{2,0},{3,1},{4,6},{5,7},{6,4},{7,5},{8,10},{9,11},{10,... | collective-permute-start | bytes 356360 | tf_op jit(solution)/shard_map/ppermute | solution.py:11
  18.8 21.4 %collective-permute-start.4 = (bf16[16,3712]{1,0:T(8,128)(2,1)S(1)}, bf16[16,3712]{1,0:T(8,128)(2,1)S(1)}, u32[]{:S(2)}, u32[]{:S(2)}) collective-permute-start(bf16[16,3712]{1,0:T(8,128)(2,1)S(1)} %collective-permute-done.3), channel_id=1, source_target_pairs={{0,2},{1,3},{2,0},{3,1},{4,6},{5,7},{6,4},{7,5},{8,10},{9,11},{10,... | collective-permute-start | bytes 356360 | tf_op jit(solution)/shard_map/ppermute | solution.py:11
  20.4 20.0 %collective-permute-start.2 = (bf16[16,3712]{1,0:T(8,128)(2,1)S(1)}, bf16[16,3712]{1,0:T(8,128)(2,1)S(1)}, u32[]{:S(2)}, u32[]{:S(2)}) collective-permute-start(bf16[16,3712]{1,0:T(8,128)(2,1)S(1)} %collective-permute-done.1), channel_id=1, source_target_pairs={{0,1},{1,0},{2,3},{3,2},{4,5},{5,4},{6,7},{7,6},{8,9},{9,8},{10,11... | collective-permute-start | bytes 356360 | tf_op jit(solution)/shard_map/ppermute | solution.py:11
  20.4 20.5 %collective-permute-start.6 = (bf16[16,3712]{1,0:T(8,128)(2,1)S(1)}, bf16[16,3712]{1,0:T(8,128)(2,1)S(1)}, u32[]{:S(2)}, u32[]{:S(2)}) collective-permute-start(bf16[16,3712]{1,0:T(8,128)(2,1)S(1)} %pad_maximum_fusion), channel_id=1, source_target_pairs={{0,6},{1,7},{2,4},{3,5},{4,2},{5,3},{6,0},{7,1},{8,14},{9,15},{10,... | collective-permute-start | bytes 356360 | tf_op jit(solution)/shard_map/ppermute | solution.py:11
  23.6 18.6 %collective-permute-start.8 = (bf16[16,3712]{1,0:T(8,128)(2,1)S(1)}, bf16[16,3712]{1,0:T(8,128)(2,1)S(1)}, u32[]{:S(2)}, u32[]{:S(2)}) collective-permute-start(bf16[16,3712]{1,0:T(8,128)(2,1)S(1)} %pad_maximum_fusion), channel_id=1, source_target_pairs={{0,2},{1,3},{2,0},{3,1},{4,6},{5,7},{6,4},{7,5},{8,10},{9,11},{10,... | collective-permute-start | bytes 356360 | tf_op jit(solution)/shard_map/ppermute | solution.py:11
  24.1 18.3 %collective-permute-start.12 = (bf16[16,3712]{1,0:T(8,128)(2,1)S(1)}, bf16[16,3712]{1,0:T(8,128)(2,1)S(1)}, u32[]{:S(2)}, u32[]{:S(2)}) collective-permute-start(bf16[16,3712]{1,0:T(8,128)(2,1)S(1)} %pad_maximum_fusion), channel_id=1, source_target_pairs={{0,4},{1,5},{2,6},{3,7},{4,0},{5,1},{6,2},{7,3},{8,12},{9,13},{10,... | collective-permute-start | bytes 356360 | tf_op jit(solution)/shard_map/ppermute | solution.py:11
  40.3 4.2 %collective-permute-start.14 = (bf16[16,3712]{1,0:T(8,128)(2,1)S(1)}, bf16[16,3712]{1,0:T(8,128)(2,1)S(1)}, u32[]{:S(2)}, u32[]{:S(2)}) collective-permute-start(bf16[16,3712]{1,0:T(8,128)(2,1)S(1)} %pad_maximum_fusion), channel_id=1, source_target_pairs={{0,1},{1,0},{2,3},{3,2},{4,5},{5,4},{6,7},{7,6},{8,9},{9,8},{10,11... | collective-permute-start | bytes 356360 | tf_op jit(solution)/shard_map/ppermute | solution.py:11
  40.3 1.5 %collective-permute-start.5 = (bf16[16,3712]{1,0:T(8,128)(2,1)S(1)}, bf16[16,3712]{1,0:T(8,128)(2,1)S(1)}, u32[]{:S(2)}, u32[]{:S(2)}) collective-permute-start(bf16[16,3712]{1,0:T(8,128)(2,1)S(1)} %collective-permute-done.4), channel_id=1, source_target_pairs={{0,1},{1,0},{2,3},{3,2},{4,5},{5,4},{6,7},{7,6},{8,9},{9,8},{10,11... | collective-permute-start | bytes 356360 | tf_op jit(solution)/shard_map/ppermute | solution.py:11
  40.9 2.9 %collective-permute-start.10 = (bf16[16,3712]{1,0:T(8,128)(2,1)S(1)}, bf16[16,3712]{1,0:T(8,128)(2,1)S(1)}, u32[]{:S(2)}, u32[]{:S(2)}) collective-permute-start(bf16[16,3712]{1,0:T(8,128)(2,1)S(1)} %collective-permute-done), channel_id=1, source_target_pairs={{0,1},{1,0},{2,3},{3,2},{4,5},{5,4},{6,7},{7,6},{8,9},{9,8},{10,11... | collective-permute-start | bytes 356360 | tf_op jit(solution)/shard_map/ppermute | solution.py:11
  41.8 1.3 %collective-permute-start.7 = (bf16[16,3712]{1,0:T(8,128)(2,1)S(1)}, bf16[16,3712]{1,0:T(8,128)(2,1)S(1)}, u32[]{:S(2)}, u32[]{:S(2)}) collective-permute-start(bf16[16,3712]{1,0:T(8,128)(2,1)S(1)} %collective-permute-done.6), channel_id=1, source_target_pairs={{0,1},{1,0},{2,3},{3,2},{4,5},{5,4},{6,7},{7,6},{8,9},{9,8},{10,11... | collective-permute-start | bytes 356360 | tf_op jit(solution)/shard_map/ppermute | solution.py:11
  42.2 1.6 %collective-permute-start.11 = (bf16[16,3712]{1,0:T(8,128)(2,1)S(1)}, bf16[16,3712]{1,0:T(8,128)(2,1)S(1)}, u32[]{:S(2)}, u32[]{:S(2)}) collective-permute-start(bf16[16,3712]{1,0:T(8,128)(2,1)S(1)} %collective-permute-done.3), channel_id=1, source_target_pairs={{0,1},{1,0},{2,3},{3,2},{4,5},{5,4},{6,7},{7,6},{8,9},{9,8},{10,11... | collective-permute-start | bytes 356360 | tf_op jit(solution)/shard_map/ppermute | solution.py:11
  42.4 1.3 %collective-permute-start.9 = (bf16[16,3712]{1,0:T(8,128)(2,1)S(1)}, bf16[16,3712]{1,0:T(8,128)(2,1)S(1)}, u32[]{:S(2)}, u32[]{:S(2)}) collective-permute-start(bf16[16,3712]{1,0:T(8,128)(2,1)S(1)} %collective-permute-done.8), channel_id=1, source_target_pairs={{0,1},{1,0},{2,3},{3,2},{4,5},{5,4},{6,7},{7,6},{8,9},{9,8},{10,11... | collective-permute-start | bytes 356360 | tf_op jit(solution)/shard_map/ppermute | solution.py:11
  43.2 1.3 %collective-permute-start.13 = (bf16[16,3712]{1,0:T(8,128)(2,1)S(1)}, bf16[16,3712]{1,0:T(8,128)(2,1)S(1)}, u32[]{:S(2)}, u32[]{:S(2)}) collective-permute-start(bf16[16,3712]{1,0:T(8,128)(2,1)S(1)} %collective-permute-done.12), channel_id=1, source_target_pairs={{0,1},{1,0},{2,3},{3,2},{4,5},{5,4},{6,7},{7,6},{8,9},{9,8},{10,11... | collective-permute-start | bytes 356360 | tf_op jit(solution)/shard_map/ppermute | solution.py:11
  44.6 7.8 %slice-start = ((s8[7340032]{0:T(1024)(128)(4,1)}), s8[4194304]{0:T(1024)(128)(4,1)S(1)}, s32[]{:S(2)}) async-start(s8[7340032]{0:T(1024)(128)(4,1)} %bitcast.17), calls=%async_computation | async-start | bytes 8388608
  44.7 7.7 %slice-start.1 = ((s8[7340032]{0:T(1024)(128)(4,1)}), s8[3145728]{0:T(1024)(128)(4,1)S(1)}, s32[]{:S(2)}) async-start(s8[7340032]{0:T(1024)(128)(4,1)} %bitcast.17), calls=%async_computation.1 | async-start | bytes 6291456
  54.7 26.7 %copy-start = (bf16[16,3584]{1,0:T(8,128)(2,1)S(1)}, bf16[16,3584]{1,0:T(8,128)(2,1)}, u32[]{:S(2)}) copy-start(bf16[16,3584]{1,0:T(8,128)(2,1)} %param.6) | copy-start | bytes 344068
  54.7 2.5 %collective-permute-start.15 = (bf16[128,3584]{1,0:T(8,128)(2,1)S(1)}, bf16[128,3584]{1,0:T(8,128)(2,1)S(1)}, u32[]{:S(2)}, u32[]{:S(2)}) collective-permute-start(bf16[128,3584]{1,0:T(8,128)(2,1)S(1)} %slice.60), channel_id=1, source_target_pairs={{0,1},{1,0},{2,3},{3,2},{4,5},{5,4},{6,7},{7,6},{8,9},{9,8},{10,11... | collective-permute-start | bytes 2752520 | tf_op jit(solution)/shard_map/ppermute | solution.py:11
  57.5 6.0 %collective-permute-start.17 = (bf16[16,3584]{1,0:T(8,128)(2,1)S(1)}, bf16[16,3584]{1,0:T(8,128)(2,1)S(1)}, u32[]{:S(2)}, u32[]{:S(2)}) collective-permute-start(bf16[16,3584]{1,0:T(8,128)(2,1)S(1)} %get-tuple-element.8), channel_id=1, source_target_pairs={{0,2},{1,3},{2,0},{3,1},{4,6},{5,7},{6,4},{7,5},{8,10},{9,11},{10,... | collective-permute-start | bytes 344072 | tf_op jit(solution)/shard_map/ppermute | solution.py:11
  59.0 7.0 %collective-permute-start.19 = (bf16[16,3584]{1,0:T(8,128)(2,1)S(1)}, bf16[16,3584]{1,0:T(8,128)(2,1)S(1)}, u32[]{:S(2)}, u32[]{:S(2)}) collective-permute-start(bf16[16,3584]{1,0:T(8,128)(2,1)S(1)} %get-tuple-element.7), channel_id=1, source_target_pairs={{0,2},{1,3},{2,0},{3,1},{4,6},{5,7},{6,4},{7,5},{8,10},{9,11},{10,... | collective-permute-start | bytes 344072 | tf_op jit(solution)/shard_map/ppermute | solution.py:11
  59.6 8.9 %collective-permute-start.21 = (bf16[16,3584]{1,0:T(8,128)(2,1)S(1)}, bf16[16,3584]{1,0:T(8,128)(2,1)S(1)}, u32[]{:S(2)}, u32[]{:S(2)}) collective-permute-start(bf16[16,3584]{1,0:T(8,128)(2,1)S(1)} %get-tuple-element.6), channel_id=1, source_target_pairs={{0,2},{1,3},{2,0},{3,1},{4,6},{5,7},{6,4},{7,5},{8,10},{9,11},{10,... | collective-permute-start | bytes 344072 | tf_op jit(solution)/shard_map/ppermute | solution.py:11
  61.0 11.9 %collective-permute-start.16 = (bf16[16,3584]{1,0:T(8,128)(2,1)S(1)}, bf16[16,3584]{1,0:T(8,128)(2,1)S(1)}, u32[]{:S(2)}, u32[]{:S(2)}) collective-permute-start(bf16[16,3584]{1,0:T(8,128)(2,1)S(1)} %get-tuple-element.5), channel_id=1, source_target_pairs={{0,2},{1,3},{2,0},{3,1},{4,6},{5,7},{6,4},{7,5},{8,10},{9,11},{10,... | collective-permute-start | bytes 344072 | tf_op jit(solution)/shard_map/ppermute | solution.py:11
  68.5 8.1 %collective-permute-start.18 = (bf16[16,3584]{1,0:T(8,128)(2,1)S(1)}, bf16[16,3584]{1,0:T(8,128)(2,1)S(1)}, u32[]{:S(2)}, u32[]{:S(2)}) collective-permute-start(bf16[16,3584]{1,0:T(8,128)(2,1)S(1)} %get-tuple-element.9), channel_id=1, source_target_pairs={{0,12},{1,13},{2,14},{3,15},{4,8},{5,9},{6,10},{7,11},{8,4},{9,5},... | collective-permute-start | bytes 344072 | tf_op jit(solution)/shard_map/ppermute | solution.py:11
  71.2 10.2 %collective-permute-start.20 = (bf16[16,3584]{1,0:T(8,128)(2,1)S(1)}, bf16[16,3584]{1,0:T(8,128)(2,1)S(1)}, u32[]{:S(2)}, u32[]{:S(2)}) collective-permute-start(bf16[16,3584]{1,0:T(8,128)(2,1)S(1)} %get-tuple-element.11), channel_id=1, source_target_pairs={{0,8},{1,9},{2,10},{3,11},{4,12},{5,13},{6,14},{7,15},{8,0},{9,1},... | collective-permute-start | bytes 344072 | tf_op jit(solution)/shard_map/ppermute | solution.py:11
  72.0 9.4 %collective-permute-start.22 = (bf16[16,3584]{1,0:T(8,128)(2,1)S(1)}, bf16[16,3584]{1,0:T(8,128)(2,1)S(1)}, u32[]{:S(2)}, u32[]{:S(2)}) collective-permute-start(bf16[16,3584]{1,0:T(8,128)(2,1)S(1)} %get-tuple-element.10), channel_id=1, source_target_pairs={{0,4},{1,5},{2,6},{3,7},{4,0},{5,1},{6,2},{7,3},{8,12},{9,13},{10,... | collective-permute-start | bytes 344072 | tf_op jit(solution)/shard_map/ppermute | solution.py:11

commit v2 on v1

v2 whole, which is shorter than its diff:
```python
import functools

import jax
import jax.numpy as jnp
from jax import lax
from jax.experimental import pallas as pl
from jax.experimental.pallas import tpu as pltpu
from jax.sharding import PartitionSpec as P

eps = 1e-06
lane = 128
VMEM = pl.BlockSpec(memory_space=pltpu.VMEM)
ANY = pl.BlockSpec(memory_space=pl.ANY)
HBM = pl.BlockSpec(memory_space=pltpu.HBM)


def limit(mib):
    return pltpu.CompilerParams(vmem_limit_bytes=mib << 20)


def in_hbm(array):
    return pltpu.with_memory_space_constraint(array, pltpu.HBM)


def in_vmem(array):
    return pltpu.with_memory_space_constraint(array, pltpu.VMEM)


def norm_kernel(*refs):
    sources, out_ref, held, sems = refs[:4], refs[4], refs[5:9], refs[9]
    copies = [
        pltpu.make_async_copy(source, ref, sems.at[i])
        for i, (source, ref) in enumerate(zip(sources, held))
    ]
    for copy in copies:
        copy.start()
    for copy in copies:
        copy.wait()
    resid_ref, gain_ref, ids_ref, weights_ref = held
    rows, width = resid_ref.shape
    values = resid_ref[...].astype(jnp.float32)
    scale = lax.rsqrt(jnp.mean(values * values, axis=-1, keepdims=True) + eps)
    gain = gain_ref[...].reshape(1, width)
    out_ref[:, :width] = (values * scale * gain).astype(jnp.bfloat16)
    chosen, count = ids_ref.shape
    experts = lax.broadcasted_iota(jnp.int32, (lane, count), 0)
    share = jnp.zeros((lane, count), jnp.float32)
    for k in range(chosen):
        weight = weights_ref[k : k + 1, :].astype(jnp.float32)
        share = share + jnp.where(experts == ids_ref[k : k + 1, :], weight, 0.0)
    out_ref[:, width:] = share.T.astype(jnp.bfloat16)


def norm(resid, gain, ids, weights):
    rows, width = resid.shape
    sources = [resid, gain, ids.T, weights.T]
    return pl.pallas_call(
        norm_kernel,
        out_shape=jax.ShapeDtypeStruct((rows, width + lane), jnp.bfloat16),
        in_specs=[HBM] * 4,
        out_specs=VMEM,
        scratch_shapes=[pltpu.VMEM(a.shape, a.dtype) for a in sources]
        + [pltpu.SemaphoreType.DMA((4,))],
        compiler_params=limit(3),
        name="norm",
    )(*[in_hbm(a) for a in sources])


def unpack_kernel(first, packed_ref, *refs):
    out_ref, token_ref, buffer, sems = refs[-4:]
    token_ref[...] = jnp.zeros_like(token_ref)
    width = packed_ref.shape[1]
    groups = buffer.shape[0]
    inner = groups * lane
    copies = [
        pltpu.make_async_copy(
            packed_ref.at[0, :, :, (first + c) * lane : (first + c + 1) * lane],
            buffer.at[c],
            sems.at[c],
        )
        for c in range(groups)
    ]
    for copy in copies:
        copy.start()
    tile = 128
    for c in range(groups):
        copies[c].wait()
        rows = buffer.at[c].reshape(2 * width, lane)

        def step(i, _):
            both = rows.at[pl.ds(pl.multiple_of(i * 2 * tile, 2 * tile), 2 * tile), :]
            to = pl.ds(pl.multiple_of(i * tile, tile), tile)
            out_ref[to, c * lane : (c + 1) * lane] = both[pl.ds(0, tile, stride=2), :]
            out_ref[to, inner + c * lane : inner + (c + 1) * lane] = both[
                pl.ds(1, tile, stride=2), :
            ]
            return 0

        lax.fori_loop(0, width // tile, step, 0, unroll=2)


def unpack(packed, first, groups, after):
    width = packed.shape[1]
    return pl.pallas_call(
        functools.partial(unpack_kernel, first),
        out_shape=[
            jax.ShapeDtypeStruct((width, 2 * groups * lane), jnp.bfloat16),
            jax.ShapeDtypeStruct((8, lane), jnp.float32),
        ],
        in_specs=[HBM] + [ANY] * len(after),
        out_specs=[VMEM, VMEM],
        scratch_shapes=[
            pltpu.VMEM((groups, width, 2, lane), jnp.bfloat16),
            pltpu.SemaphoreType.DMA((groups,)),
        ],
        compiler_params=limit(9),
        cost_estimate=pl.CostEstimate(
            flops=0, bytes_accessed=8 * width * groups * lane, transcendentals=0
        ),
        name="unpack",
    )(in_hbm(packed), *after)


def pass_kernel(*refs):
    count = (len(refs) - 1) // 2
    for source, out_ref in zip(refs[:count], refs[count + 1 :]):
        out_ref[...] = source[...]


def pass_on(blocks, after):
    return pl.pallas_call(
        pass_kernel,
        out_shape=[jax.ShapeDtypeStruct(b.shape, b.dtype) for b in blocks],
        in_specs=[VMEM] * len(blocks) + [ANY],
        out_specs=[VMEM] * len(blocks),
        compiler_params=limit(2),
        name="pass_on",
    )(*blocks, after)


def hidden_rows(rows_ref, gu_refs, hidden, at, tile):
    step = 256
    to = 0
    rows = rows_ref[at : at + tile, : gu_refs[0].shape[0]]
    for gu_ref in gu_refs:
        half = gu_ref.shape[1] // 2
        for n in range(0, half, step):
            gate = jnp.dot(rows, gu_ref[:, n : n + step], preferred_element_type=jnp.float32)
            up = jnp.dot(
                rows, gu_ref[:, half + n : half + n + step], preferred_element_type=jnp.float32
            )
            hidden[at : at + tile, to : to + step] = (jax.nn.silu(gate) * up).astype(jnp.bfloat16)
            to += step


def near_kernel(count, *refs):
    block_refs, gu_refs = refs[:count], refs[count:-2]
    hidden, rows_ref = refs[-2:]
    size = block_refs[0].shape[0]
    for at, block_ref in enumerate(block_refs):
        rows_ref[at * size : (at + 1) * size, :] = block_ref[...]
    tile = min(256, size * count)
    for at in range(0, size * count, tile):
        hidden_rows(rows_ref, gu_refs, hidden, at, tile)


def near_hidden(blocks, halves):
    size, wide = blocks[0].shape
    count = size * len(blocks)
    width, inner = halves[0].shape[0], sum(h.shape[1] // 2 for h in halves)
    return pl.pallas_call(
        functools.partial(near_kernel, len(blocks)),
        out_shape=jax.ShapeDtypeStruct((count, inner), jnp.bfloat16),
        in_specs=[VMEM] * (len(blocks) + len(halves)),
        out_specs=VMEM,
        scratch_shapes=[pltpu.VMEM((count, wide), jnp.bfloat16)],
        compiler_params=limit(6),
        cost_estimate=pl.CostEstimate(
            flops=4 * count * width * inner, bytes_accessed=0, transcendentals=count * inner
        ),
        name="near",
    )(*blocks, *halves)


def expert_kernel(near_count, far_count, order, down_hbm, near_hidden_ref, *refs):
    near_refs, far_refs = refs[:near_count], refs[near_count : near_count + far_count]
    gu_refs = refs[near_count + far_count : -7]
    away_ref, here_ref, rows_ref, far_hidden, hidden, down_ref, sem = refs[-7:]
    copy = pltpu.make_async_copy(down_hbm, down_ref, sem)
    copy.start()
    inner, width = down_ref.shape[1:]
    count = hidden.shape[0]
    size = near_refs[0].shape[0]
    for at, block_ref in enumerate(far_refs):
        rows_ref[at * size : (at + 1) * size, :] = block_ref[...]
    tile = min(256, size * far_count)
    for at in range(0, size * far_count, tile):
        hidden_rows(rows_ref, gu_refs, far_hidden, at, tile)
    shares = []
    for to, (near, at) in enumerate(order):
        source = near_hidden_ref if near else far_hidden
        hidden[to * size : (to + 1) * size, :] = source[at * size : (at + 1) * size, :]
        shares.append((near_refs if near else far_refs)[at][:, width:].astype(jnp.float32))
    shares = jnp.concatenate(shares, axis=0)
    lanes = lax.broadcasted_iota(jnp.int32, shares.shape, 1)
    share = jnp.sum(jnp.where(lanes == lax.axis_index("ep"), shares, 0.0), axis=1, keepdims=True)
    copy.wait()
    half = count // 2
    tile = min(256, count)
    step = 512
    for at in range(0, count, tile):
        for n in range(0, width, step):
            piece = jnp.dot(
                hidden[at : at + tile, :],
                down_ref[0, :, n : n + step],
                preferred_element_type=jnp.float32,
            )
            piece = piece.astype(jnp.bfloat16).astype(jnp.float32)
            terms = (share[at : at + tile] * piece).astype(jnp.bfloat16)
            if tile > half:
                away_ref[:, n : n + step] = terms[:half]
                here_ref[:, n : n + step] = terms[half:]
            else:
                out_ref, to = (away_ref, at) if at < half else (here_ref, at - half)
                out_ref[to : to + tile, n : n + step] = terms


def expert(down, near, far, halves, order):
    hidden = near_hidden(near, halves)
    size = near[0].shape[0]
    count = size * (len(near) + len(far))
    _, inner, width = down.shape
    return pl.pallas_call(
        functools.partial(expert_kernel, len(near), len(far), order),
        out_shape=[jax.ShapeDtypeStruct((count // 2, width), jnp.bfloat16)] * 2,
        in_specs=[HBM] + [VMEM] * (1 + len(near) + len(far) + len(halves)),
        out_specs=[VMEM, VMEM],
        scratch_shapes=[
            pltpu.VMEM((size * len(far), width + lane), jnp.bfloat16),
            pltpu.VMEM((size * len(far), inner), jnp.bfloat16),
            pltpu.VMEM((count, inner), jnp.bfloat16),
            pltpu.VMEM(down.shape, jnp.bfloat16),
            pltpu.SemaphoreType.DMA,
        ],
        compiler_params=limit(16 if count <= 256 else 43),
        cost_estimate=pl.CostEstimate(
            flops=4 * count * width * inner,
            bytes_accessed=2 * width * inner,
            transcendentals=count * inner // 2,
        ),
        name="expert",
    )(in_hbm(down), hidden, *near, *far, *halves)


def fold_kernel(got_ref, here_ref, *out_refs):
    *away_refs, rest_ref = out_refs
    rows = away_refs[0].shape[0]
    for at, away_ref in enumerate(away_refs):
        part = slice(at * rows, (at + 1) * rows)
        total = got_ref[part, :].astype(jnp.float32) + here_ref[part, :].astype(jnp.float32)
        away_ref[...] = total.astype(jnp.bfloat16)
    rest = rest_ref.shape[0]
    at = got_ref.shape[0] - rest
    total = got_ref[at:, :].astype(jnp.float32) + here_ref[at:, :].astype(jnp.float32)
    rest_ref[...] = total.astype(jnp.bfloat16)


def fold(got, here, count):
    total, width = got.shape
    shape = jax.ShapeDtypeStruct
    return pl.pallas_call(
        fold_kernel,
        out_shape=[shape((total // 2 // count, width), jnp.bfloat16)] * count
        + [shape((total // 2, width), jnp.bfloat16)],
        in_specs=[VMEM, VMEM],
        out_specs=[VMEM] * (count + 1),
        compiler_params=pltpu.CompilerParams(vmem_limit_bytes=6 << 20),
        name="fold",
    )(got, here)


def add_kernel(at, got_ref, here_ref, out_ref):
    rows = got_ref.shape[0]
    here = here_ref[at : at + rows, :].astype(jnp.float32)
    out_ref[...] = (got_ref[...].astype(jnp.float32) + here).astype(jnp.bfloat16)


def add(got, here, at):
    return pl.pallas_call(
        functools.partial(add_kernel, at),
        out_shape=jax.ShapeDtypeStruct(got.shape, jnp.bfloat16),
        in_specs=[VMEM, VMEM],
        out_specs=VMEM,
        compiler_params=pltpu.CompilerParams(vmem_limit_bytes=2 << 20),
        name="add",
    )(got, here)


def swap(block, offset):
    count = lax.axis_size("ep")
    return lax.ppermute(block, "ep", [(i, i ^ offset) for i in range(count)])


def gather_blocks(block, far, weights):
    near = {0: block}
    for offset in reversed(far):
        near[offset] = swap(block, offset)
    first, token = weights(0, [])
    (again,) = pass_on([block], token)
    for offset in (2, far[0] ^ 2):
        near[offset] = swap(again, offset)
    near[1] = swap(again, 1)
    late = far[:0:-1]
    second, _ = weights(1, [near[late[0]]])
    for offset in late:
        near[offset ^ 2] = swap(near[offset], 2)
    for offset in list(near):
        if offset > 1:
            near[offset ^ 1] = swap(near[offset], 1)
    return near, [first, second]


def shards(resid, norm_gain, expert_ids, route_weights, gate_up, down):
    owners = lax.axis_size("ep")
    tp = lax.axis_size("tp")
    far = tuple(range(4, owners, 4))
    inner = down.shape[1]
    resid_all = lax.all_gather(resid, "tp", axis=0, tiled=True) if tp > 1 else resid
    normed = norm(resid_all, norm_gain, expert_ids, route_weights)
    rows = normed.shape[0]
    groups = inner // lane
    cuts = ((0, groups // 2), (groups // 2, groups - groups // 2))
    blocks, halves = gather_blocks(
        normed, far, lambda i, after: unpack(gate_up, *cuts[i], after)
    )
    order = sorted(blocks, key=lambda o: (1 - (o & 1), 1 - (o >> 1 & 1), -o))
    places = [(o < 8, o % 8 if o < 8 else o - 8) for o in order]
    near = [blocks[o] for o in range(8)]
    away, here = expert(
        down, near, [blocks[o] for o in range(8, owners)], halves, places
    )
    *away, here = fold(swap(away, 1), here, len(far) + 1)
    evens = [o for o in order if o & 3 == 0]
    got = {offset: swap(block, 2) for offset, block in zip(evens, away)}
    mine = None
    for at, offset in enumerate(evens):
        if offset:
            part = swap(add(got[offset], here, at * rows), offset).astype(jnp.float32)
        else:
            part = got[0].astype(jnp.float32) + here[at * rows :].astype(jnp.float32)
        mine = part if mine is None else mine + part
    if tp > 1:
        mine = lax.psum_scatter(mine, "tp", scatter_dimension=0, tiled=True)
    return (resid.astype(jnp.float32) + mine).astype(jnp.bfloat16)


def solution(mesh):
    return jax.shard_map(
        shards,
        mesh=mesh,
        in_specs=(
            P(("parts", "ep", "tp"), None),
            P(),
            P(("parts", "ep"), None),
            P(("parts", "ep"), None),
            P("ep", None, None, "tp"),
            P("ep", "tp", None),
        ),
        out_specs=P(("parts", "ep", "tp"), None),
        check_vma=False,
    )
```

time: 82.5 us -> 57.3 us (0.69)
  Pallas kernels: 0 us -> 18.4 us
  local copies, waits for them, and re-layouts: 17.9 us -> 0.01 us
  waiting for transfers between devices: 27.8 us -> 15.3 us
  matrix products: 9.75 us -> 0 us
  other arithmetic: 3.34 us -> 0.74 us
    pallas_call x0 -> x10, Pallas kernels: none -> 18.4 us  [the longest x2 7.75 us: unpack(): pl.pallas_call(functools.partial(unpack_kernel, first), out_shape=[jax.Sh...]
    unnamed x24 -> x2, local copies, waits for them, and re-layouts: 17.8 us -> 0.01 us
    ppermute x23, waiting for transfers between devices: 27.8 us -> 15.3 us  [swap(): return lax.ppermute(block, 'ep', [(i, i ^ offset) for i in range(count)])]
    dot_general x2 -> x0, matrix products: 9.75 us -> none  [the longest x1 7.58 us: shards(): jnp.dot(everything[:, :width], weights_gu, preferred_element_type=jnp.flo...]
    convert_element_type x4 -> x1, other arithmetic: 2.04 us -> 0.74 us  [shards(): return (resid.astype(jnp.float32) + mine).astype(jnp.bfloat16)]
    reduce_sum x3 -> x0, other arithmetic: 1.26 us -> none  [the longest x1 1.04 us: shards(): scale = lax.rsqrt(jnp.mean(values * values, axis=-1, keepdims=True) + eps)]
  transfers between devices with their start and end apart: 23 -> 23, of which waited for: 12 -> 10; matrix products, arithmetic and copies ran while one was open for 20% -> 0% of each run, Pallas kernels for 0% -> 17%
where the time goes in v2:
time: 57.3 us; the launch traced here: 57.1 us
  starting transfers between devices  22.6 us (39%)
  Pallas kernels  18.4 us (32%)
  waiting for transfers between devices  15.3 us (27%)
  other arithmetic  0.74 us (1%)
    ppermute x23, starting transfers between devices, swap(): return lax.ppermute(block, 'ep', [(i, i ^ offset) for i in range(count)])  22.6 us
    ppermute x23, waiting for transfers between devices, swap(): return lax.ppermute(block, 'ep', [(i, i ^ offset) for i in range(count)])  15.3 us
    pallas_call x2, Pallas kernels, unpack(): pl.pallas_call(functools.partial(unpack_kernel, first), out_shape=[jax.Sh...  7.75 us
    pallas_call x1, Pallas kernels, expert(): pl.pallas_call(functools.partial(expert_kernel, len(near), len(far), orde...  7.11 us
    pallas_call x1, Pallas kernels, near_hidden(): pl.pallas_call(functools.partial(near_kernel, len(blocks)), out_shape=jax...  2.1 us
  transfers between devices with their start and end apart: 23, of which 10 were waited for; matrix products, arithmetic and copies ran while one was open for 0% of the time, Pallas kernels for 17%

profile of v2, /device:TPU:0, one launch (start us, length us, event | category | flops | bytes accessed | tf_op | source)
XLA Modules:
  0.0 57.1 jit_solution(5821599833821149498)
XLA Ops:
  0.0 1.1 %norm.1.refs_0_ = bf16[16,3712]{1,0:T(8,128)(2,1)S(1)} custom-call(bf16[16,3584]{1,0:T(8,128)(2,1)} %refs_0_.1, f32[3584]{0:T(1024)} %refs_1_.1, s32[8,16]{1,0:T(8,128)} %bitcast.2, bf16[8,16]{1,0:T(8,128)(2,1)} %bitcast.3), custom_call_target="tpu_custom_call" | custom-call | tf_op jit(solution)/shard_map/norm/pallas_call | solution.py:57
  1.1 4.1 %collective-permute-start.8 = (bf16[16,3712]{1,0:T(8,128)(2,1)S(1)}, bf16[16,3712]{1,0:T(8,128)(2,1)S(1)}, u32[]{:S(2)}, u32[]{:S(2)}) collective-permute-start(bf16[16,3712]{1,0:T(8,128)(2,1)S(1)} %norm.1.refs_0_), channel_id=1, source_target_pairs={{0,8},{1,9},{2,10},{3,11},{4,12},{5,13},{6,14},{7,15},{8,0},{9,1},... | collective-permute-start | bytes 356360 | tf_op jit(solution)/shard_map/ppermute | solution.py:301
  5.2 1.3 %collective-permute-start.7 = (bf16[16,3712]{1,0:T(8,128)(2,1)S(1)}, bf16[16,3712]{1,0:T(8,128)(2,1)S(1)}, u32[]{:S(2)}, u32[]{:S(2)}) collective-permute-start(bf16[16,3712]{1,0:T(8,128)(2,1)S(1)} %norm.1.refs_0_), channel_id=1, source_target_pairs={{0,12},{1,13},{2,14},{3,15},{4,8},{5,9},{6,10},{7,11},{8,4},{9,5},... | collective-permute-start | bytes 356360 | tf_op jit(solution)/shard_map/ppermute | solution.py:301
  6.8 3.6 %unpack.2 = (bf16[3584,1024]{1,0:T(8,128)(2,1)S(1)}, f32[8,128]{1,0:T(8,128)S(1)}) custom-call(bf16[1,3584,2,1024]{3,2,1,0:T(2,128)(2,1)} %packed_ref.3), custom_call_target="tpu_custom_call" | custom-call | bytes 14680064 | tf_op jit(solution)/shard_map/unpack/pallas_call | solution.py:104
  10.4 2.8 %collective-permute-start.5 = (bf16[16,3712]{1,0:T(8,128)(2,1)S(1)}, bf16[16,3712]{1,0:T(8,128)(2,1)S(1)}, u32[]{:S(2)}, u32[]{:S(2)}) collective-permute-start(bf16[16,3712]{1,0:T(8,128)(2,1)S(1)} %pass_on.1), channel_id=1, source_target_pairs={{0,6},{1,7},{2,4},{3,5},{4,2},{5,3},{6,0},{7,1},{8,14},{9,15},{10,... | collective-permute-start | bytes 356360 | tf_op jit(solution)/shard_map/ppermute | solution.py:301
  13.2 0.5 collective-permute-start.1
  13.7 0.7 %collective-permute-done.8.refs_8_ = bf16[16,3712]{1,0:T(8,128)(2,1)S(1)} collective-permute-done((bf16[16,3712]{1,0:T(8,128)(2,1)S(1)}, bf16[16,3712]{1,0:T(8,128)(2,1)S(1)}, u32[]{:S(2)}, u32[]{:S(2)}) %collective-permute-start.8) | collective-permute-done | bytes 118816 | tf_op jit(solution)/shard_map/ppermute | solution.py:301
  14.4 1.9 %collective-permute-start.10 = (bf16[16,3712]{1,0:T(8,128)(2,1)S(1)}, bf16[16,3712]{1,0:T(8,128)(2,1)S(1)}, u32[]{:S(2)}, u32[]{:S(2)}) collective-permute-start(bf16[16,3712]{1,0:T(8,128)(2,1)S(1)} %collective-permute-done.8.refs_8_), channel_id=1, source_target_pairs={{0,2},{1,3},{2,0},{3,1},{4,6},{5,7},{6,4},{7,5},{8,10},{9,11},{10,... | collective-permute-start | bytes 356360 | tf_op jit(solution)/shard_map/ppermute | solution.py:301
  16.3 1.4 %collective-permute-start.13 = (bf16[16,3712]{1,0:T(8,128)(2,1)S(1)}, bf16[16,3712]{1,0:T(8,128)(2,1)S(1)}, u32[]{:S(2)}, u32[]{:S(2)}) collective-permute-start(bf16[16,3712]{1,0:T(8,128)(2,1)S(1)} %collective-permute-done.7.refs_0_.refs_12_), channel_id=1, source_target_pairs={{0,2},{1,3},{2,0},{3,1},{4,6},{5,7},{6,4},{7,5},{8,10},{9,11},{10,... | collective-permute-start | bytes 356360 | tf_op jit(solution)/shard_map/ppermute | solution.py:301
  17.7 0.9 %collective-permute-done.5.refs_6_ = bf16[16,3712]{1,0:T(8,128)(2,1)S(1)} collective-permute-done((bf16[16,3712]{1,0:T(8,128)(2,1)S(1)}, bf16[16,3712]{1,0:T(8,128)(2,1)S(1)}, u32[]{:S(2)}, u32[]{:S(2)}) %collective-permute-start.5) | collective-permute-done | bytes 118816 | tf_op jit(solution)/shard_map/ppermute | solution.py:301
  18.6 2.0 %collective-permute-done.1.refs_2_ = bf16[16,3712]{1,0:T(8,128)(2,1)S(1)} collective-permute-done((bf16[16,3712]{1,0:T(8,128)(2,1)S(1)}, bf16[16,3712]{1,0:T(8,128)(2,1)S(1)}, u32[]{:S(2)}, u32[]{:S(2)}) %collective-permute-start.1) | collective-permute-done | bytes 118816 | tf_op jit(solution)/shard_map/ppermute | solution.py:301
  20.5 0.5 collective-permute-start.2
  21.1 4.2 %unpack.3 = (bf16[3584,1024]{1,0:T(8,128)(2,1)S(1)}, f32[8,128]{1,0:T(8,128)}) custom-call(bf16[1,3584,2,1024]{3,2,1,0:T(2,128)(2,1)} %packed_ref.3, bf16[16,3712]{1,0:T(8,128)(2,1)S(1)} %collective-permute-done.7.refs_0_.refs_12_), custom_call_target="tpu_custom_call" | custom-call | bytes 14680064 | tf_op jit(solution)/shard_map/unpack/pallas_call | solution.py:104
  25.3 0.5 collective-permute-start.12
  25.9 0.4 collective-permute-start.14
  26.3 2.1 %near.1.near_hidden_ref = bf16[128,1024]{1,0:T(8,128)(2,1)S(1)} custom-call(bf16[16,3712]{1,0:T(8,128)(2,1)S(1)} %norm.1.refs_0_, bf16[16,3712]{1,0:T(8,128)(2,1)S(1)} %collective-permute-done.refs_1_, bf16[16,3712]{1,0:T(8,128)(2,1)S(1)} %collective-permute-done.1.refs_2_, bf16[16,3712]{1,0:T(8,128)(2,1)S(1)} %collective-permute-done.2.refs_3_, ...), custom_call_target="tpu_custom_call" | custom-call | flops 1879048192 | tf_op jit(solution)/shard_map/near/pallas_call | solution.py:171
  28.5 7.1 %expert.1 = (bf16[128,3584]{1,0:T(8,128)(2,1)S(1)}, bf16[128,3584]{1,0:T(8,128)(2,1)S(1)}) custom-call(bf16[1,1024,3584]{2,1,0:T(8,128)(2,1)} %down_hbm.1, bf16[128,1024]{1,0:T(8,128)(2,1)S(1)} %near.1.near_hidden_ref, bf16[16,3712]{1,0:T(8,128)(2,1)S(1)} %norm.1.refs_0_, bf16[16,3712]{1,0:T(8,128)(2,1)S(1)} %collective-permute-done.refs_1_, ...), custom_call_target="tpu_custom_call" | custom-call | flops 3758096384 | bytes 7340032 | tf_op jit(solution)/shard_map/expert/pallas_call | solution.py:233
  35.8 2.4 %collective-permute-done.15.got_ref = bf16[128,3584]{1,0:T(8,128)(2,1)S(1)} collective-permute-done((bf16[128,3584]{1,0:T(8,128)(2,1)S(1)}, bf16[128,3584]{1,0:T(8,128)(2,1)S(1)}, u32[]{:S(2)}, u32[]{:S(2)}) %collective-permute-start.15) | collective-permute-done | bytes 917536 | tf_op jit(solution)/shard_map/ppermute | solution.py:301
  38.4 0.3 collective-permute-start.16
  38.7 1.8 %collective-permute-start.18 = (bf16[16,3584]{1,0:T(8,128)(2,1)S(1)}, bf16[16,3584]{1,0:T(8,128)(2,1)S(1)}, u32[]{:S(2)}, u32[]{:S(2)}) collective-permute-start(bf16[16,3584]{1,0:T(8,128)(2,1)S(1)} %get-tuple-element.22), channel_id=1, source_target_pairs={{0,2},{1,3},{2,0},{3,1},{4,6},{5,7},{6,4},{7,5},{8,10},{9,11},{10,... | collective-permute-start | bytes 344072 | tf_op jit(solution)/shard_map/ppermute | solution.py:301
  40.5 0.3 collective-permute-start.20
  40.7 1.8 %collective-permute-start.22 = (bf16[16,3584]{1,0:T(8,128)(2,1)S(1)}, bf16[16,3584]{1,0:T(8,128)(2,1)S(1)}, u32[]{:S(2)}, u32[]{:S(2)}) collective-permute-start(bf16[16,3584]{1,0:T(8,128)(2,1)S(1)} %get-tuple-element.24), channel_id=1, source_target_pairs={{0,2},{1,3},{2,0},{3,1},{4,6},{5,7},{6,4},{7,5},{8,10},{9,11},{10,... | collective-permute-start | bytes 344072 | tf_op jit(solution)/shard_map/ppermute | solution.py:301
  42.5 1.9 %collective-permute-done.16.got_ref = bf16[16,3584]{1,0:T(8,128)(2,1)S(1)} collective-permute-done((bf16[16,3584]{1,0:T(8,128)(2,1)S(1)}, bf16[16,3584]{1,0:T(8,128)(2,1)S(1)}, u32[]{:S(2)}, u32[]{:S(2)}) %collective-permute-start.16) | collective-permute-done | bytes 114720 | tf_op jit(solution)/shard_map/ppermute | solution.py:301
  44.5 2.9 %collective-permute-start.17 = (bf16[16,3584]{1,0:T(8,128)(2,1)S(1)}, bf16[16,3584]{1,0:T(8,128)(2,1)S(1)}, u32[]{:S(2)}, u32[]{:S(2)}) collective-permute-start(bf16[16,3584]{1,0:T(8,128)(2,1)S(1)} %add.28), channel_id=1, source_target_pairs={{0,12},{1,13},{2,14},{3,15},{4,8},{5,9},{6,10},{7,11},{8,4},{9,5},... | collective-permute-start | bytes 344072 | tf_op jit(solution)/shard_map/ppermute | solution.py:301
  47.4 0.3 collective-permute-start.19
  47.8 1.6 %collective-permute-done.20.got_ref = bf16[16,3584]{1,0:T(8,128)(2,1)S(1)} collective-permute-done((bf16[16,3584]{1,0:T(8,128)(2,1)S(1)}, bf16[16,3584]{1,0:T(8,128)(2,1)S(1)}, u32[]{:S(2)}, u32[]{:S(2)}) %collective-permute-start.20) | collective-permute-done | bytes 114720 | tf_op jit(solution)/shard_map/ppermute | solution.py:301
  49.4 1.2 %collective-permute-start.21 = (bf16[16,3584]{1,0:T(8,128)(2,1)S(1)}, bf16[16,3584]{1,0:T(8,128)(2,1)S(1)}, u32[]{:S(2)}, u32[]{:S(2)}) collective-permute-start(bf16[16,3584]{1,0:T(8,128)(2,1)S(1)} %add.30), channel_id=1, source_target_pairs={{0,4},{1,5},{2,6},{3,7},{4,0},{5,1},{6,2},{7,3},{8,12},{9,13},{10,... | collective-permute-start | bytes 344072 | tf_op jit(solution)/shard_map/ppermute | solution.py:301
  50.5 0.5 collective-permute-done.22
  51.0 0.9 %collective-permute-done.17 = bf16[16,3584]{1,0:T(8,128)(2,1)S(1)} collective-permute-done((bf16[16,3584]{1,0:T(8,128)(2,1)S(1)}, bf16[16,3584]{1,0:T(8,128)(2,1)S(1)}, u32[]{:S(2)}, u32[]{:S(2)}) %collective-permute-start.17) | collective-permute-done | bytes 114720 | tf_op jit(solution)/shard_map/ppermute | solution.py:301
  51.9 4.2 %collective-permute-done.19 = bf16[16,3584]{1,0:T(8,128)(2,1)S(1)} collective-permute-done((bf16[16,3584]{1,0:T(8,128)(2,1)S(1)}, bf16[16,3584]{1,0:T(8,128)(2,1)S(1)}, u32[]{:S(2)}, u32[]{:S(2)}) %collective-permute-start.19) | collective-permute-done | bytes 114720 | tf_op jit(solution)/shard_map/ppermute | solution.py:301
  56.1 0.3 collective-permute-done.21
  56.4 0.7 %add_convert_fusion = bf16[16,3584]{1,0:T(8,128)(2,1)} fusion(bf16[16,3584]{1,0:T(8,128)(2,1)S(1)} %collective-permute-done.22, bf16[16,3584]{1,0:T(8,128)(2,1)S(1)} %collective-permute-done.21, bf16[16,3584]{1,0:T(8,128)(2,1)S(1)} %collective-permute-done.19, bf16[16,3584]{1,0:T(8,128)(2,1)S(1)} %collective-permute-done.17, bf16[16,3584]{1,0:T(8,128)(2,1)S(1)} %copy-done, ...), kind=kLoop, calls=%fused_computation | loop fusion | flops 688128 | bytes 802816 | tf_op jit(solution)/shard_map/convert_element_type | solution.py:354
  (27 shorter events, 0.9 us)
Async XLA Ops:
  1.1 13.3 %collective-permute-start.8 = (bf16[16,3712]{1,0:T(8,128)(2,1)S(1)}, bf16[16,3712]{1,0:T(8,128)(2,1)S(1)}, u32[]{:S(2)}, u32[]{:S(2)}) collective-permute-start(bf16[16,3712]{1,0:T(8,128)(2,1)S(1)} %norm.1.refs_0_), channel_id=1, source_target_pairs={{0,8},{1,9},{2,10},{3,11},{4,12},{5,13},{6,14},{7,15},{8,0},{9,1},... | collective-permute-start | bytes 356360 | tf_op jit(solution)/shard_map/ppermute | solution.py:301
  5.2 9.2 %collective-permute-start.7 = (bf16[16,3712]{1,0:T(8,128)(2,1)S(1)}, bf16[16,3712]{1,0:T(8,128)(2,1)S(1)}, u32[]{:S(2)}, u32[]{:S(2)}) collective-permute-start(bf16[16,3712]{1,0:T(8,128)(2,1)S(1)} %norm.1.refs_0_), channel_id=1, source_target_pairs={{0,12},{1,13},{2,14},{3,15},{4,8},{5,9},{6,10},{7,11},{8,4},{9,5},... | collective-permute-start | bytes 356360 | tf_op jit(solution)/shard_map/ppermute | solution.py:301
  6.6 9.7 %collective-permute-start.3 = (bf16[16,3712]{1,0:T(8,128)(2,1)S(1)}, bf16[16,3712]{1,0:T(8,128)(2,1)S(1)}, u32[]{:S(2)}, u32[]{:S(2)}) collective-permute-start(bf16[16,3712]{1,0:T(8,128)(2,1)S(1)} %norm.1.refs_0_), channel_id=1, source_target_pairs={{0,4},{1,5},{2,6},{3,7},{4,0},{5,1},{6,2},{7,3},{8,12},{9,13},{10,... | collective-permute-start | bytes 356360 | tf_op jit(solution)/shard_map/ppermute | solution.py:301
  10.4 8.2 %collective-permute-start.5 = (bf16[16,3712]{1,0:T(8,128)(2,1)S(1)}, bf16[16,3712]{1,0:T(8,128)(2,1)S(1)}, u32[]{:S(2)}, u32[]{:S(2)}) collective-permute-start(bf16[16,3712]{1,0:T(8,128)(2,1)S(1)} %pass_on.1), channel_id=1, source_target_pairs={{0,6},{1,7},{2,4},{3,5},{4,2},{5,3},{6,0},{7,1},{8,14},{9,15},{10,... | collective-permute-start | bytes 356360 | tf_op jit(solution)/shard_map/ppermute | solution.py:301
  13.2 7.3 %collective-permute-start.1 = (bf16[16,3712]{1,0:T(8,128)(2,1)S(1)}, bf16[16,3712]{1,0:T(8,128)(2,1)S(1)}, u32[]{:S(2)}, u32[]{:S(2)}) collective-permute-start(bf16[16,3712]{1,0:T(8,128)(2,1)S(1)} %pass_on.1), channel_id=1, source_target_pairs={{0,2},{1,3},{2,0},{3,1},{4,6},{5,7},{6,4},{7,5},{8,10},{9,11},{10,... | collective-permute-start | bytes 356360 | tf_op jit(solution)/shard_map/ppermute | solution.py:301
  14.4 6.1 %collective-permute-start = (bf16[16,3712]{1,0:T(8,128)(2,1)S(1)}, bf16[16,3712]{1,0:T(8,128)(2,1)S(1)}, u32[]{:S(2)}, u32[]{:S(2)}) collective-permute-start(bf16[16,3712]{1,0:T(8,128)(2,1)S(1)} %pass_on.1), channel_id=1, source_target_pairs={{0,1},{1,0},{2,3},{3,2},{4,5},{5,4},{6,7},{7,6},{8,9},{9,8},{10,11... | collective-permute-start | bytes 356360 | tf_op jit(solution)/shard_map/ppermute | solution.py:301
  14.4 10.8 %collective-permute-start.10 = (bf16[16,3712]{1,0:T(8,128)(2,1)S(1)}, bf16[16,3712]{1,0:T(8,128)(2,1)S(1)}, u32[]{:S(2)}, u32[]{:S(2)}) collective-permute-start(bf16[16,3712]{1,0:T(8,128)(2,1)S(1)} %collective-permute-done.8.refs_8_), channel_id=1, source_target_pairs={{0,2},{1,3},{2,0},{3,1},{4,6},{5,7},{6,4},{7,5},{8,10},{9,11},{10,... | collective-permute-start | bytes 356360 | tf_op jit(solution)/shard_map/ppermute | solution.py:301
  16.3 9.0 %collective-permute-start.13 = (bf16[16,3712]{1,0:T(8,128)(2,1)S(1)}, bf16[16,3712]{1,0:T(8,128)(2,1)S(1)}, u32[]{:S(2)}, u32[]{:S(2)}) collective-permute-start(bf16[16,3712]{1,0:T(8,128)(2,1)S(1)} %collective-permute-done.7.refs_0_.refs_12_), channel_id=1, source_target_pairs={{0,2},{1,3},{2,0},{3,1},{4,6},{5,7},{6,4},{7,5},{8,10},{9,11},{10,... | collective-permute-start | bytes 356360 | tf_op jit(solution)/shard_map/ppermute | solution.py:301
  18.6 7.2 %collective-permute-start.4 = (bf16[16,3712]{1,0:T(8,128)(2,1)S(1)}, bf16[16,3712]{1,0:T(8,128)(2,1)S(1)}, u32[]{:S(2)}, u32[]{:S(2)}) collective-permute-start(bf16[16,3712]{1,0:T(8,128)(2,1)S(1)} %collective-permute-done.3.refs_4_), channel_id=1, source_target_pairs={{0,1},{1,0},{2,3},{3,2},{4,5},{5,4},{6,7},{7,6},{8,9},{9,8},{10,11... | collective-permute-start | bytes 356360 | tf_op jit(solution)/shard_map/ppermute | solution.py:301
  20.5 5.4 %collective-permute-start.6 = (bf16[16,3712]{1,0:T(8,128)(2,1)S(1)}, bf16[16,3712]{1,0:T(8,128)(2,1)S(1)}, u32[]{:S(2)}, u32[]{:S(2)}) collective-permute-start(bf16[16,3712]{1,0:T(8,128)(2,1)S(1)} %collective-permute-done.5.refs_6_), channel_id=1, source_target_pairs={{0,1},{1,0},{2,3},{3,2},{4,5},{5,4},{6,7},{7,6},{8,9},{9,8},{10,11... | collective-permute-start | bytes 356360 | tf_op jit(solution)/shard_map/ppermute | solution.py:301
  20.5 5.8 %collective-permute-start.2 = (bf16[16,3712]{1,0:T(8,128)(2,1)S(1)}, bf16[16,3712]{1,0:T(8,128)(2,1)S(1)}, u32[]{:S(2)}, u32[]{:S(2)}) collective-permute-start(bf16[16,3712]{1,0:T(8,128)(2,1)S(1)} %collective-permute-done.1.refs_2_), channel_id=1, source_target_pairs={{0,1},{1,0},{2,3},{3,2},{4,5},{5,4},{6,7},{7,6},{8,9},{9,8},{10,11... | collective-permute-start | bytes 356360 | tf_op jit(solution)/shard_map/ppermute | solution.py:301
  25.2 3.2 %collective-permute-start.9 = (bf16[16,3712]{1,0:T(8,128)(2,1)S(1)}, bf16[16,3712]{1,0:T(8,128)(2,1)S(1)}, u32[]{:S(2)}, u32[]{:S(2)}) collective-permute-start(bf16[16,3712]{1,0:T(8,128)(2,1)S(1)} %collective-permute-done.8.refs_8_), channel_id=1, source_target_pairs={{0,1},{1,0},{2,3},{3,2},{4,5},{5,4},{6,7},{7,6},{8,9},{9,8},{10,11... | collective-permute-start | bytes 356360 | tf_op jit(solution)/shard_map/ppermute | solution.py:301
  25.3 3.1 %collective-permute-start.12 = (bf16[16,3712]{1,0:T(8,128)(2,1)S(1)}, bf16[16,3712]{1,0:T(8,128)(2,1)S(1)}, u32[]{:S(2)}, u32[]{:S(2)}) collective-permute-start(bf16[16,3712]{1,0:T(8,128)(2,1)S(1)} %collective-permute-done.7.refs_0_.refs_12_), channel_id=1, source_target_pairs={{0,1},{1,0},{2,3},{3,2},{4,5},{5,4},{6,7},{7,6},{8,9},{9,8},{10,11... | collective-permute-start | bytes 356360 | tf_op jit(solution)/shard_map/ppermute | solution.py:301
  25.8 2.7 %collective-permute-start.11 = (bf16[16,3712]{1,0:T(8,128)(2,1)S(1)}, bf16[16,3712]{1,0:T(8,128)(2,1)S(1)}, u32[]{:S(2)}, u32[]{:S(2)}) collective-permute-start(bf16[16,3712]{1,0:T(8,128)(2,1)S(1)} %collective-permute-done.10.refs_10_), channel_id=1, source_target_pairs={{0,1},{1,0},{2,3},{3,2},{4,5},{5,4},{6,7},{7,6},{8,9},{9,8},{10,11... | collective-permute-start | bytes 356360 | tf_op jit(solution)/shard_map/ppermute | solution.py:301
  25.9 2.6 %collective-permute-start.14 = (bf16[16,3712]{1,0:T(8,128)(2,1)S(1)}, bf16[16,3712]{1,0:T(8,128)(2,1)S(1)}, u32[]{:S(2)}, u32[]{:S(2)}) collective-permute-start(bf16[16,3712]{1,0:T(8,128)(2,1)S(1)} %collective-permute-done.13.refs_14_), channel_id=1, source_target_pairs={{0,1},{1,0},{2,3},{3,2},{4,5},{5,4},{6,7},{7,6},{8,9},{9,8},{10,11... | collective-permute-start | bytes 356360 | tf_op jit(solution)/shard_map/ppermute | solution.py:301
  28.4 27.9 %copy-start = (bf16[16,3584]{1,0:T(8,128)(2,1)S(1)}, bf16[16,3584]{1,0:T(8,128)(2,1)}, u32[]{:S(2)}) copy-start(bf16[16,3584]{1,0:T(8,128)(2,1)} %refs_0_.1) | copy-start | bytes 344068
  35.6 2.5 %collective-permute-start.15 = (bf16[128,3584]{1,0:T(8,128)(2,1)S(1)}, bf16[128,3584]{1,0:T(8,128)(2,1)S(1)}, u32[]{:S(2)}, u32[]{:S(2)}) collective-permute-start(bf16[128,3584]{1,0:T(8,128)(2,1)S(1)} %get-tuple-element.18), channel_id=1, source_target_pairs={{0,1},{1,0},{2,3},{3,2},{4,5},{5,4},{6,7},{7,6},{8,9},{9,8},{10,11... | collective-permute-start | bytes 2752520 | tf_op jit(solution)/shard_map/ppermute | solution.py:301
  38.4 6.1 %collective-permute-start.16 = (bf16[16,3584]{1,0:T(8,128)(2,1)S(1)}, bf16[16,3584]{1,0:T(8,128)(2,1)S(1)}, u32[]{:S(2)}, u32[]{:S(2)}) collective-permute-start(bf16[16,3584]{1,0:T(8,128)(2,1)S(1)} %get-tuple-element.20), channel_id=1, source_target_pairs={{0,2},{1,3},{2,0},{3,1},{4,6},{5,7},{6,4},{7,5},{8,10},{9,11},{10,... | collective-permute-start | bytes 344072 | tf_op jit(solution)/shard_map/ppermute | solution.py:301
  38.7 8.7 %collective-permute-start.18 = (bf16[16,3584]{1,0:T(8,128)(2,1)S(1)}, bf16[16,3584]{1,0:T(8,128)(2,1)S(1)}, u32[]{:S(2)}, u32[]{:S(2)}) collective-permute-start(bf16[16,3584]{1,0:T(8,128)(2,1)S(1)} %get-tuple-element.22), channel_id=1, source_target_pairs={{0,2},{1,3},{2,0},{3,1},{4,6},{5,7},{6,4},{7,5},{8,10},{9,11},{10,... | collective-permute-start | bytes 344072 | tf_op jit(solution)/shard_map/ppermute | solution.py:301
  40.5 8.9 %collective-permute-start.20 = (bf16[16,3584]{1,0:T(8,128)(2,1)S(1)}, bf16[16,3584]{1,0:T(8,128)(2,1)S(1)}, u32[]{:S(2)}, u32[]{:S(2)}) collective-permute-start(bf16[16,3584]{1,0:T(8,128)(2,1)S(1)} %get-tuple-element.23), channel_id=1, source_target_pairs={{0,2},{1,3},{2,0},{3,1},{4,6},{5,7},{6,4},{7,5},{8,10},{9,11},{10,... | collective-permute-start | bytes 344072 | tf_op jit(solution)/shard_map/ppermute | solution.py:301
  40.7 10.3 %collective-permute-start.22 = (bf16[16,3584]{1,0:T(8,128)(2,1)S(1)}, bf16[16,3584]{1,0:T(8,128)(2,1)S(1)}, u32[]{:S(2)}, u32[]{:S(2)}) collective-permute-start(bf16[16,3584]{1,0:T(8,128)(2,1)S(1)} %get-tuple-element.24), channel_id=1, source_target_pairs={{0,2},{1,3},{2,0},{3,1},{4,6},{5,7},{6,4},{7,5},{8,10},{9,11},{10,... | collective-permute-start | bytes 344072 | tf_op jit(solution)/shard_map/ppermute | solution.py:301
  44.5 7.4 %collective-permute-start.17 = (bf16[16,3584]{1,0:T(8,128)(2,1)S(1)}, bf16[16,3584]{1,0:T(8,128)(2,1)S(1)}, u32[]{:S(2)}, u32[]{:S(2)}) collective-permute-start(bf16[16,3584]{1,0:T(8,128)(2,1)S(1)} %add.28), channel_id=1, source_target_pairs={{0,12},{1,13},{2,14},{3,15},{4,8},{5,9},{6,10},{7,11},{8,4},{9,5},... | collective-permute-start | bytes 344072 | tf_op jit(solution)/shard_map/ppermute | solution.py:301
  47.4 8.6 %collective-permute-start.19 = (bf16[16,3584]{1,0:T(8,128)(2,1)S(1)}, bf16[16,3584]{1,0:T(8,128)(2,1)S(1)}, u32[]{:S(2)}, u32[]{:S(2)}) collective-permute-start(bf16[16,3584]{1,0:T(8,128)(2,1)S(1)} %add.29), channel_id=1, source_target_pairs={{0,8},{1,9},{2,10},{3,11},{4,12},{5,13},{6,14},{7,15},{8,0},{9,1},... | collective-permute-start | bytes 344072 | tf_op jit(solution)/shard_map/ppermute | solution.py:301
  49.4 7.0 %collective-permute-start.21 = (bf16[16,3584]{1,0:T(8,128)(2,1)S(1)}, bf16[16,3584]{1,0:T(8,128)(2,1)S(1)}, u32[]{:S(2)}, u32[]{:S(2)}) collective-permute-start(bf16[16,3584]{1,0:T(8,128)(2,1)S(1)} %add.30), channel_id=1, source_target_pairs={{0,4},{1,5},{2,6},{3,7},{4,0},{5,1},{6,2},{7,3},{8,12},{9,13},{10,... | collective-permute-start | bytes 344072 | tf_op jit(solution)/shard_map/ppermute | solution.py:301

commit v3 on v2

--- a/solution.py
+++ b/solution.py
@@ -99,7 +99,7 @@
         lax.fori_loop(0, width // tile, step, 0, unroll=2)
 
 
-def unpack(packed, first, groups, after):
+def unpack(packed, first, groups, after, cost=0):
     width = packed.shape[1]
     return pl.pallas_call(
         functools.partial(unpack_kernel, first),
@@ -114,9 +114,7 @@
             pltpu.SemaphoreType.DMA((groups,)),
         ],
         compiler_params=limit(9),
-        cost_estimate=pl.CostEstimate(
-            flops=0, bytes_accessed=8 * width * groups * lane, transcendentals=0
-        ),
+        cost_estimate=pl.CostEstimate(flops=0, bytes_accessed=cost, transcendentals=0),
         name="unpack",
     )(in_hbm(packed), *after)
 
@@ -139,11 +137,11 @@
 
 
 def hidden_rows(rows_ref, gu_refs, hidden, at, tile):
-    step = 256
     to = 0
     rows = rows_ref[at : at + tile, : gu_refs[0].shape[0]]
     for gu_ref in gu_refs:
         half = gu_ref.shape[1] // 2
+        step = min(256, half)
         for n in range(0, half, step):
             gate = jnp.dot(rows, gu_ref[:, n : n + step], preferred_element_type=jnp.float32)
             up = jnp.dot(
@@ -153,8 +151,8 @@
             to += step
 
 
-def near_kernel(count, *refs):
-    block_refs, gu_refs = refs[:count], refs[count:-2]
+def near_kernel(count, after, *refs):
+    block_refs, gu_refs = refs[:count], refs[count : -2 - after]
     hidden, rows_ref = refs[-2:]
     size = block_refs[0].shape[0]
     for at, block_ref in enumerate(block_refs):
@@ -164,48 +162,24 @@
         hidden_rows(rows_ref, gu_refs, hidden, at, tile)
 
 
-def near_hidden(blocks, halves):
+def near_hidden(blocks, halves, after):
     size, wide = blocks[0].shape
     count = size * len(blocks)
     width, inner = halves[0].shape[0], sum(h.shape[1] // 2 for h in halves)
     return pl.pallas_call(
-        functools.partial(near_kernel, len(blocks)),
+        functools.partial(near_kernel, len(blocks), len(after)),
         out_shape=jax.ShapeDtypeStruct((count, inner), jnp.bfloat16),
-        in_specs=[VMEM] * (len(blocks) + len(halves)),
+        in_specs=[VMEM] * (len(blocks) + len(halves)) + [ANY] * len(after),
         out_specs=VMEM,
         scratch_shapes=[pltpu.VMEM((count, wide), jnp.bfloat16)],
         compiler_params=limit(6),
-        cost_estimate=pl.CostEstimate(
-            flops=4 * count * width * inner, bytes_accessed=0, transcendentals=count * inner
-        ),
+        cost_estimate=pl.CostEstimate(flops=0, bytes_accessed=0, transcendentals=0),
         name="near",
-    )(*blocks, *halves)
-
-
-def expert_kernel(near_count, far_count, order, down_hbm, near_hidden_ref, *refs):
-    near_refs, far_refs = refs[:near_count], refs[near_count : near_count + far_count]
-    gu_refs = refs[near_count + far_count : -7]
-    away_ref, here_ref, rows_ref, far_hidden, hidden, down_ref, sem = refs[-7:]
-    copy = pltpu.make_async_copy(down_hbm, down_ref, sem)
-    copy.start()
-    inner, width = down_ref.shape[1:]
-    count = hidden.shape[0]
-    size = near_refs[0].shape[0]
-    for at, block_ref in enumerate(far_refs):
-        rows_ref[at * size : (at + 1) * size, :] = block_ref[...]
-    tile = min(256, size * far_count)
-    for at in range(0, size * far_count, tile):
-        hidden_rows(rows_ref, gu_refs, far_hidden, at, tile)
-    shares = []
-    for to, (near, at) in enumerate(order):
-        source = near_hidden_ref if near else far_hidden
-        hidden[to * size : (to + 1) * size, :] = source[at * size : (at + 1) * size, :]
-        shares.append((near_refs if near else far_refs)[at][:, width:].astype(jnp.float32))
-    shares = jnp.concatenate(shares, axis=0)
-    lanes = lax.broadcasted_iota(jnp.int32, shares.shape, 1)
-    share = jnp.sum(jnp.where(lanes == lax.axis_index("ep"), shares, 0.0), axis=1, keepdims=True)
-    copy.wait()
-    half = count // 2
+    )(*blocks, *halves, *after)
+
+
+def down_rows(hidden, share, down_ref, out_ref):
+    count, width = out_ref.shape
     tile = min(256, count)
     step = 512
     for at in range(0, count, tile):
@@ -216,40 +190,81 @@
                 preferred_element_type=jnp.float32,
             )
             piece = piece.astype(jnp.bfloat16).astype(jnp.float32)
-            terms = (share[at : at + tile] * piece).astype(jnp.bfloat16)
-            if tile > half:
-                away_ref[:, n : n + step] = terms[:half]
-                here_ref[:, n : n + step] = terms[half:]
-            else:
-                out_ref, to = (away_ref, at) if at < half else (here_ref, at - half)
-                out_ref[to : to + tile, n : n + step] = terms
-
-
-def expert(down, near, far, halves, order):
-    hidden = near_hidden(near, halves)
+            terms = (share[at : at + tile, :1] * piece).astype(jnp.bfloat16)
+            out_ref[at : at + tile, n : n + step] = terms
+
+
+def away_kernel(near_count, far_count, order, down_ref, near_hidden_ref, *refs):
+    near_refs, far_refs = refs[:near_count], refs[near_count : near_count + far_count]
+    gu_refs = refs[near_count + far_count : -6]
+    away_ref, here_hidden, here_share, rows_ref, far_hidden, away_hidden = refs[-6:]
+    width = down_ref.shape[2]
+    size = near_refs[0].shape[0]
+    for at, block_ref in enumerate(far_refs):
+        rows_ref[at * size : (at + 1) * size, :] = block_ref[...]
+    tile = min(256, size * far_count)
+    for at in range(0, size * far_count, tile):
+        hidden_rows(rows_ref, gu_refs, far_hidden, at, tile)
+    half = len(order) // 2
+    lanes = lax.broadcasted_iota(jnp.int32, (size, lane), 1)
+    parts = []
+    for to, (near, at) in enumerate(order):
+        source = near_hidden_ref if near else far_hidden
+        block = (near_refs if near else far_refs)[at][:, width:].astype(jnp.float32)
+        mine = jnp.where(lanes == lax.axis_index("ep"), block, 0.0)
+        share = jnp.sum(mine, axis=1, keepdims=True)
+        place = slice(to % half * size, (to % half + 1) * size)
+        if to < half:
+            away_hidden[place, :] = source[at * size : (at + 1) * size, :]
+            parts.append(share)
+        else:
+            here_hidden[place, :] = source[at * size : (at + 1) * size, :]
+            here_share[place, :] = jnp.broadcast_to(share, (size, lane))
+    down_rows(away_hidden, jnp.concatenate(parts, axis=0), down_ref, away_ref)
+
+
+def here_kernel(down_ref, hidden_ref, share_ref, out_ref):
+    down_rows(hidden_ref, share_ref, down_ref, out_ref)
+
+
+def expert(down, hidden, near, far, halves, order):
     size = near[0].shape[0]
     count = size * (len(near) + len(far))
+    half = count // 2
     _, inner, width = down.shape
-    return pl.pallas_call(
-        functools.partial(expert_kernel, len(near), len(far), order),
-        out_shape=[jax.ShapeDtypeStruct((count // 2, width), jnp.bfloat16)] * 2,
-        in_specs=[HBM] + [VMEM] * (1 + len(near) + len(far) + len(halves)),
-        out_specs=[VMEM, VMEM],
+    shape = jax.ShapeDtypeStruct
+    away, here_hidden, here_share = pl.pallas_call(
+        functools.partial(away_kernel, len(near), len(far), order),
+        out_shape=[
+            shape((half, width), jnp.bfloat16),
+            shape((half, inner), jnp.bfloat16),
+            shape((half, lane), jnp.float32),
+        ],
+        in_specs=[VMEM] * (2 + len(near) + len(far) + len(halves)),
+        out_specs=[VMEM] * 3,
         scratch_shapes=[
             pltpu.VMEM((size * len(far), width + lane), jnp.bfloat16),
             pltpu.VMEM((size * len(far), inner), jnp.bfloat16),
-            pltpu.VMEM((count, inner), jnp.bfloat16),
-            pltpu.VMEM(down.shape, jnp.bfloat16),
-            pltpu.SemaphoreType.DMA,
+            pltpu.VMEM((half, inner), jnp.bfloat16),
         ],
-        compiler_params=limit(16 if count <= 256 else 43),
+        compiler_params=limit(8 if count <= 256 else 24),
         cost_estimate=pl.CostEstimate(
-            flops=4 * count * width * inner,
-            bytes_accessed=2 * width * inner,
-            transcendentals=count * inner // 2,
+            flops=3 * count * width * inner, bytes_accessed=0, transcendentals=count * inner // 2
         ),
-        name="expert",
-    )(in_hbm(down), hidden, *near, *far, *halves)
+        name="away",
+    )(down, hidden, *near, *far, *halves)
+    here = pl.pallas_call(
+        here_kernel,
+        out_shape=shape((half, width), jnp.bfloat16),
+        in_specs=[VMEM] * 3,
+        out_specs=VMEM,
+        compiler_params=limit(4 if count <= 256 else 8),
+        cost_estimate=pl.CostEstimate(
+            flops=count * width * inner, bytes_accessed=0, transcendentals=0
+        ),
+        name="here",
+    )(down, here_hidden, here_share)
+    return away, here
 
 
 def fold_kernel(got_ref, here_ref, *out_refs):
@@ -279,21 +294,25 @@
     )(got, here)
 
 
-def add_kernel(at, got_ref, here_ref, out_ref):
+def add_kernel(at, got_ref, here_ref, *refs):
+    count = (len(refs) - 1) // 2
+    out_ref = refs[count]
     rows = got_ref.shape[0]
     here = here_ref[at : at + rows, :].astype(jnp.float32)
     out_ref[...] = (got_ref[...].astype(jnp.float32) + here).astype(jnp.bfloat16)
-
-
-def add(got, here, at):
+    for source, copy_ref in zip(refs[:count], refs[count + 1 :]):
+        copy_ref[...] = source[...]
+
+
+def add(got, here, at, *later):
     return pl.pallas_call(
         functools.partial(add_kernel, at),
-        out_shape=jax.ShapeDtypeStruct(got.shape, jnp.bfloat16),
-        in_specs=[VMEM, VMEM],
-        out_specs=VMEM,
-        compiler_params=pltpu.CompilerParams(vmem_limit_bytes=2 << 20),
+        out_shape=[jax.ShapeDtypeStruct(got.shape, jnp.bfloat16)] * (1 + len(later)),
+        in_specs=[VMEM] * (2 + len(later)),
+        out_specs=[VMEM] * (1 + len(later)),
+        compiler_params=limit(2),
         name="add",
-    )(got, here)
+    )(got, here, *later)
 
 
 def swap(block, offset):
@@ -301,54 +320,68 @@
     return lax.ppermute(block, "ep", [(i, i ^ offset) for i in range(count)])
 
 
-def gather_blocks(block, far, weights):
+def gather_blocks(block, far, gate_up):
+    groups = gate_up.shape[3] // lane // 2
     near = {0: block}
-    for offset in reversed(far):
-        near[offset] = swap(block, offset)
-    first, token = weights(0, [])
+    lead, *late = far[:0:-1]
+    close = far[0]
+    near[lead], near[2] = swap(block, lead), swap(block, 2)
+    first, token = unpack(gate_up, 0, groups, [], 1 << 24)
     (again,) = pass_on([block], token)
-    for offset in (2, far[0] ^ 2):
+    for offset in (*late, close, close ^ 2):
         near[offset] = swap(again, offset)
-    near[1] = swap(again, 1)
-    late = far[:0:-1]
-    second, _ = weights(1, [near[late[0]]])
+    (near[lead],) = pass_on([near[lead]], near[2])
+    near[lead ^ 2] = swap(near[lead], 2)
+    second, token = unpack(gate_up, groups, gate_up.shape[3] // lane - groups, [again], 1 << 24)
+    first_late = (lead, lead ^ 2, *late)
+    near[lead], near[lead ^ 2], *held = pass_on([near[offset] for offset in first_late], token)
+    for offset, array in zip(late, held):
+        near[offset] = array
+        near[offset ^ 2] = swap(array, 2)
+    ready = (0, 2, close, close ^ 2)
+    near[lead ^ 1] = swap(near[lead], 1)
+    for offset, array in zip(ready, pass_on([near[offset] for offset in ready], near[lead ^ 1])):
+        near[offset] = array
+    for offset in (*ready, lead ^ 2, *late):
+        near[offset ^ 1] = swap(near[offset], 1)
     for offset in late:
-        near[offset ^ 2] = swap(near[offset], 2)
-    for offset in list(near):
-        if offset > 1:
-            near[offset ^ 1] = swap(near[offset], 1)
-    return near, [first, second]
+        near[offset ^ 3] = swap(near[offset ^ 2], 1)
+    hidden = near_hidden(
+        [near[offset] for offset in range(8)], [first, second], [near[late[-1] ^ 2]]
+    )
+    return near, [first, second], hidden
 
 
 def shards(resid, norm_gain, expert_ids, route_weights, gate_up, down):
     owners = lax.axis_size("ep")
     tp = lax.axis_size("tp")
     far = tuple(range(4, owners, 4))
-    inner = down.shape[1]
     resid_all = lax.all_gather(resid, "tp", axis=0, tiled=True) if tp > 1 else resid
     normed = norm(resid_all, norm_gain, expert_ids, route_weights)
     rows = normed.shape[0]
-    groups = inner // lane
-    cuts = ((0, groups // 2), (groups // 2, groups - groups // 2))
-    blocks, halves = gather_blocks(
-        normed, far, lambda i, after: unpack(gate_up, *cuts[i], after)
-    )
+    blocks, parts, hidden = gather_blocks(normed, far, gate_up)
     order = sorted(blocks, key=lambda o: (1 - (o & 1), 1 - (o >> 1 & 1), -o))
     places = [(o < 8, o % 8 if o < 8 else o - 8) for o in order]
-    near = [blocks[o] for o in range(8)]
-    away, here = expert(
-        down, near, [blocks[o] for o in range(8, owners)], halves, places
-    )
+    near, late = [blocks[o] for o in range(8)], [blocks[o] for o in range(8, owners)]
+    away, here = expert(down, hidden, near, late, parts, places)
     *away, here = fold(swap(away, 1), here, len(far) + 1)
-    evens = [o for o in order if o & 3 == 0]
-    got = {offset: swap(block, 2) for offset, block in zip(evens, away)}
-    mine = None
-    for at, offset in enumerate(evens):
-        if offset:
-            part = swap(add(got[offset], here, at * rows), offset).astype(jnp.float32)
+    away = dict(zip((o for o in order if o & 3 == 0), away))
+    at_rows = {o: at * rows for at, o in enumerate(away)}
+    close, late = far[0], far[:0:-1]
+    got = {offset: swap(away[offset], 2) for offset in late}
+    beside = swap(here[at_rows[close] : at_rows[close] + rows], close)
+    later = [away[close], away[0], beside]
+    sent = []
+    for offset in late:
+        if offset == late[-1]:
+            block, *later = add(got[offset], here, at_rows[offset], *later)
         else:
-            part = got[0].astype(jnp.float32) + here[at * rows :].astype(jnp.float32)
-        mine = part if mine is None else mine + part
+            (block,) = add(got[offset], here, at_rows[offset])
+        sent.append(swap(block, offset))
+    sent += [swap(later[0], close ^ 2), swap(later[1], 2), later[2]]
+    mine = here[at_rows[0] :].astype(jnp.float32)
+    for block in sent:
+        mine = mine + block.astype(jnp.float32)
     if tp > 1:
         mine = lax.psum_scatter(mine, "tp", scatter_dimension=0, tiled=True)
     return (resid.astype(jnp.float32) + mine).astype(jnp.bfloat16)

time: 57.3 us -> 53.1 us (0.927)
  Pallas kernels: 18.4 us -> 15.2 us
  waiting for transfers between devices: 15.3 us -> 13.9 us
    pallas_call x5, Pallas kernels: 9.3 us -> 6.62 us  [the longest x1 3.18 us: expert(): pl.pallas_call(functools.partial(away_kernel, len(near), len(far), order)...]
    ppermute x23, waiting for transfers between devices: 15.3 us -> 13.9 us  [swap(): return lax.ppermute(block, 'ep', [(i, i ^ offset) for i in range(count)])]
    pallas_call x2, Pallas kernels: 7.75 us -> 7.17 us  [unpack(): pl.pallas_call(functools.partial(unpack_kernel, first), out_shape=[jax.Sh...]
  transfers between devices with their start and end apart: 23 -> 23, of which waited for: 10 -> 8; matrix products, arithmetic and copies ran while one was open for 0% -> 0% of each run, Pallas kernels for 17% -> 20%
where the time goes in v3:
time: 53.1 us; the launch traced here: 52.9 us
  starting transfers between devices  22.9 us (43%)
  Pallas kernels  15.2 us (29%)
  waiting for transfers between devices  13.9 us (26%)
  other arithmetic  0.75 us (1%)
    ppermute x23, starting transfers between devices, swap(): return lax.ppermute(block, 'ep', [(i, i ^ offset) for i in range(count)])  22.9 us
    ppermute x23, waiting for transfers between devices, swap(): return lax.ppermute(block, 'ep', [(i, i ^ offset) for i in range(count)])  13.9 us
    pallas_call x2, Pallas kernels, unpack(): pl.pallas_call(functools.partial(unpack_kernel, first), out_shape=[jax.Sh...  7.17 us
    pallas_call x1, Pallas kernels, expert(): pl.pallas_call(functools.partial(away_kernel, len(near), len(far), order)...  3.18 us
    pallas_call x1, Pallas kernels, near_hidden(): pl.pallas_call(functools.partial(near_kernel, len(blocks), len(after)), o...  2.1 us
    pallas_call x1, Pallas kernels, expert(): pl.pallas_call(here_kernel, out_shape=shape((half, width), jnp.bfloat16),...  1.26 us
    pallas_call x1, Pallas kernels, norm(): pl.pallas_call(norm_kernel, out_shape=jax.ShapeDtypeStruct((rows, width +...  1.1 us
  transfers between devices with their start and end apart: 23, of which 8 were waited for; matrix products, arithmetic and copies ran while one was open for 0% of the time, Pallas kernels for 20%

profile of v3, /device:TPU:0, one launch (start us, length us, event | category | flops | bytes accessed | tf_op | source)
XLA Modules:
  0.0 52.9 jit_solution(14162353660248450604)
XLA Ops:
  0.0 1.1 %norm.1.refs_0_ = bf16[16,3712]{1,0:T(8,128)(2,1)S(1)} custom-call(bf16[16,3584]{1,0:T(8,128)(2,1)} %refs_0_.1, f32[3584]{0:T(1024)} %refs_1_.1, s32[8,16]{1,0:T(8,128)} %bitcast.4, bf16[8,16]{1,0:T(8,128)(2,1)} %bitcast.5), custom_call_target="tpu_custom_call" | custom-call | tf_op jit(solution)/shard_map/norm/pallas_call | solution.py:57
  1.1 5.1 %collective-permute-start.3 = (bf16[16,3712]{1,0:T(8,128)(2,1)S(1)}, bf16[16,3712]{1,0:T(8,128)(2,1)S(1)}, u32[]{:S(2)}, u32[]{:S(2)}) collective-permute-start(bf16[16,3712]{1,0:T(8,128)(2,1)S(1)} %norm.1.refs_0_), channel_id=1, source_target_pairs={{0,12},{1,13},{2,14},{3,15},{4,8},{5,9},{6,10},{7,11},{8,4},{9,5},... | collective-permute-start | bytes 356360 | tf_op jit(solution)/shard_map/ppermute | solution.py:320
  6.2 1.5 %collective-permute-start = (bf16[16,3712]{1,0:T(8,128)(2,1)S(1)}, bf16[16,3712]{1,0:T(8,128)(2,1)S(1)}, u32[]{:S(2)}, u32[]{:S(2)}) collective-permute-start(bf16[16,3712]{1,0:T(8,128)(2,1)S(1)} %norm.1.refs_0_), channel_id=1, source_target_pairs={{0,2},{1,3},{2,0},{3,1},{4,6},{5,7},{6,4},{7,5},{8,10},{9,11},{10,... | collective-permute-start | bytes 356360 | tf_op jit(solution)/shard_map/ppermute | solution.py:320
  7.7 3.6 %unpack.2 = (bf16[3584,1024]{1,0:T(8,128)(2,1)S(1)}, f32[8,128]{1,0:T(8,128)S(1)}) custom-call(bf16[1,3584,2,1024]{3,2,1,0:T(2,128)(2,1)} %packed_ref.3), custom_call_target="tpu_custom_call" | custom-call | bytes 16777216 | tf_op jit(solution)/shard_map/unpack/pallas_call | solution.py:104
  11.5 1.2 %collective-permute-start.4 = (bf16[16,3712]{1,0:T(8,128)(2,1)S(1)}, bf16[16,3712]{1,0:T(8,128)(2,1)S(1)}, u32[]{:S(2)}, u32[]{:S(2)}) collective-permute-start(bf16[16,3712]{1,0:T(8,128)(2,1)S(1)} %pass_on.5.refs_0_), channel_id=1, source_target_pairs={{0,2},{1,3},{2,0},{3,1},{4,6},{5,7},{6,4},{7,5},{8,10},{9,11},{10,... | collective-permute-start | bytes 356360 | tf_op jit(solution)/shard_map/ppermute | solution.py:320
  12.7 1.1 %collective-permute-start.2 = (bf16[16,3712]{1,0:T(8,128)(2,1)S(1)}, bf16[16,3712]{1,0:T(8,128)(2,1)S(1)}, u32[]{:S(2)}, u32[]{:S(2)}) collective-permute-start(bf16[16,3712]{1,0:T(8,128)(2,1)S(1)} %pass_on.4.refs_0_), channel_id=1, source_target_pairs={{0,6},{1,7},{2,4},{3,5},{4,2},{5,3},{6,0},{7,1},{8,14},{9,15},{10,... | collective-permute-start | bytes 356360 | tf_op jit(solution)/shard_map/ppermute | solution.py:320
  13.8 1.3 %collective-permute-start.1 = (bf16[16,3712]{1,0:T(8,128)(2,1)S(1)}, bf16[16,3712]{1,0:T(8,128)(2,1)S(1)}, u32[]{:S(2)}, u32[]{:S(2)}) collective-permute-start(bf16[16,3712]{1,0:T(8,128)(2,1)S(1)} %pass_on.4.refs_0_), channel_id=1, source_target_pairs={{0,4},{1,5},{2,6},{3,7},{4,0},{5,1},{6,2},{7,3},{8,12},{9,13},{10,... | collective-permute-start | bytes 356360 | tf_op jit(solution)/shard_map/ppermute | solution.py:320
  15.0 3.6 %unpack.3 = (bf16[3584,1024]{1,0:T(8,128)(2,1)S(1)}, f32[8,128]{1,0:T(8,128)S(1)}) custom-call(bf16[1,3584,2,1024]{3,2,1,0:T(2,128)(2,1)} %packed_ref.3, bf16[16,3712]{1,0:T(8,128)(2,1)S(1)} %pass_on.4.refs_0_), custom_call_target="tpu_custom_call" | custom-call | bytes 16777216 | tf_op jit(solution)/shard_map/unpack/pallas_call | solution.py:104
  18.8 1.2 %collective-permute-start.11 = (bf16[16,3712]{1,0:T(8,128)(2,1)S(1)}, bf16[16,3712]{1,0:T(8,128)(2,1)S(1)}, u32[]{:S(2)}, u32[]{:S(2)}) collective-permute-start(bf16[16,3712]{1,0:T(8,128)(2,1)S(1)} %get-tuple-element.37.refs_8_), channel_id=1, source_target_pairs={{0,2},{1,3},{2,0},{3,1},{4,6},{5,7},{6,4},{7,5},{8,10},{9,11},{10,... | collective-permute-start | bytes 356360 | tf_op jit(solution)/shard_map/ppermute | solution.py:320
  19.9 0.8 %collective-permute-done.2.refs_3_ = bf16[16,3712]{1,0:T(8,128)(2,1)S(1)} collective-permute-done((bf16[16,3712]{1,0:T(8,128)(2,1)S(1)}, bf16[16,3712]{1,0:T(8,128)(2,1)S(1)}, u32[]{:S(2)}, u32[]{:S(2)}) %collective-permute-start.2) | collective-permute-done | bytes 118816 | tf_op jit(solution)/shard_map/ppermute | solution.py:320
  20.8 1.4 %collective-permute-done.1.refs_2_ = bf16[16,3712]{1,0:T(8,128)(2,1)S(1)} collective-permute-done((bf16[16,3712]{1,0:T(8,128)(2,1)S(1)}, bf16[16,3712]{1,0:T(8,128)(2,1)S(1)}, u32[]{:S(2)}, u32[]{:S(2)}) %collective-permute-start.1) | collective-permute-done | bytes 118816 | tf_op jit(solution)/shard_map/ppermute | solution.py:320
  22.2 0.5 collective-permute-start.8
  22.8 0.4 collective-permute-start.10
  23.3 1.1 %collective-permute-done.11.refs_10_ = bf16[16,3712]{1,0:T(8,128)(2,1)S(1)} collective-permute-done((bf16[16,3712]{1,0:T(8,128)(2,1)S(1)}, bf16[16,3712]{1,0:T(8,128)(2,1)S(1)}, u32[]{:S(2)}, u32[]{:S(2)}) %collective-permute-start.11) | collective-permute-done | bytes 118816 | tf_op jit(solution)/shard_map/ppermute | solution.py:320
  24.4 0.5 collective-permute-start.14
  25.0 2.1 %near.1.near_hidden_ref = bf16[128,1024]{1,0:T(8,128)(2,1)S(1)} custom-call(bf16[16,3712]{1,0:T(8,128)(2,1)S(1)} %get-tuple-element.31.refs_0_, bf16[16,3712]{1,0:T(8,128)(2,1)S(1)} %collective-permute-done.7.refs_1_, bf16[16,3712]{1,0:T(8,128)(2,1)S(1)} %get-tuple-element.32.refs_2_, bf16[16,3712]{1,0:T(8,128)(2,1)S(1)} %collective-permute-done.8.refs_3_, ...), custom_call_target="tpu_custom_call" | custom-call | tf_op jit(solution)/shard_map/near/pallas_call | solution.py:169
  27.2 3.2 %away.1 = (bf16[128,3584]{1,0:T(8,128)(2,1)S(1)}, bf16[128,1024]{1,0:T(8,128)(2,1)S(1)}, f32[128,128]{1,0:T(8,128)S(1)}) custom-call(bf16[1,1024,3584]{2,1,0:T(8,128)(2,1)S(1)} %bitcast.3, bf16[128,1024]{1,0:T(8,128)(2,1)S(1)} %near.1.near_hidden_ref, bf16[16,3712]{1,0:T(8,128)(2,1)S(1)} %get-tuple-element.31.refs_0_, ...), custom_call_target="tpu_custom_call" | custom-call | flops 2818572288 | tf_op jit(solution)/shard_map/away/pallas_call | solution.py:236
  30.4 0.5 collective-permute-start.15
  30.9 1.3 %here.1.here_ref = bf16[128,3584]{1,0:T(8,128)(2,1)S(1)} custom-call(bf16[1,1024,3584]{2,1,0:T(8,128)(2,1)S(1)} %bitcast.3, bf16[128,1024]{1,0:T(8,128)(2,1)S(1)} %get-tuple-element.40.hidden_ref, f32[128,128]{1,0:T(8,128)S(1)} %get-tuple-element.41.share_ref), custom_call_target="tpu_custom_call" | custom-call | flops 939524096 | tf_op jit(solution)/shard_map/here/pallas_call | solution.py:256
  32.2 0.8 %collective-permute-done.15.got_ref = bf16[128,3584]{1,0:T(8,128)(2,1)S(1)} collective-permute-done((bf16[128,3584]{1,0:T(8,128)(2,1)S(1)}, bf16[128,3584]{1,0:T(8,128)(2,1)S(1)}, u32[]{:S(2)}, u32[]{:S(2)}) %collective-permute-start.15) | collective-permute-done | bytes 917536 | tf_op jit(solution)/shard_map/ppermute | solution.py:320
  33.2 1.2 %collective-permute-start.16 = (bf16[16,3584]{1,0:T(8,128)(2,1)S(1)}, bf16[16,3584]{1,0:T(8,128)(2,1)S(1)}, u32[]{:S(2)}, u32[]{:S(2)}) collective-permute-start(bf16[16,3584]{1,0:T(8,128)(2,1)S(1)} %get-tuple-element.43), channel_id=1, source_target_pairs={{0,2},{1,3},{2,0},{3,1},{4,6},{5,7},{6,4},{7,5},{8,10},{9,11},{10,... | collective-permute-start | bytes 344072 | tf_op jit(solution)/shard_map/ppermute | solution.py:320
  34.4 0.7 %collective-permute-start.19 = (bf16[16,3584]{1,0:T(8,128)(2,1)S(1)}, bf16[16,3584]{1,0:T(8,128)(2,1)S(1)}, u32[]{:S(2)}, u32[]{:S(2)}) collective-permute-start(bf16[16,3584]{1,0:T(8,128)(2,1)S(1)} %slice.7), channel_id=1, source_target_pairs={{0,4},{1,5},{2,6},{3,7},{4,0},{5,1},{6,2},{7,3},{8,12},{9,13},{10,... | collective-permute-start | bytes 344072 | tf_op jit(solution)/shard_map/ppermute | solution.py:320
  35.1 1.0 %collective-permute-start.18 = (bf16[16,3584]{1,0:T(8,128)(2,1)S(1)}, bf16[16,3584]{1,0:T(8,128)(2,1)S(1)}, u32[]{:S(2)}, u32[]{:S(2)}) collective-permute-start(bf16[16,3584]{1,0:T(8,128)(2,1)S(1)} %get-tuple-element.44), channel_id=1, source_target_pairs={{0,2},{1,3},{2,0},{3,1},{4,6},{5,7},{6,4},{7,5},{8,10},{9,11},{10,... | collective-permute-start | bytes 344072 | tf_op jit(solution)/shard_map/ppermute | solution.py:320
  36.1 3.1 %collective-permute-done.16.got_ref = bf16[16,3584]{1,0:T(8,128)(2,1)S(1)} collective-permute-done((bf16[16,3584]{1,0:T(8,128)(2,1)S(1)}, bf16[16,3584]{1,0:T(8,128)(2,1)S(1)}, u32[]{:S(2)}, u32[]{:S(2)}) %collective-permute-start.16) | collective-permute-done | bytes 114720 | tf_op jit(solution)/shard_map/ppermute | solution.py:320
  39.3 2.2 %collective-permute-start.17 = (bf16[16,3584]{1,0:T(8,128)(2,1)S(1)}, bf16[16,3584]{1,0:T(8,128)(2,1)S(1)}, u32[]{:S(2)}, u32[]{:S(2)}) collective-permute-start(bf16[16,3584]{1,0:T(8,128)(2,1)S(1)} %add.32), channel_id=1, source_target_pairs={{0,12},{1,13},{2,14},{3,15},{4,8},{5,9},{6,10},{7,11},{8,4},{9,5},... | collective-permute-start | bytes 344072 | tf_op jit(solution)/shard_map/ppermute | solution.py:320
  41.5 2.6 %collective-permute-start.20 = (bf16[16,3584]{1,0:T(8,128)(2,1)S(1)}, bf16[16,3584]{1,0:T(8,128)(2,1)S(1)}, u32[]{:S(2)}, u32[]{:S(2)}) collective-permute-start(bf16[16,3584]{1,0:T(8,128)(2,1)S(1)} %get-tuple-element.47), channel_id=1, source_target_pairs={{0,8},{1,9},{2,10},{3,11},{4,12},{5,13},{6,14},{7,15},{8,0},{9,1},... | collective-permute-start | bytes 344072 | tf_op jit(solution)/shard_map/ppermute | solution.py:320
  44.1 0.5 %collective-permute-start.21 = (bf16[16,3584]{1,0:T(8,128)(2,1)S(1)}, bf16[16,3584]{1,0:T(8,128)(2,1)S(1)}, u32[]{:S(2)}, u32[]{:S(2)}) collective-permute-start(bf16[16,3584]{1,0:T(8,128)(2,1)S(1)} %get-tuple-element.48), channel_id=1, source_target_pairs={{0,6},{1,7},{2,4},{3,5},{4,2},{5,3},{6,0},{7,1},{8,14},{9,15},{10,... | collective-permute-start | bytes 344072 | tf_op jit(solution)/shard_map/ppermute | solution.py:320
  44.7 0.9 %collective-permute-start.22 = (bf16[16,3584]{1,0:T(8,128)(2,1)S(1)}, bf16[16,3584]{1,0:T(8,128)(2,1)S(1)}, u32[]{:S(2)}, u32[]{:S(2)}) collective-permute-start(bf16[16,3584]{1,0:T(8,128)(2,1)S(1)} %get-tuple-element.49), channel_id=1, source_target_pairs={{0,2},{1,3},{2,0},{3,1},{4,6},{5,7},{6,4},{7,5},{8,10},{9,11},{10,... | collective-permute-start | bytes 344072 | tf_op jit(solution)/shard_map/ppermute | solution.py:320
  45.6 1.6 %collective-permute-done.17 = bf16[16,3584]{1,0:T(8,128)(2,1)S(1)} collective-permute-done((bf16[16,3584]{1,0:T(8,128)(2,1)S(1)}, bf16[16,3584]{1,0:T(8,128)(2,1)S(1)}, u32[]{:S(2)}, u32[]{:S(2)}) %collective-permute-start.17) | collective-permute-done | bytes 114720 | tf_op jit(solution)/shard_map/ppermute | solution.py:320
  47.2 4.7 %collective-permute-done.20 = bf16[16,3584]{1,0:T(8,128)(2,1)S(1)} collective-permute-done((bf16[16,3584]{1,0:T(8,128)(2,1)S(1)}, bf16[16,3584]{1,0:T(8,128)(2,1)S(1)}, u32[]{:S(2)}, u32[]{:S(2)}) %collective-permute-start.20) | collective-permute-done | bytes 114720 | tf_op jit(solution)/shard_map/ppermute | solution.py:320
  51.9 0.3 collective-permute-done.21
  52.2 0.8 %add_convert_fusion = bf16[16,3584]{1,0:T(8,128)(2,1)} fusion(bf16[16,3584]{1,0:T(8,128)(2,1)S(1)} %get-tuple-element.50, bf16[16,3584]{1,0:T(8,128)(2,1)S(1)} %collective-permute-done.22, bf16[16,3584]{1,0:T(8,128)(2,1)S(1)} %collective-permute-done.21, bf16[16,3584]{1,0:T(8,128)(2,1)S(1)} %collective-permute-done.20, ...), kind=kLoop, calls=%fused_computation | loop fusion | flops 802816 | bytes 917504 | tf_op jit(solution)/shard_map/convert_element_type | solution.py:387
  (36 shorter events, 0.8 us)
Async XLA Ops:
  1.1 10.3 %collective-permute-start.3 = (bf16[16,3712]{1,0:T(8,128)(2,1)S(1)}, bf16[16,3712]{1,0:T(8,128)(2,1)S(1)}, u32[]{:S(2)}, u32[]{:S(2)}) collective-permute-start(bf16[16,3712]{1,0:T(8,128)(2,1)S(1)} %norm.1.refs_0_), channel_id=1, source_target_pairs={{0,12},{1,13},{2,14},{3,15},{4,8},{5,9},{6,10},{7,11},{8,4},{9,5},... | collective-permute-start | bytes 356360 | tf_op jit(solution)/shard_map/ppermute | solution.py:320
  6.2 5.2 %collective-permute-start = (bf16[16,3712]{1,0:T(8,128)(2,1)S(1)}, bf16[16,3712]{1,0:T(8,128)(2,1)S(1)}, u32[]{:S(2)}, u32[]{:S(2)}) collective-permute-start(bf16[16,3712]{1,0:T(8,128)(2,1)S(1)} %norm.1.refs_0_), channel_id=1, source_target_pairs={{0,2},{1,3},{2,0},{3,1},{4,6},{5,7},{6,4},{7,5},{8,10},{9,11},{10,... | collective-permute-start | bytes 356360 | tf_op jit(solution)/shard_map/ppermute | solution.py:320
  11.4 7.3 %collective-permute-start.5 = (bf16[16,3712]{1,0:T(8,128)(2,1)S(1)}, bf16[16,3712]{1,0:T(8,128)(2,1)S(1)}, u32[]{:S(2)}, u32[]{:S(2)}) collective-permute-start(bf16[16,3712]{1,0:T(8,128)(2,1)S(1)} %pass_on.4.refs_0_), channel_id=1, source_target_pairs={{0,8},{1,9},{2,10},{3,11},{4,12},{5,13},{6,14},{7,15},{8,0},{9,1},... | collective-permute-start | bytes 356360 | tf_op jit(solution)/shard_map/ppermute | solution.py:320
  11.5 7.2 %collective-permute-start.4 = (bf16[16,3712]{1,0:T(8,128)(2,1)S(1)}, bf16[16,3712]{1,0:T(8,128)(2,1)S(1)}, u32[]{:S(2)}, u32[]{:S(2)}) collective-permute-start(bf16[16,3712]{1,0:T(8,128)(2,1)S(1)} %pass_on.5.refs_0_), channel_id=1, source_target_pairs={{0,2},{1,3},{2,0},{3,1},{4,6},{5,7},{6,4},{7,5},{8,10},{9,11},{10,... | collective-permute-start | bytes 356360 | tf_op jit(solution)/shard_map/ppermute | solution.py:320
  12.7 8.1 %collective-permute-start.2 = (bf16[16,3712]{1,0:T(8,128)(2,1)S(1)}, bf16[16,3712]{1,0:T(8,128)(2,1)S(1)}, u32[]{:S(2)}, u32[]{:S(2)}) collective-permute-start(bf16[16,3712]{1,0:T(8,128)(2,1)S(1)} %pass_on.4.refs_0_), channel_id=1, source_target_pairs={{0,6},{1,7},{2,4},{3,5},{4,2},{5,3},{6,0},{7,1},{8,14},{9,15},{10,... | collective-permute-start | bytes 356360 | tf_op jit(solution)/shard_map/ppermute | solution.py:320
  13.8 8.4 %collective-permute-start.1 = (bf16[16,3712]{1,0:T(8,128)(2,1)S(1)}, bf16[16,3712]{1,0:T(8,128)(2,1)S(1)}, u32[]{:S(2)}, u32[]{:S(2)}) collective-permute-start(bf16[16,3712]{1,0:T(8,128)(2,1)S(1)} %pass_on.4.refs_0_), channel_id=1, source_target_pairs={{0,4},{1,5},{2,6},{3,7},{4,0},{5,1},{6,2},{7,3},{8,12},{9,13},{10,... | collective-permute-start | bytes 356360 | tf_op jit(solution)/shard_map/ppermute | solution.py:320
  18.7 3.5 %collective-permute-start.6 = (bf16[16,3712]{1,0:T(8,128)(2,1)S(1)}, bf16[16,3712]{1,0:T(8,128)(2,1)S(1)}, u32[]{:S(2)}, u32[]{:S(2)}) collective-permute-start(bf16[16,3712]{1,0:T(8,128)(2,1)S(1)} %get-tuple-element.30.refs_12_), channel_id=1, source_target_pairs={{0,1},{1,0},{2,3},{3,2},{4,5},{5,4},{6,7},{7,6},{8,9},{9,8},{10,11... | collective-permute-start | bytes 356360 | tf_op jit(solution)/shard_map/ppermute | solution.py:320
  18.8 5.7 %collective-permute-start.11 = (bf16[16,3712]{1,0:T(8,128)(2,1)S(1)}, bf16[16,3712]{1,0:T(8,128)(2,1)S(1)}, u32[]{:S(2)}, u32[]{:S(2)}) collective-permute-start(bf16[16,3712]{1,0:T(8,128)(2,1)S(1)} %get-tuple-element.37.refs_8_), channel_id=1, source_target_pairs={{0,2},{1,3},{2,0},{3,1},{4,6},{5,7},{6,4},{7,5},{8,10},{9,11},{10,... | collective-permute-start | bytes 356360 | tf_op jit(solution)/shard_map/ppermute | solution.py:320
  22.1 5.0 %slice-start = ((s8[7340032]{0:T(1024)(128)(4,1)}), s8[4194304]{0:T(1024)(128)(4,1)S(1)}, s32[]{:S(2)}) async-start(s8[7340032]{0:T(1024)(128)(4,1)} %bitcast.2), calls=%async_computation | async-start | bytes 8388608
  22.2 2.2 %collective-permute-start.7 = (bf16[16,3712]{1,0:T(8,128)(2,1)S(1)}, bf16[16,3712]{1,0:T(8,128)(2,1)S(1)}, u32[]{:S(2)}, u32[]{:S(2)}) collective-permute-start(bf16[16,3712]{1,0:T(8,128)(2,1)S(1)} %get-tuple-element.31.refs_0_), channel_id=1, source_target_pairs={{0,1},{1,0},{2,3},{3,2},{4,5},{5,4},{6,7},{7,6},{8,9},{9,8},{10,11... | collective-permute-start | bytes 356360 | tf_op jit(solution)/shard_map/ppermute | solution.py:320
  22.2 2.7 %collective-permute-start.8 = (bf16[16,3712]{1,0:T(8,128)(2,1)S(1)}, bf16[16,3712]{1,0:T(8,128)(2,1)S(1)}, u32[]{:S(2)}, u32[]{:S(2)}) collective-permute-start(bf16[16,3712]{1,0:T(8,128)(2,1)S(1)} %get-tuple-element.32.refs_2_), channel_id=1, source_target_pairs={{0,1},{1,0},{2,3},{3,2},{4,5},{5,4},{6,7},{7,6},{8,9},{9,8},{10,11... | collective-permute-start | bytes 356360 | tf_op jit(solution)/shard_map/ppermute | solution.py:320
  22.7 2.2 %collective-permute-start.9 = (bf16[16,3712]{1,0:T(8,128)(2,1)S(1)}, bf16[16,3712]{1,0:T(8,128)(2,1)S(1)}, u32[]{:S(2)}, u32[]{:S(2)}) collective-permute-start(bf16[16,3712]{1,0:T(8,128)(2,1)S(1)} %get-tuple-element.33.refs_4_), channel_id=1, source_target_pairs={{0,1},{1,0},{2,3},{3,2},{4,5},{5,4},{6,7},{7,6},{8,9},{9,8},{10,11... | collective-permute-start | bytes 356360 | tf_op jit(solution)/shard_map/ppermute | solution.py:320
  22.8 2.2 %collective-permute-start.10 = (bf16[16,3712]{1,0:T(8,128)(2,1)S(1)}, bf16[16,3712]{1,0:T(8,128)(2,1)S(1)}, u32[]{:S(2)}, u32[]{:S(2)}) collective-permute-start(bf16[16,3712]{1,0:T(8,128)(2,1)S(1)} %get-tuple-element.34.refs_6_), channel_id=1, source_target_pairs={{0,1},{1,0},{2,3},{3,2},{4,5},{5,4},{6,7},{7,6},{8,9},{9,8},{10,11... | collective-permute-start | bytes 356360 | tf_op jit(solution)/shard_map/ppermute | solution.py:320
  24.4 2.7 %collective-permute-start.12 = (bf16[16,3712]{1,0:T(8,128)(2,1)S(1)}, bf16[16,3712]{1,0:T(8,128)(2,1)S(1)}, u32[]{:S(2)}, u32[]{:S(2)}) collective-permute-start(bf16[16,3712]{1,0:T(8,128)(2,1)S(1)} %get-tuple-element.37.refs_8_), channel_id=1, source_target_pairs={{0,1},{1,0},{2,3},{3,2},{4,5},{5,4},{6,7},{7,6},{8,9},{9,8},{10,11... | collective-permute-start | bytes 356360 | tf_op jit(solution)/shard_map/ppermute | solution.py:320
  24.4 2.7 %collective-permute-start.14 = (bf16[16,3712]{1,0:T(8,128)(2,1)S(1)}, bf16[16,3712]{1,0:T(8,128)(2,1)S(1)}, u32[]{:S(2)}, u32[]{:S(2)}) collective-permute-start(bf16[16,3712]{1,0:T(8,128)(2,1)S(1)} %get-tuple-element.38.refs_14_), channel_id=1, source_target_pairs={{0,1},{1,0},{2,3},{3,2},{4,5},{5,4},{6,7},{7,6},{8,9},{9,8},{10,11... | collective-permute-start | bytes 356360 | tf_op jit(solution)/shard_map/ppermute | solution.py:320
  24.9 2.2 %collective-permute-start.13 = (bf16[16,3712]{1,0:T(8,128)(2,1)S(1)}, bf16[16,3712]{1,0:T(8,128)(2,1)S(1)}, u32[]{:S(2)}, u32[]{:S(2)}) collective-permute-start(bf16[16,3712]{1,0:T(8,128)(2,1)S(1)} %collective-permute-done.11.refs_10_), channel_id=1, source_target_pairs={{0,1},{1,0},{2,3},{3,2},{4,5},{5,4},{6,7},{7,6},{8,9},{9,8},{10,11... | collective-permute-start | bytes 356360 | tf_op jit(solution)/shard_map/ppermute | solution.py:320
  25.0 2.2 %slice-start.1 = ((s8[7340032]{0:T(1024)(128)(4,1)}), s8[3145728]{0:T(1024)(128)(4,1)S(1)}, s32[]{:S(2)}) async-start(s8[7340032]{0:T(1024)(128)(4,1)} %bitcast.2), calls=%async_computation.1 | async-start | bytes 6291456
  30.4 21.8 %copy-start = (bf16[16,3584]{1,0:T(8,128)(2,1)S(1)}, bf16[16,3584]{1,0:T(8,128)(2,1)}, u32[]{:S(2)}) copy-start(bf16[16,3584]{1,0:T(8,128)(2,1)} %refs_0_.1) | copy-start | bytes 344068
  30.4 2.6 %collective-permute-start.15 = (bf16[128,3584]{1,0:T(8,128)(2,1)S(1)}, bf16[128,3584]{1,0:T(8,128)(2,1)S(1)}, u32[]{:S(2)}, u32[]{:S(2)}) collective-permute-start(bf16[128,3584]{1,0:T(8,128)(2,1)S(1)} %get-tuple-element.39), channel_id=1, source_target_pairs={{0,1},{1,0},{2,3},{3,2},{4,5},{5,4},{6,7},{7,6},{8,9},{9,8},{10,11... | collective-permute-start | bytes 2752520 | tf_op jit(solution)/shard_map/ppermute | solution.py:320
  33.2 6.0 %collective-permute-start.16 = (bf16[16,3584]{1,0:T(8,128)(2,1)S(1)}, bf16[16,3584]{1,0:T(8,128)(2,1)S(1)}, u32[]{:S(2)}, u32[]{:S(2)}) collective-permute-start(bf16[16,3584]{1,0:T(8,128)(2,1)S(1)} %get-tuple-element.43), channel_id=1, source_target_pairs={{0,2},{1,3},{2,0},{3,1},{4,6},{5,7},{6,4},{7,5},{8,10},{9,11},{10,... | collective-permute-start | bytes 344072 | tf_op jit(solution)/shard_map/ppermute | solution.py:320
  34.4 7.1 %collective-permute-start.19 = (bf16[16,3584]{1,0:T(8,128)(2,1)S(1)}, bf16[16,3584]{1,0:T(8,128)(2,1)S(1)}, u32[]{:S(2)}, u32[]{:S(2)}) collective-permute-start(bf16[16,3584]{1,0:T(8,128)(2,1)S(1)} %slice.7), channel_id=1, source_target_pairs={{0,4},{1,5},{2,6},{3,7},{4,0},{5,1},{6,2},{7,3},{8,12},{9,13},{10,... | collective-permute-start | bytes 344072 | tf_op jit(solution)/shard_map/ppermute | solution.py:320
  35.1 6.3 %collective-permute-start.18 = (bf16[16,3584]{1,0:T(8,128)(2,1)S(1)}, bf16[16,3584]{1,0:T(8,128)(2,1)S(1)}, u32[]{:S(2)}, u32[]{:S(2)}) collective-permute-start(bf16[16,3584]{1,0:T(8,128)(2,1)S(1)} %get-tuple-element.44), channel_id=1, source_target_pairs={{0,2},{1,3},{2,0},{3,1},{4,6},{5,7},{6,4},{7,5},{8,10},{9,11},{10,... | collective-permute-start | bytes 344072 | tf_op jit(solution)/shard_map/ppermute | solution.py:320
  39.3 7.9 %collective-permute-start.17 = (bf16[16,3584]{1,0:T(8,128)(2,1)S(1)}, bf16[16,3584]{1,0:T(8,128)(2,1)S(1)}, u32[]{:S(2)}, u32[]{:S(2)}) collective-permute-start(bf16[16,3584]{1,0:T(8,128)(2,1)S(1)} %add.32), channel_id=1, source_target_pairs={{0,12},{1,13},{2,14},{3,15},{4,8},{5,9},{6,10},{7,11},{8,4},{9,5},... | collective-permute-start | bytes 344072 | tf_op jit(solution)/shard_map/ppermute | solution.py:320
  41.5 10.4 %collective-permute-start.20 = (bf16[16,3584]{1,0:T(8,128)(2,1)S(1)}, bf16[16,3584]{1,0:T(8,128)(2,1)S(1)}, u32[]{:S(2)}, u32[]{:S(2)}) collective-permute-start(bf16[16,3584]{1,0:T(8,128)(2,1)S(1)} %get-tuple-element.47), channel_id=1, source_target_pairs={{0,8},{1,9},{2,10},{3,11},{4,12},{5,13},{6,14},{7,15},{8,0},{9,1},... | collective-permute-start | bytes 344072 | tf_op jit(solution)/shard_map/ppermute | solution.py:320
  44.1 8.0 %collective-permute-start.21 = (bf16[16,3584]{1,0:T(8,128)(2,1)S(1)}, bf16[16,3584]{1,0:T(8,128)(2,1)S(1)}, u32[]{:S(2)}, u32[]{:S(2)}) collective-permute-start(bf16[16,3584]{1,0:T(8,128)(2,1)S(1)} %get-tuple-element.48), channel_id=1, source_target_pairs={{0,6},{1,7},{2,4},{3,5},{4,2},{5,3},{6,0},{7,1},{8,14},{9,15},{10,... | collective-permute-start | bytes 344072 | tf_op jit(solution)/shard_map/ppermute | solution.py:320
  44.7 7.5 %collective-permute-start.22 = (bf16[16,3584]{1,0:T(8,128)(2,1)S(1)}, bf16[16,3584]{1,0:T(8,128)(2,1)S(1)}, u32[]{:S(2)}, u32[]{:S(2)}) collective-permute-start(bf16[16,3584]{1,0:T(8,128)(2,1)S(1)} %get-tuple-element.49), channel_id=1, source_target_pairs={{0,2},{1,3},{2,0},{3,1},{4,6},{5,7},{6,4},{7,5},{8,10},{9,11},{10,... | collective-permute-start | bytes 344072 | tf_op jit(solution)/shard_map/ppermute | solution.py:320

commit v4 on v3

--- a/solution.py
+++ b/solution.py
@@ -267,50 +267,29 @@
     return away, here
 
 
-def fold_kernel(got_ref, here_ref, *out_refs):
-    *away_refs, rest_ref = out_refs
-    rows = away_refs[0].shape[0]
-    for at, away_ref in enumerate(away_refs):
-        part = slice(at * rows, (at + 1) * rows)
-        total = got_ref[part, :].astype(jnp.float32) + here_ref[part, :].astype(jnp.float32)
-        away_ref[...] = total.astype(jnp.bfloat16)
-    rest = rest_ref.shape[0]
-    at = got_ref.shape[0] - rest
-    total = got_ref[at:, :].astype(jnp.float32) + here_ref[at:, :].astype(jnp.float32)
-    rest_ref[...] = total.astype(jnp.bfloat16)
-
-
-def fold(got, here, count):
-    total, width = got.shape
-    shape = jax.ShapeDtypeStruct
-    return pl.pallas_call(
-        fold_kernel,
-        out_shape=[shape((total // 2 // count, width), jnp.bfloat16)] * count
-        + [shape((total // 2, width), jnp.bfloat16)],
-        in_specs=[VMEM, VMEM],
-        out_specs=[VMEM] * (count + 1),
-        compiler_params=pltpu.CompilerParams(vmem_limit_bytes=6 << 20),
-        name="fold",
-    )(got, here)
-
-
-def add_kernel(at, got_ref, here_ref, *refs):
-    count = (len(refs) - 1) // 2
-    out_ref = refs[count]
-    rows = got_ref.shape[0]
-    here = here_ref[at : at + rows, :].astype(jnp.float32)
-    out_ref[...] = (got_ref[...].astype(jnp.float32) + here).astype(jnp.bfloat16)
-    for source, copy_ref in zip(refs[:count], refs[count + 1 :]):
-        copy_ref[...] = source[...]
-
-
-def add(got, here, at, *later):
-    return pl.pallas_call(
-        functools.partial(add_kernel, at),
-        out_shape=[jax.ShapeDtypeStruct(got.shape, jnp.bfloat16)] * (1 + len(later)),
+def add_kernel(pieces, got_ref, here_ref, *refs):
+    later = (len(refs) - len(pieces)) // 2
+    for piece, out_ref in zip(pieces, refs[later:]):
+        to = 0
+        for rows, columns in piece:
+            here = here_ref[slice(*rows), slice(*columns)].astype(jnp.float32)
+            got = got_ref[slice(*rows), slice(*columns)].astype(jnp.float32)
+            end = to + columns[1] - columns[0]
+            out_ref[:, to:end] = (got + here).astype(jnp.bfloat16)
+            to = end
+    for source, out_ref in zip(refs, refs[len(refs) - later :]):
+        out_ref[...] = source[...]
+
+
+def add(got, here, pieces, later=()):
+    shapes = [(piece[0][0][1] - piece[0][0][0], sum(c[1] - c[0] for _, c in piece)) for piece in pieces]
+    shapes += [array.shape for array in later]
+    return pl.pallas_call(
+        functools.partial(add_kernel, tuple(tuple(piece) for piece in pieces)),
+        out_shape=[jax.ShapeDtypeStruct(shape, jnp.bfloat16) for shape in shapes],
         in_specs=[VMEM] * (2 + len(later)),
-        out_specs=[VMEM] * (1 + len(later)),
-        compiler_params=limit(2),
+        out_specs=[VMEM] * len(shapes),
+        compiler_params=limit(2 if got.shape[0] <= 16 else 6 if got.shape[0] <= 128 else 16),
         name="add",
     )(got, here, *later)
 
@@ -364,24 +343,36 @@
     places = [(o < 8, o % 8 if o < 8 else o - 8) for o in order]
     near, late = [blocks[o] for o in range(8)], [blocks[o] for o in range(8, owners)]
     away, here = expert(down, hidden, near, late, parts, places)
-    *away, here = fold(swap(away, 1), here, len(far) + 1)
-    away = dict(zip((o for o in order if o & 3 == 0), away))
-    at_rows = {o: at * rows for at, o in enumerate(away)}
-    close, late = far[0], far[:0:-1]
-    got = {offset: swap(away[offset], 2) for offset in late}
-    beside = swap(here[at_rows[close] : at_rows[close] + rows], close)
-    later = [away[close], away[0], beside]
-    sent = []
-    for offset in late:
-        if offset == late[-1]:
-            block, *later = add(got[offset], here, at_rows[offset], *later)
-        else:
-            (block,) = add(got[offset], here, at_rows[offset])
-        sent.append(swap(block, offset))
-    sent += [swap(later[0], close ^ 2), swap(later[1], 2), later[2]]
-    mine = here[at_rows[0] :].astype(jnp.float32)
-    for block in sent:
-        mine = mine + block.astype(jnp.float32)
+    lead, *late = far[:0:-1]
+    close = far[0]
+    width = away.shape[1]
+    cut = width // lane * 4 // 8 * lane
+    keys = [o for o in order if o & 3 == 0]
+    half = len(keys) * rows
+    away_rows = {o: (at * rows, at * rows + rows) for at, o in enumerate(keys)}
+    here_rows = {o: (half + at * rows, half + at * rows + rows) for at, o in enumerate(keys)}
+    full, low, high = (0, width), (0, cut), (cut, width)
+    pieces = {}
+    for name, table in (("away", away_rows), ("here", here_rows)):
+        pieces[name] = [(table[lead], full), *((table[o], low) for o in late)]
+        pieces.update({(name, o): [(table[o], high)] for o in late})
+        pieces.update({(name, o): [(table[o], full)] for o in (close, 0)})
+    sums = dict(zip(pieces, add(swap(away, 1), here, list(pieces.values()))))
+    got = swap(sums["away"], 2)
+    direct = [swap(sums["here", o], o) for o in late]
+    direct += [swap(sums["away", o], o ^ 2) for o in late]
+    whole = [sums["here", 0], swap(sums["here", close], close)]
+    whole.append(swap(sums["away", close], close ^ 2))
+    later = [sums["away", 0]]
+    ends = [width + at * cut for at in range(len(late) + 1)]
+    parts = [full, *zip(ends, ends[1:])]
+    total, *lows, own = add(got, sums["here"], [[((0, rows), part)] for part in parts], later)
+    whole.append(swap(total, lead))
+    summed = [swap(array, o) for o, array in zip(late, lows)]
+    whole.append(swap(own, 2))
+    mine = sum(array.astype(jnp.float32) for array in whole)
+    halves = [sum(array.astype(jnp.float32) for array in part) for part in (summed, direct)]
+    mine = mine + jnp.concatenate(halves, axis=1)
     if tp > 1:
         mine = lax.psum_scatter(mine, "tp", scatter_dimension=0, tiled=True)
     return (resid.astype(jnp.float32) + mine).astype(jnp.bfloat16)

time: 53.1 us -> 51.8 us (0.976)
  waiting for transfers between devices: 13.9 us -> 9.66 us
  starting transfers between devices: 22.9 us -> 25.8 us
    ppermute x23 -> x24, waiting for transfers between devices: 13.9 us -> 9.66 us  [swap(): return lax.ppermute(block, 'ep', [(i, i ^ offset) for i in range(count)])]
    ppermute x23 -> x24, starting transfers between devices: 22.9 us -> 25.8 us  [swap(): return lax.ppermute(block, 'ep', [(i, i ^ offset) for i in range(count)])]
  transfers between devices with their start and end apart: 23 -> 24, of which waited for: 8 -> 7; matrix products, arithmetic and copies ran while one was open for 0% -> 0% of each run, Pallas kernels for 20% -> 21%
where the time goes in v4:
time: 51.8 us; the launch traced here: 51.6 us
  starting transfers between devices  25.8 us (50%)
  Pallas kernels  15.1 us (29%)
  waiting for transfers between devices  9.66 us (19%)
  other arithmetic  0.77 us (1%)
    ppermute x24, starting transfers between devices, swap(): return lax.ppermute(block, 'ep', [(i, i ^ offset) for i in range(count)])  25.8 us
    ppermute x24, waiting for transfers between devices, swap(): return lax.ppermute(block, 'ep', [(i, i ^ offset) for i in range(count)])  9.66 us
    pallas_call x2, Pallas kernels, unpack(): pl.pallas_call(functools.partial(unpack_kernel, first), out_shape=[jax.Sh...  7.17 us
    pallas_call x1, Pallas kernels, expert(): pl.pallas_call(functools.partial(away_kernel, len(near), len(far), order)...  3.18 us
    pallas_call x1, Pallas kernels, near_hidden(): pl.pallas_call(functools.partial(near_kernel, len(blocks), len(after)), o...  2.1 us
    pallas_call x1, Pallas kernels, expert(): pl.pallas_call(here_kernel, out_shape=shape((half, width), jnp.bfloat16),...  1.26 us
    pallas_call x1, Pallas kernels, norm(): pl.pallas_call(norm_kernel, out_shape=jax.ShapeDtypeStruct((rows, width +...  1.1 us
  transfers between devices with their start and end apart: 24, of which 7 were waited for; matrix products, arithmetic and copies ran while one was open for 0% of the time, Pallas kernels for 21%

profile of v4, /device:TPU:0, one launch (start us, length us, event | category | flops | bytes accessed | tf_op | source)
XLA Modules:
  0.0 51.6 jit_solution(6526982429730421274)
XLA Ops:
  0.0 1.1 %norm.1.refs_0_ = bf16[16,3712]{1,0:T(8,128)(2,1)S(1)} custom-call(bf16[16,3584]{1,0:T(8,128)(2,1)} %refs_0_.1, f32[3584]{0:T(1024)} %refs_1_.1, s32[8,16]{1,0:T(8,128)} %bitcast.4, bf16[8,16]{1,0:T(8,128)(2,1)} %bitcast.5), custom_call_target="tpu_custom_call" | custom-call | tf_op jit(solution)/shard_map/norm/pallas_call | solution.py:57
  1.1 5.1 %collective-permute-start.3 = (bf16[16,3712]{1,0:T(8,128)(2,1)S(1)}, bf16[16,3712]{1,0:T(8,128)(2,1)S(1)}, u32[]{:S(2)}, u32[]{:S(2)}) collective-permute-start(bf16[16,3712]{1,0:T(8,128)(2,1)S(1)} %norm.1.refs_0_), channel_id=1, source_target_pairs={{0,12},{1,13},{2,14},{3,15},{4,8},{5,9},{6,10},{7,11},{8,4},{9,5},... | collective-permute-start | bytes 356360 | tf_op jit(solution)/shard_map/ppermute | solution.py:299
  6.2 1.5 %collective-permute-start = (bf16[16,3712]{1,0:T(8,128)(2,1)S(1)}, bf16[16,3712]{1,0:T(8,128)(2,1)S(1)}, u32[]{:S(2)}, u32[]{:S(2)}) collective-permute-start(bf16[16,3712]{1,0:T(8,128)(2,1)S(1)} %norm.1.refs_0_), channel_id=1, source_target_pairs={{0,2},{1,3},{2,0},{3,1},{4,6},{5,7},{6,4},{7,5},{8,10},{9,11},{10,... | collective-permute-start | bytes 356360 | tf_op jit(solution)/shard_map/ppermute | solution.py:299
  7.7 3.6 %unpack.2 = (bf16[3584,1024]{1,0:T(8,128)(2,1)S(1)}, f32[8,128]{1,0:T(8,128)S(1)}) custom-call(bf16[1,3584,2,1024]{3,2,1,0:T(2,128)(2,1)} %packed_ref.3), custom_call_target="tpu_custom_call" | custom-call | bytes 16777216 | tf_op jit(solution)/shard_map/unpack/pallas_call | solution.py:104
  11.5 1.2 %collective-permute-start.4 = (bf16[16,3712]{1,0:T(8,128)(2,1)S(1)}, bf16[16,3712]{1,0:T(8,128)(2,1)S(1)}, u32[]{:S(2)}, u32[]{:S(2)}) collective-permute-start(bf16[16,3712]{1,0:T(8,128)(2,1)S(1)} %pass_on.5.refs_0_), channel_id=1, source_target_pairs={{0,2},{1,3},{2,0},{3,1},{4,6},{5,7},{6,4},{7,5},{8,10},{9,11},{10,... | collective-permute-start | bytes 356360 | tf_op jit(solution)/shard_map/ppermute | solution.py:299
  12.7 1.1 %collective-permute-start.2 = (bf16[16,3712]{1,0:T(8,128)(2,1)S(1)}, bf16[16,3712]{1,0:T(8,128)(2,1)S(1)}, u32[]{:S(2)}, u32[]{:S(2)}) collective-permute-start(bf16[16,3712]{1,0:T(8,128)(2,1)S(1)} %pass_on.4.refs_0_), channel_id=1, source_target_pairs={{0,6},{1,7},{2,4},{3,5},{4,2},{5,3},{6,0},{7,1},{8,14},{9,15},{10,... | collective-permute-start | bytes 356360 | tf_op jit(solution)/shard_map/ppermute | solution.py:299
  13.8 1.3 %collective-permute-start.1 = (bf16[16,3712]{1,0:T(8,128)(2,1)S(1)}, bf16[16,3712]{1,0:T(8,128)(2,1)S(1)}, u32[]{:S(2)}, u32[]{:S(2)}) collective-permute-start(bf16[16,3712]{1,0:T(8,128)(2,1)S(1)} %pass_on.4.refs_0_), channel_id=1, source_target_pairs={{0,4},{1,5},{2,6},{3,7},{4,0},{5,1},{6,2},{7,3},{8,12},{9,13},{10,... | collective-permute-start | bytes 356360 | tf_op jit(solution)/shard_map/ppermute | solution.py:299
  15.0 3.6 %unpack.3 = (bf16[3584,1024]{1,0:T(8,128)(2,1)S(1)}, f32[8,128]{1,0:T(8,128)S(1)}) custom-call(bf16[1,3584,2,1024]{3,2,1,0:T(2,128)(2,1)} %packed_ref.3, bf16[16,3712]{1,0:T(8,128)(2,1)S(1)} %pass_on.4.refs_0_), custom_call_target="tpu_custom_call" | custom-call | bytes 16777216 | tf_op jit(solution)/shard_map/unpack/pallas_call | solution.py:104
  18.8 1.2 %collective-permute-start.11 = (bf16[16,3712]{1,0:T(8,128)(2,1)S(1)}, bf16[16,3712]{1,0:T(8,128)(2,1)S(1)}, u32[]{:S(2)}, u32[]{:S(2)}) collective-permute-start(bf16[16,3712]{1,0:T(8,128)(2,1)S(1)} %get-tuple-element.39.refs_8_), channel_id=1, source_target_pairs={{0,2},{1,3},{2,0},{3,1},{4,6},{5,7},{6,4},{7,5},{8,10},{9,11},{10,... | collective-permute-start | bytes 356360 | tf_op jit(solution)/shard_map/ppermute | solution.py:299
  19.9 0.8 %collective-permute-done.2.refs_3_ = bf16[16,3712]{1,0:T(8,128)(2,1)S(1)} collective-permute-done((bf16[16,3712]{1,0:T(8,128)(2,1)S(1)}, bf16[16,3712]{1,0:T(8,128)(2,1)S(1)}, u32[]{:S(2)}, u32[]{:S(2)}) %collective-permute-start.2) | collective-permute-done | bytes 118816 | tf_op jit(solution)/shard_map/ppermute | solution.py:299
  20.8 1.4 %collective-permute-done.1.refs_2_ = bf16[16,3712]{1,0:T(8,128)(2,1)S(1)} collective-permute-done((bf16[16,3712]{1,0:T(8,128)(2,1)S(1)}, bf16[16,3712]{1,0:T(8,128)(2,1)S(1)}, u32[]{:S(2)}, u32[]{:S(2)}) %collective-permute-start.1) | collective-permute-done | bytes 118816 | tf_op jit(solution)/shard_map/ppermute | solution.py:299
  22.2 0.5 collective-permute-start.8
  22.8 0.4 collective-permute-start.10
  23.3 1.1 %collective-permute-done.11.refs_10_ = bf16[16,3712]{1,0:T(8,128)(2,1)S(1)} collective-permute-done((bf16[16,3712]{1,0:T(8,128)(2,1)S(1)}, bf16[16,3712]{1,0:T(8,128)(2,1)S(1)}, u32[]{:S(2)}, u32[]{:S(2)}) %collective-permute-start.11) | collective-permute-done | bytes 118816 | tf_op jit(solution)/shard_map/ppermute | solution.py:299
  24.4 0.5 collective-permute-start.14
  25.0 2.1 %near.1.near_hidden_ref = bf16[128,1024]{1,0:T(8,128)(2,1)S(1)} custom-call(bf16[16,3712]{1,0:T(8,128)(2,1)S(1)} %get-tuple-element.33.refs_0_, bf16[16,3712]{1,0:T(8,128)(2,1)S(1)} %collective-permute-done.7.refs_1_, bf16[16,3712]{1,0:T(8,128)(2,1)S(1)} %get-tuple-element.34.refs_2_, bf16[16,3712]{1,0:T(8,128)(2,1)S(1)} %collective-permute-done.8.refs_3_, ...), custom_call_target="tpu_custom_call" | custom-call | tf_op jit(solution)/shard_map/near/pallas_call | solution.py:169
  27.2 3.2 %away.1 = (bf16[128,3584]{1,0:T(8,128)(2,1)S(1)}, bf16[128,1024]{1,0:T(8,128)(2,1)S(1)}, f32[128,128]{1,0:T(8,128)S(1)}) custom-call(bf16[1,1024,3584]{2,1,0:T(8,128)(2,1)S(1)} %bitcast.3, bf16[128,1024]{1,0:T(8,128)(2,1)S(1)} %near.1.near_hidden_ref, bf16[16,3712]{1,0:T(8,128)(2,1)S(1)} %get-tuple-element.33.refs_0_, ...), custom_call_target="tpu_custom_call" | custom-call | flops 2818572288 | tf_op jit(solution)/shard_map/away/pallas_call | solution.py:236
  30.4 0.5 %collective-permute-start.15 = (bf16[128,3584]{1,0:T(8,128)(2,1)S(1)}, bf16[128,3584]{1,0:T(8,128)(2,1)S(1)}, u32[]{:S(2)}, u32[]{:S(2)}) collective-permute-start(bf16[128,3584]{1,0:T(8,128)(2,1)S(1)} %get-tuple-element.41), channel_id=1, source_target_pairs={{0,1},{1,0},{2,3},{3,2},{4,5},{5,4},{6,7},{7,6},{8,9},{9,8},{10,11... | collective-permute-start | bytes 2752520 | tf_op jit(solution)/shard_map/ppermute | solution.py:299
  30.9 1.3 %here.1.here_ref = bf16[128,3584]{1,0:T(8,128)(2,1)S(1)} custom-call(bf16[1,1024,3584]{2,1,0:T(8,128)(2,1)S(1)} %bitcast.3, bf16[128,1024]{1,0:T(8,128)(2,1)S(1)} %get-tuple-element.42.hidden_ref, f32[128,128]{1,0:T(8,128)S(1)} %get-tuple-element.43.share_ref), custom_call_target="tpu_custom_call" | custom-call | flops 939524096 | tf_op jit(solution)/shard_map/here/pallas_call | solution.py:256
  32.2 0.8 %collective-permute-done.15.got_ref = bf16[128,3584]{1,0:T(8,128)(2,1)S(1)} collective-permute-done((bf16[128,3584]{1,0:T(8,128)(2,1)S(1)}, bf16[128,3584]{1,0:T(8,128)(2,1)S(1)}, u32[]{:S(2)}, u32[]{:S(2)}) %collective-permute-start.15) | collective-permute-done | bytes 917536 | tf_op jit(solution)/shard_map/ppermute | solution.py:299
  33.2 1.2 %collective-permute-start.18 = (bf16[16,5376]{1,0:T(8,128)(2,1)S(1)}, bf16[16,5376]{1,0:T(8,128)(2,1)S(1)}, u32[]{:S(2)}, u32[]{:S(2)}) collective-permute-start(bf16[16,5376]{1,0:T(8,128)(2,1)S(1)} %get-tuple-element.47), channel_id=1, source_target_pairs={{0,2},{1,3},{2,0},{3,1},{4,6},{5,7},{6,4},{7,5},{8,10},{9,11},{10,... | collective-permute-start | bytes 516104 | tf_op jit(solution)/shard_map/ppermute | solution.py:299
  34.4 2.3 %collective-permute-start.22 = (bf16[16,1792]{1,0:T(8,128)(2,1)S(1)}, bf16[16,1792]{1,0:T(8,128)(2,1)S(1)}, u32[]{:S(2)}, u32[]{:S(2)}) collective-permute-start(bf16[16,1792]{1,0:T(8,128)(2,1)S(1)} %get-tuple-element.53), channel_id=1, source_target_pairs={{0,8},{1,9},{2,10},{3,11},{4,12},{5,13},{6,14},{7,15},{8,0},{9,1},... | collective-permute-start | bytes 172040 | tf_op jit(solution)/shard_map/ppermute | solution.py:299
  36.7 1.0 %collective-permute-start.23 = (bf16[16,1792]{1,0:T(8,128)(2,1)S(1)}, bf16[16,1792]{1,0:T(8,128)(2,1)S(1)}, u32[]{:S(2)}, u32[]{:S(2)}) collective-permute-start(bf16[16,1792]{1,0:T(8,128)(2,1)S(1)} %get-tuple-element.54), channel_id=1, source_target_pairs={{0,10},{1,11},{2,8},{3,9},{4,14},{5,15},{6,12},{7,13},{8,2},{9,3},... | collective-permute-start | bytes 172040 | tf_op jit(solution)/shard_map/ppermute | solution.py:299
  37.7 0.7 %collective-permute-start.16 = (bf16[16,3584]{1,0:T(8,128)(2,1)S(1)}, bf16[16,3584]{1,0:T(8,128)(2,1)S(1)}, u32[]{:S(2)}, u32[]{:S(2)}) collective-permute-start(bf16[16,3584]{1,0:T(8,128)(2,1)S(1)} %get-tuple-element.45), channel_id=1, source_target_pairs={{0,4},{1,5},{2,6},{3,7},{4,0},{5,1},{6,2},{7,3},{8,12},{9,13},{10,... | collective-permute-start | bytes 344072 | tf_op jit(solution)/shard_map/ppermute | solution.py:299
  38.4 1.8 %collective-permute-start.17 = (bf16[16,3584]{1,0:T(8,128)(2,1)S(1)}, bf16[16,3584]{1,0:T(8,128)(2,1)S(1)}, u32[]{:S(2)}, u32[]{:S(2)}) collective-permute-start(bf16[16,3584]{1,0:T(8,128)(2,1)S(1)} %get-tuple-element.46), channel_id=1, source_target_pairs={{0,6},{1,7},{2,4},{3,5},{4,2},{5,3},{6,0},{7,1},{8,14},{9,15},{10,... | collective-permute-start | bytes 344072 | tf_op jit(solution)/shard_map/ppermute | solution.py:299
  40.3 3.3 %collective-permute-start.21 = (bf16[16,1792]{1,0:T(8,128)(2,1)S(1)}, bf16[16,1792]{1,0:T(8,128)(2,1)S(1)}, u32[]{:S(2)}, u32[]{:S(2)}) collective-permute-start(bf16[16,1792]{1,0:T(8,128)(2,1)S(1)} %get-tuple-element.52), channel_id=1, source_target_pairs={{0,8},{1,9},{2,10},{3,11},{4,12},{5,13},{6,14},{7,15},{8,0},{9,1},... | collective-permute-start | bytes 172040 | tf_op jit(solution)/shard_map/ppermute | solution.py:299
  43.6 0.7 %collective-permute-start.19 = (bf16[16,3584]{1,0:T(8,128)(2,1)S(1)}, bf16[16,3584]{1,0:T(8,128)(2,1)S(1)}, u32[]{:S(2)}, u32[]{:S(2)}) collective-permute-start(bf16[16,3584]{1,0:T(8,128)(2,1)S(1)} %get-tuple-element.50), channel_id=1, source_target_pairs={{0,12},{1,13},{2,14},{3,15},{4,8},{5,9},{6,10},{7,11},{8,4},{9,5},... | collective-permute-start | bytes 344072 | tf_op jit(solution)/shard_map/ppermute | solution.py:299
  44.3 1.1 %collective-permute-start.20 = (bf16[16,3584]{1,0:T(8,128)(2,1)S(1)}, bf16[16,3584]{1,0:T(8,128)(2,1)S(1)}, u32[]{:S(2)}, u32[]{:S(2)}) collective-permute-start(bf16[16,3584]{1,0:T(8,128)(2,1)S(1)} %get-tuple-element.51), channel_id=1, source_target_pairs={{0,2},{1,3},{2,0},{3,1},{4,6},{5,7},{6,4},{7,5},{8,10},{9,11},{10,... | collective-permute-start | bytes 344072 | tf_op jit(solution)/shard_map/ppermute | solution.py:299
  45.4 1.7 %collective-permute-done.21 = bf16[16,1792]{1,0:T(8,128)(2,1)S(1)} collective-permute-done((bf16[16,1792]{1,0:T(8,128)(2,1)S(1)}, bf16[16,1792]{1,0:T(8,128)(2,1)S(1)}, u32[]{:S(2)}, u32[]{:S(2)}) %collective-permute-start.21) | collective-permute-done | bytes 57376 | tf_op jit(solution)/shard_map/ppermute | solution.py:299
  47.1 2.0 %collective-permute-done.17 = bf16[16,3584]{1,0:T(8,128)(2,1)S(1)} collective-permute-done((bf16[16,3584]{1,0:T(8,128)(2,1)S(1)}, bf16[16,3584]{1,0:T(8,128)(2,1)S(1)}, u32[]{:S(2)}, u32[]{:S(2)}) %collective-permute-start.17) | collective-permute-done | bytes 114720 | tf_op jit(solution)/shard_map/ppermute | solution.py:299
  49.1 1.7 %collective-permute-done.19 = bf16[16,3584]{1,0:T(8,128)(2,1)S(1)} collective-permute-done((bf16[16,3584]{1,0:T(8,128)(2,1)S(1)}, bf16[16,3584]{1,0:T(8,128)(2,1)S(1)}, u32[]{:S(2)}, u32[]{:S(2)}) %collective-permute-start.19) | collective-permute-done | bytes 114720 | tf_op jit(solution)/shard_map/ppermute | solution.py:299
  50.9 0.7 %fusion.1 = bf16[16,3584]{1,0:T(8,128)(2,1)} fusion(f32[16,1792]{1,0:T(8,128)S(1)} %convert_add_fusion, f32[16,1792]{1,0:T(8,128)S(1)} %convert_element_type.36, bf16[16,3584]{1,0:T(8,128)(2,1)S(1)} %collective-permute-done.20, bf16[16,3584]{1,0:T(8,128)(2,1)S(1)} %collective-permute-done.19, bf16[16,3584]{1,0:T(8,128)(2,1)S(1)} %collective-permute-done.17, ...), kind=kLoop, calls=%fused_computation.2 | loop fusion | flops 802816 | bytes 1032192 | tf_op jit(solution)/shard_map/convert_element_type | solution.py:378
  (38 shorter events, 0.8 us)
Async XLA Ops:
  1.1 10.3 %collective-permute-start.3 = (bf16[16,3712]{1,0:T(8,128)(2,1)S(1)}, bf16[16,3712]{1,0:T(8,128)(2,1)S(1)}, u32[]{:S(2)}, u32[]{:S(2)}) collective-permute-start(bf16[16,3712]{1,0:T(8,128)(2,1)S(1)} %norm.1.refs_0_), channel_id=1, source_target_pairs={{0,12},{1,13},{2,14},{3,15},{4,8},{5,9},{6,10},{7,11},{8,4},{9,5},... | collective-permute-start | bytes 356360 | tf_op jit(solution)/shard_map/ppermute | solution.py:299
  6.2 5.2 %collective-permute-start = (bf16[16,3712]{1,0:T(8,128)(2,1)S(1)}, bf16[16,3712]{1,0:T(8,128)(2,1)S(1)}, u32[]{:S(2)}, u32[]{:S(2)}) collective-permute-start(bf16[16,3712]{1,0:T(8,128)(2,1)S(1)} %norm.1.refs_0_), channel_id=1, source_target_pairs={{0,2},{1,3},{2,0},{3,1},{4,6},{5,7},{6,4},{7,5},{8,10},{9,11},{10,... | collective-permute-start | bytes 356360 | tf_op jit(solution)/shard_map/ppermute | solution.py:299
  11.4 7.3 %collective-permute-start.5 = (bf16[16,3712]{1,0:T(8,128)(2,1)S(1)}, bf16[16,3712]{1,0:T(8,128)(2,1)S(1)}, u32[]{:S(2)}, u32[]{:S(2)}) collective-permute-start(bf16[16,3712]{1,0:T(8,128)(2,1)S(1)} %pass_on.4.refs_0_), channel_id=1, source_target_pairs={{0,8},{1,9},{2,10},{3,11},{4,12},{5,13},{6,14},{7,15},{8,0},{9,1},... | collective-permute-start | bytes 356360 | tf_op jit(solution)/shard_map/ppermute | solution.py:299
  11.5 7.2 %collective-permute-start.4 = (bf16[16,3712]{1,0:T(8,128)(2,1)S(1)}, bf16[16,3712]{1,0:T(8,128)(2,1)S(1)}, u32[]{:S(2)}, u32[]{:S(2)}) collective-permute-start(bf16[16,3712]{1,0:T(8,128)(2,1)S(1)} %pass_on.5.refs_0_), channel_id=1, source_target_pairs={{0,2},{1,3},{2,0},{3,1},{4,6},{5,7},{6,4},{7,5},{8,10},{9,11},{10,... | collective-permute-start | bytes 356360 | tf_op jit(solution)/shard_map/ppermute | solution.py:299
  12.7 8.1 %collective-permute-start.2 = (bf16[16,3712]{1,0:T(8,128)(2,1)S(1)}, bf16[16,3712]{1,0:T(8,128)(2,1)S(1)}, u32[]{:S(2)}, u32[]{:S(2)}) collective-permute-start(bf16[16,3712]{1,0:T(8,128)(2,1)S(1)} %pass_on.4.refs_0_), channel_id=1, source_target_pairs={{0,6},{1,7},{2,4},{3,5},{4,2},{5,3},{6,0},{7,1},{8,14},{9,15},{10,... | collective-permute-start | bytes 356360 | tf_op jit(solution)/shard_map/ppermute | solution.py:299
  13.8 8.4 %collective-permute-start.1 = (bf16[16,3712]{1,0:T(8,128)(2,1)S(1)}, bf16[16,3712]{1,0:T(8,128)(2,1)S(1)}, u32[]{:S(2)}, u32[]{:S(2)}) collective-permute-start(bf16[16,3712]{1,0:T(8,128)(2,1)S(1)} %pass_on.4.refs_0_), channel_id=1, source_target_pairs={{0,4},{1,5},{2,6},{3,7},{4,0},{5,1},{6,2},{7,3},{8,12},{9,13},{10,... | collective-permute-start | bytes 356360 | tf_op jit(solution)/shard_map/ppermute | solution.py:299
  18.7 3.5 %collective-permute-start.6 = (bf16[16,3712]{1,0:T(8,128)(2,1)S(1)}, bf16[16,3712]{1,0:T(8,128)(2,1)S(1)}, u32[]{:S(2)}, u32[]{:S(2)}) collective-permute-start(bf16[16,3712]{1,0:T(8,128)(2,1)S(1)} %get-tuple-element.32.refs_12_), channel_id=1, source_target_pairs={{0,1},{1,0},{2,3},{3,2},{4,5},{5,4},{6,7},{7,6},{8,9},{9,8},{10,11... | collective-permute-start | bytes 356360 | tf_op jit(solution)/shard_map/ppermute | solution.py:299
  18.8 5.7 %collective-permute-start.11 = (bf16[16,3712]{1,0:T(8,128)(2,1)S(1)}, bf16[16,3712]{1,0:T(8,128)(2,1)S(1)}, u32[]{:S(2)}, u32[]{:S(2)}) collective-permute-start(bf16[16,3712]{1,0:T(8,128)(2,1)S(1)} %get-tuple-element.39.refs_8_), channel_id=1, source_target_pairs={{0,2},{1,3},{2,0},{3,1},{4,6},{5,7},{6,4},{7,5},{8,10},{9,11},{10,... | collective-permute-start | bytes 356360 | tf_op jit(solution)/shard_map/ppermute | solution.py:299
  22.1 5.0 %slice-start = ((s8[7340032]{0:T(1024)(128)(4,1)}), s8[4194304]{0:T(1024)(128)(4,1)S(1)}, s32[]{:S(2)}) async-start(s8[7340032]{0:T(1024)(128)(4,1)} %bitcast.2), calls=%async_computation | async-start | bytes 8388608
  22.2 2.2 %collective-permute-start.7 = (bf16[16,3712]{1,0:T(8,128)(2,1)S(1)}, bf16[16,3712]{1,0:T(8,128)(2,1)S(1)}, u32[]{:S(2)}, u32[]{:S(2)}) collective-permute-start(bf16[16,3712]{1,0:T(8,128)(2,1)S(1)} %get-tuple-element.33.refs_0_), channel_id=1, source_target_pairs={{0,1},{1,0},{2,3},{3,2},{4,5},{5,4},{6,7},{7,6},{8,9},{9,8},{10,11... | collective-permute-start | bytes 356360 | tf_op jit(solution)/shard_map/ppermute | solution.py:299
  22.2 2.7 %collective-permute-start.8 = (bf16[16,3712]{1,0:T(8,128)(2,1)S(1)}, bf16[16,3712]{1,0:T(8,128)(2,1)S(1)}, u32[]{:S(2)}, u32[]{:S(2)}) collective-permute-start(bf16[16,3712]{1,0:T(8,128)(2,1)S(1)} %get-tuple-element.34.refs_2_), channel_id=1, source_target_pairs={{0,1},{1,0},{2,3},{3,2},{4,5},{5,4},{6,7},{7,6},{8,9},{9,8},{10,11... | collective-permute-start | bytes 356360 | tf_op jit(solution)/shard_map/ppermute | solution.py:299
  22.7 2.2 %collective-permute-start.9 = (bf16[16,3712]{1,0:T(8,128)(2,1)S(1)}, bf16[16,3712]{1,0:T(8,128)(2,1)S(1)}, u32[]{:S(2)}, u32[]{:S(2)}) collective-permute-start(bf16[16,3712]{1,0:T(8,128)(2,1)S(1)} %get-tuple-element.35.refs_4_), channel_id=1, source_target_pairs={{0,1},{1,0},{2,3},{3,2},{4,5},{5,4},{6,7},{7,6},{8,9},{9,8},{10,11... | collective-permute-start | bytes 356360 | tf_op jit(solution)/shard_map/ppermute | solution.py:299
  22.8 2.2 %collective-permute-start.10 = (bf16[16,3712]{1,0:T(8,128)(2,1)S(1)}, bf16[16,3712]{1,0:T(8,128)(2,1)S(1)}, u32[]{:S(2)}, u32[]{:S(2)}) collective-permute-start(bf16[16,3712]{1,0:T(8,128)(2,1)S(1)} %get-tuple-element.36.refs_6_), channel_id=1, source_target_pairs={{0,1},{1,0},{2,3},{3,2},{4,5},{5,4},{6,7},{7,6},{8,9},{9,8},{10,11... | collective-permute-start | bytes 356360 | tf_op jit(solution)/shard_map/ppermute | solution.py:299
  24.4 2.7 %collective-permute-start.12 = (bf16[16,3712]{1,0:T(8,128)(2,1)S(1)}, bf16[16,3712]{1,0:T(8,128)(2,1)S(1)}, u32[]{:S(2)}, u32[]{:S(2)}) collective-permute-start(bf16[16,3712]{1,0:T(8,128)(2,1)S(1)} %get-tuple-element.39.refs_8_), channel_id=1, source_target_pairs={{0,1},{1,0},{2,3},{3,2},{4,5},{5,4},{6,7},{7,6},{8,9},{9,8},{10,11... | collective-permute-start | bytes 356360 | tf_op jit(solution)/shard_map/ppermute | solution.py:299
  24.4 2.7 %collective-permute-start.14 = (bf16[16,3712]{1,0:T(8,128)(2,1)S(1)}, bf16[16,3712]{1,0:T(8,128)(2,1)S(1)}, u32[]{:S(2)}, u32[]{:S(2)}) collective-permute-start(bf16[16,3712]{1,0:T(8,128)(2,1)S(1)} %get-tuple-element.40.refs_14_), channel_id=1, source_target_pairs={{0,1},{1,0},{2,3},{3,2},{4,5},{5,4},{6,7},{7,6},{8,9},{9,8},{10,11... | collective-permute-start | bytes 356360 | tf_op jit(solution)/shard_map/ppermute | solution.py:299
  24.9 2.2 %collective-permute-start.13 = (bf16[16,3712]{1,0:T(8,128)(2,1)S(1)}, bf16[16,3712]{1,0:T(8,128)(2,1)S(1)}, u32[]{:S(2)}, u32[]{:S(2)}) collective-permute-start(bf16[16,3712]{1,0:T(8,128)(2,1)S(1)} %collective-permute-done.11.refs_10_), channel_id=1, source_target_pairs={{0,1},{1,0},{2,3},{3,2},{4,5},{5,4},{6,7},{7,6},{8,9},{9,8},{10,11... | collective-permute-start | bytes 356360 | tf_op jit(solution)/shard_map/ppermute | solution.py:299
  25.0 2.2 %slice-start.1 = ((s8[7340032]{0:T(1024)(128)(4,1)}), s8[3145728]{0:T(1024)(128)(4,1)S(1)}, s32[]{:S(2)}) async-start(s8[7340032]{0:T(1024)(128)(4,1)} %bitcast.2), calls=%async_computation.1 | async-start | bytes 6291456
  30.4 20.5 %copy-start = (bf16[16,3584]{1,0:T(8,128)(2,1)S(1)}, bf16[16,3584]{1,0:T(8,128)(2,1)}, u32[]{:S(2)}) copy-start(bf16[16,3584]{1,0:T(8,128)(2,1)} %refs_0_.1) | copy-start | bytes 344068
  30.4 2.6 %collective-permute-start.15 = (bf16[128,3584]{1,0:T(8,128)(2,1)S(1)}, bf16[128,3584]{1,0:T(8,128)(2,1)S(1)}, u32[]{:S(2)}, u32[]{:S(2)}) collective-permute-start(bf16[128,3584]{1,0:T(8,128)(2,1)S(1)} %get-tuple-element.41), channel_id=1, source_target_pairs={{0,1},{1,0},{2,3},{3,2},{4,5},{5,4},{6,7},{7,6},{8,9},{9,8},{10,11... | collective-permute-start | bytes 2752520 | tf_op jit(solution)/shard_map/ppermute | solution.py:299
  33.2 7.0 %collective-permute-start.18 = (bf16[16,5376]{1,0:T(8,128)(2,1)S(1)}, bf16[16,5376]{1,0:T(8,128)(2,1)S(1)}, u32[]{:S(2)}, u32[]{:S(2)}) collective-permute-start(bf16[16,5376]{1,0:T(8,128)(2,1)S(1)} %get-tuple-element.47), channel_id=1, source_target_pairs={{0,2},{1,3},{2,0},{3,1},{4,6},{5,7},{6,4},{7,5},{8,10},{9,11},{10,... | collective-permute-start | bytes 516104 | tf_op jit(solution)/shard_map/ppermute | solution.py:299
  34.4 9.2 %collective-permute-start.22 = (bf16[16,1792]{1,0:T(8,128)(2,1)S(1)}, bf16[16,1792]{1,0:T(8,128)(2,1)S(1)}, u32[]{:S(2)}, u32[]{:S(2)}) collective-permute-start(bf16[16,1792]{1,0:T(8,128)(2,1)S(1)} %get-tuple-element.53), channel_id=1, source_target_pairs={{0,8},{1,9},{2,10},{3,11},{4,12},{5,13},{6,14},{7,15},{8,0},{9,1},... | collective-permute-start | bytes 172040 | tf_op jit(solution)/shard_map/ppermute | solution.py:299
  36.7 7.6 %collective-permute-start.23 = (bf16[16,1792]{1,0:T(8,128)(2,1)S(1)}, bf16[16,1792]{1,0:T(8,128)(2,1)S(1)}, u32[]{:S(2)}, u32[]{:S(2)}) collective-permute-start(bf16[16,1792]{1,0:T(8,128)(2,1)S(1)} %get-tuple-element.54), channel_id=1, source_target_pairs={{0,10},{1,11},{2,8},{3,9},{4,14},{5,15},{6,12},{7,13},{8,2},{9,3},... | collective-permute-start | bytes 172040 | tf_op jit(solution)/shard_map/ppermute | solution.py:299
  37.7 9.4 %collective-permute-start.16 = (bf16[16,3584]{1,0:T(8,128)(2,1)S(1)}, bf16[16,3584]{1,0:T(8,128)(2,1)S(1)}, u32[]{:S(2)}, u32[]{:S(2)}) collective-permute-start(bf16[16,3584]{1,0:T(8,128)(2,1)S(1)} %get-tuple-element.45), channel_id=1, source_target_pairs={{0,4},{1,5},{2,6},{3,7},{4,0},{5,1},{6,2},{7,3},{8,12},{9,13},{10,... | collective-permute-start | bytes 344072 | tf_op jit(solution)/shard_map/ppermute | solution.py:299
  38.4 10.7 %collective-permute-start.17 = (bf16[16,3584]{1,0:T(8,128)(2,1)S(1)}, bf16[16,3584]{1,0:T(8,128)(2,1)S(1)}, u32[]{:S(2)}, u32[]{:S(2)}) collective-permute-start(bf16[16,3584]{1,0:T(8,128)(2,1)S(1)} %get-tuple-element.46), channel_id=1, source_target_pairs={{0,6},{1,7},{2,4},{3,5},{4,2},{5,3},{6,0},{7,1},{8,14},{9,15},{10,... | collective-permute-start | bytes 344072 | tf_op jit(solution)/shard_map/ppermute | solution.py:299
  40.3 6.8 %collective-permute-start.21 = (bf16[16,1792]{1,0:T(8,128)(2,1)S(1)}, bf16[16,1792]{1,0:T(8,128)(2,1)S(1)}, u32[]{:S(2)}, u32[]{:S(2)}) collective-permute-start(bf16[16,1792]{1,0:T(8,128)(2,1)S(1)} %get-tuple-element.52), channel_id=1, source_target_pairs={{0,8},{1,9},{2,10},{3,11},{4,12},{5,13},{6,14},{7,15},{8,0},{9,1},... | collective-permute-start | bytes 172040 | tf_op jit(solution)/shard_map/ppermute | solution.py:299
  43.6 7.3 %collective-permute-start.19 = (bf16[16,3584]{1,0:T(8,128)(2,1)S(1)}, bf16[16,3584]{1,0:T(8,128)(2,1)S(1)}, u32[]{:S(2)}, u32[]{:S(2)}) collective-permute-start(bf16[16,3584]{1,0:T(8,128)(2,1)S(1)} %get-tuple-element.50), channel_id=1, source_target_pairs={{0,12},{1,13},{2,14},{3,15},{4,8},{5,9},{6,10},{7,11},{8,4},{9,5},... | collective-permute-start | bytes 344072 | tf_op jit(solution)/shard_map/ppermute | solution.py:299
  44.3 6.6 %collective-permute-start.20 = (bf16[16,3584]{1,0:T(8,128)(2,1)S(1)}, bf16[16,3584]{1,0:T(8,128)(2,1)S(1)}, u32[]{:S(2)}, u32[]{:S(2)}) collective-permute-start(bf16[16,3584]{1,0:T(8,128)(2,1)S(1)} %get-tuple-element.51), channel_id=1, source_target_pairs={{0,2},{1,3},{2,0},{3,1},{4,6},{5,7},{6,4},{7,5},{8,10},{9,11},{10,... | collective-permute-start | bytes 344072 | tf_op jit(solution)/shard_map/ppermute | solution.py:299

commit v5 on v4

--- a/solution.py
+++ b/solution.py
@@ -119,21 +119,29 @@
     )(in_hbm(packed), *after)
 
 
-def pass_kernel(*refs):
-    count = (len(refs) - 1) // 2
-    for source, out_ref in zip(refs[:count], refs[count + 1 :]):
-        out_ref[...] = source[...]
-
-
-def pass_on(blocks, after):
-    return pl.pallas_call(
-        pass_kernel,
-        out_shape=[jax.ShapeDtypeStruct(b.shape, b.dtype) for b in blocks],
-        in_specs=[VMEM] * len(blocks) + [ANY],
-        out_specs=[VMEM] * len(blocks),
-        compiler_params=limit(2),
-        name="pass_on",
-    )(*blocks, after)
+def join_kernel(sizes, *refs):
+    sources, out_refs = refs[: sum(sizes)], refs[-len(sizes) :]
+    at = 0
+    for size, out_ref in zip(sizes, out_refs):
+        to = 0
+        for source in sources[at : at + size]:
+            rows = source.shape[0]
+            out_ref[to : to + rows, :] = source[...]
+            to += rows
+        at += size
+
+
+def join(groups, after):
+    blocks = [block for group in groups for block in group]
+    shapes = [(sum(b.shape[0] for b in group), group[0].shape[1]) for group in groups]
+    return pl.pallas_call(
+        functools.partial(join_kernel, tuple(len(group) for group in groups)),
+        out_shape=[jax.ShapeDtypeStruct(shape, jnp.bfloat16) for shape in shapes],
+        in_specs=[VMEM] * len(blocks) + [ANY] * len(after),
+        out_specs=[VMEM] * len(groups),
+        compiler_params=limit(4 if len(blocks) < 8 else 12),
+        name="join",
+    )(*blocks, *after)
 
 
 def hidden_rows(rows_ref, gu_refs, hidden, at, tile):
@@ -151,30 +159,48 @@
             to += step
 
 
-def near_kernel(count, after, *refs):
-    block_refs, gu_refs = refs[:count], refs[count : -2 - after]
-    hidden, rows_ref = refs[-2:]
-    size = block_refs[0].shape[0]
-    for at, block_ref in enumerate(block_refs):
-        rows_ref[at * size : (at + 1) * size, :] = block_ref[...]
-    tile = min(256, size * count)
-    for at in range(0, size * count, tile):
-        hidden_rows(rows_ref, gu_refs, hidden, at, tile)
-
-
-def near_hidden(blocks, halves, after):
-    size, wide = blocks[0].shape
-    count = size * len(blocks)
+def fill(rows_ref, block_refs):
+    to = 0
+    for block_ref in block_refs:
+        rows = block_ref.shape[0]
+        rows_ref[to : to + rows, :] = block_ref[...]
+        to += rows
+
+
+def hidden_and_share(rows_ref, gu_refs, hidden, share_ref):
+    rows = rows_ref.shape[0]
+    width = gu_refs[0].shape[0]
+    tile = min(256, rows)
+    for at in range(0, rows, tile):
+        hidden_rows(rows_ref, gu_refs, hidden, at, min(tile, rows - at))
+    shares = rows_ref[:, width:].astype(jnp.float32)
+    lanes = lax.broadcasted_iota(jnp.int32, shares.shape, 1)
+    mine = jnp.where(lanes == lax.axis_index("ep"), shares, 0.0)
+    share_ref[...] = jnp.broadcast_to(jnp.sum(mine, axis=1, keepdims=True), shares.shape)
+
+
+def hidden_kernel(count, after, *refs):
+    block_refs, gu_refs = refs[:count], refs[count : -3 - after]
+    hidden, share_ref, rows_ref = refs[-3:]
+    fill(rows_ref, block_refs)
+    hidden_and_share(rows_ref, gu_refs, hidden, share_ref)
+
+
+def hidden_of(blocks, halves, after):
+    count, wide = sum(b.shape[0] for b in blocks), blocks[0].shape[1]
     width, inner = halves[0].shape[0], sum(h.shape[1] // 2 for h in halves)
     return pl.pallas_call(
-        functools.partial(near_kernel, len(blocks), len(after)),
-        out_shape=jax.ShapeDtypeStruct((count, inner), jnp.bfloat16),
+        functools.partial(hidden_kernel, len(blocks), len(after)),
+        out_shape=[
+            jax.ShapeDtypeStruct((count, inner), jnp.bfloat16),
+            jax.ShapeDtypeStruct((count, lane), jnp.float32),
+        ],
         in_specs=[VMEM] * (len(blocks) + len(halves)) + [ANY] * len(after),
-        out_specs=VMEM,
+        out_specs=[VMEM, VMEM],
         scratch_shapes=[pltpu.VMEM((count, wide), jnp.bfloat16)],
-        compiler_params=limit(6),
+        compiler_params=limit(6 if count <= 256 else 16),
         cost_estimate=pl.CostEstimate(flops=0, bytes_accessed=0, transcendentals=0),
-        name="near",
+        name="hidden",
     )(*blocks, *halves, *after)
 
 
@@ -194,73 +220,67 @@
             out_ref[at : at + tile, n : n + step] = terms
 
 
-def away_kernel(near_count, far_count, order, down_ref, near_hidden_ref, *refs):
-    near_refs, far_refs = refs[:near_count], refs[near_count : near_count + far_count]
-    gu_refs = refs[near_count + far_count : -6]
-    away_ref, here_hidden, here_share, rows_ref, far_hidden, away_hidden = refs[-6:]
-    width = down_ref.shape[2]
-    size = near_refs[0].shape[0]
-    for at, block_ref in enumerate(far_refs):
-        rows_ref[at * size : (at + 1) * size, :] = block_ref[...]
-    tile = min(256, size * far_count)
-    for at in range(0, size * far_count, tile):
-        hidden_rows(rows_ref, gu_refs, far_hidden, at, tile)
-    half = len(order) // 2
-    lanes = lax.broadcasted_iota(jnp.int32, (size, lane), 1)
-    parts = []
-    for to, (near, at) in enumerate(order):
-        source = near_hidden_ref if near else far_hidden
-        block = (near_refs if near else far_refs)[at][:, width:].astype(jnp.float32)
-        mine = jnp.where(lanes == lax.axis_index("ep"), block, 0.0)
-        share = jnp.sum(mine, axis=1, keepdims=True)
-        place = slice(to % half * size, (to % half + 1) * size)
-        if to < half:
-            away_hidden[place, :] = source[at * size : (at + 1) * size, :]
-            parts.append(share)
+def away_kernel(sets, count, places, down_ref, *refs):
+    hidden_refs, share_refs, refs = refs[:sets], refs[sets : 2 * sets], refs[2 * sets :]
+    block_refs, gu_refs = refs[:count], refs[count:-7]
+    away_ref, here_hidden, here_share, last_rows, last_hidden, last_share, hidden = refs[-7:]
+    half = away_ref.shape[0]
+    size = 2 * half // len(places)
+    fill(last_rows, block_refs)
+    hidden_and_share(last_rows, gu_refs, last_hidden, last_share)
+    hidden_refs = (*hidden_refs, last_hidden)
+    share_refs = (*share_refs, last_share)
+    shares = []
+    for to, (which, at) in enumerate(places):
+        part = slice(at, at + size)
+        place = slice(to * size % half, to * size % half + size)
+        if to * size < half:
+            hidden[place, :] = hidden_refs[which][part, :]
+            shares.append(share_refs[which][part, :])
         else:
-            here_hidden[place, :] = source[at * size : (at + 1) * size, :]
-            here_share[place, :] = jnp.broadcast_to(share, (size, lane))
-    down_rows(away_hidden, jnp.concatenate(parts, axis=0), down_ref, away_ref)
+            here_hidden[place, :] = hidden_refs[which][part, :]
+            here_share[place, :] = share_refs[which][part, :]
+    down_rows(hidden, jnp.concatenate(shares, axis=0), down_ref, away_ref)
 
 
 def here_kernel(down_ref, hidden_ref, share_ref, out_ref):
     down_rows(hidden_ref, share_ref, down_ref, out_ref)
 
 
-def expert(down, hidden, near, far, halves, order):
-    size = near[0].shape[0]
-    count = size * (len(near) + len(far))
-    half = count // 2
+def expert(down, hidden, shares, last, halves, places, rows):
+    half = rows * len(places) // 2
+    last_count = sum(b.shape[0] for b in last)
     _, inner, width = down.shape
     shape = jax.ShapeDtypeStruct
     away, here_hidden, here_share = pl.pallas_call(
-        functools.partial(away_kernel, len(near), len(far), order),
+        functools.partial(away_kernel, len(hidden), len(last), tuple(places)),
         out_shape=[
             shape((half, width), jnp.bfloat16),
             shape((half, inner), jnp.bfloat16),
             shape((half, lane), jnp.float32),
         ],
-        in_specs=[VMEM] * (2 + len(near) + len(far) + len(halves)),
+        in_specs=[VMEM] * (1 + 2 * len(hidden) + len(last) + len(halves)),
         out_specs=[VMEM] * 3,
         scratch_shapes=[
-            pltpu.VMEM((size * len(far), width + lane), jnp.bfloat16),
-            pltpu.VMEM((size * len(far), inner), jnp.bfloat16),
+            pltpu.VMEM((last_count, width + lane), jnp.bfloat16),
+            pltpu.VMEM((last_count, inner), jnp.bfloat16),
+            pltpu.VMEM((last_count, lane), jnp.float32),
             pltpu.VMEM((half, inner), jnp.bfloat16),
         ],
-        compiler_params=limit(8 if count <= 256 else 24),
+        compiler_params=limit(8 if half <= 128 else 24),
         cost_estimate=pl.CostEstimate(
-            flops=3 * count * width * inner, bytes_accessed=0, transcendentals=count * inner // 2
+            flops=6 * half * width * inner, bytes_accessed=0, transcendentals=half * inner
         ),
         name="away",
-    )(down, hidden, *near, *far, *halves)
+    )(down, *hidden, *shares, *last, *halves)
     here = pl.pallas_call(
         here_kernel,
         out_shape=shape((half, width), jnp.bfloat16),
         in_specs=[VMEM] * 3,
         out_specs=VMEM,
-        compiler_params=limit(4 if count <= 256 else 8),
+        compiler_params=limit(4 if half <= 128 else 8),
         cost_estimate=pl.CostEstimate(
-            flops=count * width * inner, bytes_accessed=0, transcendentals=0
+            flops=2 * half * width * inner, bytes_accessed=0, transcendentals=0
         ),
         name="here",
     )(down, here_hidden, here_share)
@@ -299,36 +319,231 @@
     return lax.ppermute(block, "ep", [(i, i ^ offset) for i in range(count)])
 
 
+def join_kernel(sizes, *refs):
+    sources, out_refs = refs[: sum(sizes)], refs[-len(sizes) :]
+    at = 0
+    for size, out_ref in zip(sizes, out_refs):
+        to = 0
+        for source in sources[at : at + size]:
+            rows = source.shape[0]
+            out_ref[to : to + rows, :] = source[...]
+            to += rows
+        at += size
+
+
+def join(groups, after):
+    blocks = [block for group in groups for block in group]
+    shapes = [(sum(b.shape[0] for b in group), group[0].shape[1]) for group in groups]
+    return pl.pallas_call(
+        functools.partial(join_kernel, tuple(len(group) for group in groups)),
+        out_shape=[jax.ShapeDtypeStruct(shape, jnp.bfloat16) for shape in shapes],
+        in_specs=[VMEM] * len(blocks) + [ANY] * len(after),
+        out_specs=[VMEM] * len(groups),
+        compiler_params=limit(4 if len(blocks) < 8 else 12),
+        name="join",
+    )(*blocks, *after)
+
+
+def hidden_rows(rows_ref, gu_refs, hidden, at, tile):
+    to = 0
+    rows = rows_ref[at : at + tile, : gu_refs[0].shape[0]]
+    for gu_ref in gu_refs:
+        half = gu_ref.shape[1] // 2
+        step = min(256, half)
+        for n in range(0, half, step):
+            gate = jnp.dot(rows, gu_ref[:, n : n + step], preferred_element_type=jnp.float32)
+            up = jnp.dot(
+                rows, gu_ref[:, half + n : half + n + step], preferred_element_type=jnp.float32
+            )
+            hidden[at : at + tile, to : to + step] = (jax.nn.silu(gate) * up).astype(jnp.bfloat16)
+            to += step
+
+
+def fill(rows_ref, block_refs):
+    to = 0
+    for block_ref in block_refs:
+        rows = block_ref.shape[0]
+        rows_ref[to : to + rows, :] = block_ref[...]
+        to += rows
+
+
+def hidden_and_share(rows_ref, gu_refs, hidden, share_ref):
+    rows = rows_ref.shape[0]
+    width = gu_refs[0].shape[0]
+    tile = min(256, rows)
+    for at in range(0, rows, tile):
+        hidden_rows(rows_ref, gu_refs, hidden, at, min(tile, rows - at))
+    shares = rows_ref[:, width:].astype(jnp.float32)
+    lanes = lax.broadcasted_iota(jnp.int32, shares.shape, 1)
+    mine = jnp.where(lanes == lax.axis_index("ep"), shares, 0.0)
+    share_ref[...] = jnp.broadcast_to(jnp.sum(mine, axis=1, keepdims=True), shares.shape)
+
+
+def hidden_kernel(count, after, *refs):
+    block_refs, gu_refs = refs[:count], refs[count : -3 - after]
+    hidden, share_ref, rows_ref = refs[-3:]
+    fill(rows_ref, block_refs)
+    hidden_and_share(rows_ref, gu_refs, hidden, share_ref)
+
+
+def hidden_of(blocks, halves, after):
+    count, wide = sum(b.shape[0] for b in blocks), blocks[0].shape[1]
+    width, inner = halves[0].shape[0], sum(h.shape[1] // 2 for h in halves)
+    return pl.pallas_call(
+        functools.partial(hidden_kernel, len(blocks), len(after)),
+        out_shape=[
+            jax.ShapeDtypeStruct((count, inner), jnp.bfloat16),
+            jax.ShapeDtypeStruct((count, lane), jnp.float32),
+        ],
+        in_specs=[VMEM] * (len(blocks) + len(halves)) + [ANY] * len(after),
+        out_specs=[VMEM, VMEM],
+        scratch_shapes=[pltpu.VMEM((count, wide), jnp.bfloat16)],
+        compiler_params=limit(6 if count <= 256 else 16),
+        cost_estimate=pl.CostEstimate(flops=0, bytes_accessed=0, transcendentals=0),
+        name="hidden",
+    )(*blocks, *halves, *after)
+
+
+def down_rows(hidden, share, down_ref, out_ref):
+    count, width = out_ref.shape
+    tile = min(256, count)
+    step = 512
+    for at in range(0, count, tile):
+        for n in range(0, width, step):
+            piece = jnp.dot(
+                hidden[at : at + tile, :],
+                down_ref[0, :, n : n + step],
+                preferred_element_type=jnp.float32,
+            )
+            piece = piece.astype(jnp.bfloat16).astype(jnp.float32)
+            terms = (share[at : at + tile, :1] * piece).astype(jnp.bfloat16)
+            out_ref[at : at + tile, n : n + step] = terms
+
+
+def away_kernel(sets, count, places, down_ref, *refs):
+    hidden_refs, share_refs, refs = refs[:sets], refs[sets : 2 * sets], refs[2 * sets :]
+    block_refs, gu_refs = refs[:count], refs[count:-7]
+    away_ref, here_hidden, here_share, last_rows, last_hidden, last_share, hidden = refs[-7:]
+    half = away_ref.shape[0]
+    size = 2 * half // len(places)
+    fill(last_rows, block_refs)
+    hidden_and_share(last_rows, gu_refs, last_hidden, last_share)
+    hidden_refs = (*hidden_refs, last_hidden)
+    share_refs = (*share_refs, last_share)
+    shares = []
+    for to, (which, at) in enumerate(places):
+        part = slice(at, at + size)
+        place = slice(to * size % half, to * size % half + size)
+        if to * size < half:
+            hidden[place, :] = hidden_refs[which][part, :]
+            shares.append(share_refs[which][part, :])
+        else:
+            here_hidden[place, :] = hidden_refs[which][part, :]
+            here_share[place, :] = share_refs[which][part, :]
+    down_rows(hidden, jnp.concatenate(shares, axis=0), down_ref, away_ref)
+
+
+def here_kernel(down_ref, hidden_ref, share_ref, out_ref):
+    down_rows(hidden_ref, share_ref, down_ref, out_ref)
+
+
+def expert(down, hidden, shares, last, halves, places, rows):
+    half = rows * len(places) // 2
+    last_count = sum(b.shape[0] for b in last)
+    _, inner, width = down.shape
+    shape = jax.ShapeDtypeStruct
+    away, here_hidden, here_share = pl.pallas_call(
+        functools.partial(away_kernel, len(hidden), len(last), tuple(places)),
+        out_shape=[
+            shape((half, width), jnp.bfloat16),
+            shape((half, inner), jnp.bfloat16),
+            shape((half, lane), jnp.float32),
+        ],
+        in_specs=[VMEM] * (1 + 2 * len(hidden) + len(last) + len(halves)),
+        out_specs=[VMEM] * 3,
+        scratch_shapes=[
+            pltpu.VMEM((last_count, width + lane), jnp.bfloat16),
+            pltpu.VMEM((last_count, inner), jnp.bfloat16),
+            pltpu.VMEM((last_count, lane), jnp.float32),
+            pltpu.VMEM((half, inner), jnp.bfloat16),
+        ],
+        compiler_params=limit(8 if half <= 128 else 24),
+        cost_estimate=pl.CostEstimate(
+            flops=6 * half * width * inner, bytes_accessed=0, transcendentals=half * inner
+        ),
+        name="away",
+    )(down, *hidden, *shares, *last, *halves)
+    here = pl.pallas_call(
+        here_kernel,
+        out_shape=shape((half, width), jnp.bfloat16),
+        in_specs=[VMEM] * 3,
+        out_specs=VMEM,
+        compiler_params=limit(4 if half <= 128 else 8),
+        cost_estimate=pl.CostEstimate(
+            flops=2 * half * width * inner, bytes_accessed=0, transcendentals=0
+        ),
+        name="here",
+    )(down, here_hidden, here_share)
+    return away, here
+
+
+def add_kernel(pieces, got_ref, here_ref, *refs):
+    later = (len(refs) - len(pieces)) // 2
+    for piece, out_ref in zip(pieces, refs[later:]):
+        to = 0
+        for rows, columns in piece:
+            here = here_ref[slice(*rows), slice(*columns)].astype(jnp.float32)
+            got = got_ref[slice(*rows), slice(*columns)].astype(jnp.float32)
+            end = to + columns[1] - columns[0]
+            out_ref[:, to:end] = (got + here).astype(jnp.bfloat16)
+            to = end
+    for source, out_ref in zip(refs, refs[len(refs) - later :]):
+        out_ref[...] = source[...]
+
+
+def add(got, here, pieces, later=()):
+    shapes = [(piece[0][0][1] - piece[0][0][0], sum(c[1] - c[0] for _, c in piece)) for piece in pieces]
+    shapes += [array.shape for array in later]
+    return pl.pallas_call(
+        functools.partial(add_kernel, tuple(tuple(piece) for piece in pieces)),
+        out_shape=[jax.ShapeDtypeStruct(shape, jnp.bfloat16) for shape in shapes],
+        in_specs=[VMEM] * (2 + len(later)),
+        out_specs=[VMEM] * len(shapes),
+        compiler_params=limit(2 if got.shape[0] <= 16 else 6 if got.shape[0] <= 128 else 16),
+        name="add",
+    )(got, here, *later)
+
+
+def swap(block, offset):
+    count = lax.axis_size("ep")
+    return lax.ppermute(block, "ep", [(i, i ^ offset) for i in range(count)])
+
+
 def gather_blocks(block, far, gate_up):
     groups = gate_up.shape[3] // lane // 2
-    near = {0: block}
     lead, *late = far[:0:-1]
     close = far[0]
-    near[lead], near[2] = swap(block, lead), swap(block, 2)
+    along, beside = swap(block, lead), swap(block, 2)
     first, token = unpack(gate_up, 0, groups, [], 1 << 24)
-    (again,) = pass_on([block], token)
-    for offset in (*late, close, close ^ 2):
-        near[offset] = swap(again, offset)
-    (near[lead],) = pass_on([near[lead]], near[2])
-    near[lead ^ 2] = swap(near[lead], 2)
+    (again,) = join([[block]], [token])
+    others = {offset: swap(again, offset) for offset in (*late, close, close ^ 2)}
+    along, early = join([[along], [block, beside, along]], [beside])
+    across = swap(along, 2)
     second, token = unpack(gate_up, groups, gate_up.shape[3] // lane - groups, [again], 1 << 24)
-    first_late = (lead, lead ^ 2, *late)
-    near[lead], near[lead ^ 2], *held = pass_on([near[offset] for offset in first_late], token)
-    for offset, array in zip(late, held):
-        near[offset] = array
-        near[offset ^ 2] = swap(array, 2)
-    ready = (0, 2, close, close ^ 2)
-    near[lead ^ 1] = swap(near[lead], 1)
-    for offset, array in zip(ready, pass_on([near[offset] for offset in ready], near[lead ^ 1])):
-        near[offset] = array
-    for offset in (*ready, lead ^ 2, *late):
-        near[offset ^ 1] = swap(near[offset], 1)
-    for offset in late:
-        near[offset ^ 3] = swap(near[offset ^ 2], 1)
-    hidden = near_hidden(
-        [near[offset] for offset in range(8)], [first, second], [near[late[-1] ^ 2]]
+    halves = [first, second]
+    middle, *held = join(
+        [[across, *(others[o] for o in late)], *([others[o]] for o in late)], [token]
     )
-    return near, [first, second], hidden
+    last = [swap(array, 2) for array in held]
+    near = [early, middle, others[close], others[close ^ 2]]
+    hidden, share = hidden_of(near, halves, [])
+    *last, both = join([*([array] for array in last), near[2:]], [share])
+    pairs = [swap(array, 1) for array in (*near[:2], both)]
+    last = [*pairs, *last, *(swap(array, 1) for array in last)]
+    keys = [0, 2, lead, lead ^ 2, *late, close, close ^ 2]
+    ends = [o ^ 2 for o in late]
+    keys = [keys, [*(o ^ 1 for o in keys), *ends, *(o ^ 1 for o in ends)]]
+    return [hidden], [share], last, halves, keys
 
 
 def shards(resid, norm_gain, expert_ids, route_weights, gate_up, down):
@@ -338,15 +553,14 @@
     resid_all = lax.all_gather(resid, "tp", axis=0, tiled=True) if tp > 1 else resid
     normed = norm(resid_all, norm_gain, expert_ids, route_weights)
     rows = normed.shape[0]
-    blocks, parts, hidden = gather_blocks(normed, far, gate_up)
-    order = sorted(blocks, key=lambda o: (1 - (o & 1), 1 - (o >> 1 & 1), -o))
-    places = [(o < 8, o % 8 if o < 8 else o - 8) for o in order]
-    near, late = [blocks[o] for o in range(8)], [blocks[o] for o in range(8, owners)]
-    away, here = expert(down, hidden, near, late, parts, places)
+    hidden, shares, last, halves, keys = gather_blocks(normed, far, gate_up)
+    order = sorted(range(owners), key=lambda o: (1 - (o & 1), 1 - (o >> 1 & 1), -o))
+    found = {o: (which, at * rows) for which, part in enumerate(keys) for at, o in enumerate(part)}
+    away, here = expert(down, hidden, shares, last, halves, [found[o] for o in order], rows)
     lead, *late = far[:0:-1]
     close = far[0]
     width = away.shape[1]
-    cut = width // lane * 4 // 8 * lane
+    cut = width // lane * 3 // 8 * lane
     keys = [o for o in order if o & 3 == 0]
     half = len(keys) * rows
     away_rows = {o: (at * rows, at * rows + rows) for at, o in enumerate(keys)}

time: 51.8 us -> 50.9 us (0.983)
  waiting for transfers between devices: 9.66 us -> 8.33 us
  Pallas kernels: 15.1 us -> 15.7 us
    ppermute x24 -> x20, waiting for transfers between devices: 9.66 us -> 8.33 us  [swap(): return lax.ppermute(block, 'ep', [(i, i ^ offset) for i in range(count)])]
    ppermute x24 -> x20, starting transfers between devices: 25.8 us -> 25.7 us  [swap(): return lax.ppermute(block, 'ep', [(i, i ^ offset) for i in range(count)])]
  transfers between devices with their start and end apart: 24 -> 20, of which waited for: 7 -> 5; matrix products, arithmetic and copies ran while one was open for 0% -> 0% of each run, Pallas kernels for 21% -> 22%
where the time goes in v5:
time: 50.9 us; the launch traced here: 50.7 us
  starting transfers between devices  25.7 us (50%)
  Pallas kernels  15.7 us (31%)
  waiting for transfers between devices  8.33 us (16%)
  other arithmetic  0.78 us (2%)
    ppermute x20, starting transfers between devices, swap(): return lax.ppermute(block, 'ep', [(i, i ^ offset) for i in range(count)])  25.7 us
    ppermute x20, waiting for transfers between devices, swap(): return lax.ppermute(block, 'ep', [(i, i ^ offset) for i in range(count)])  8.33 us
    pallas_call x2, Pallas kernels, unpack(): pl.pallas_call(functools.partial(unpack_kernel, first), out_shape=[jax.Sh...  7.32 us
    pallas_call x1, Pallas kernels, expert(): pl.pallas_call(functools.partial(away_kernel, len(hidden), len(last), tup...  3.42 us
    pallas_call x1, Pallas kernels, hidden_of(): pl.pallas_call(functools.partial(hidden_kernel, len(blocks), len(after)),...  2.36 us
    pallas_call x1, Pallas kernels, expert(): pl.pallas_call(here_kernel, out_shape=shape((half, width), jnp.bfloat16),...  1.14 us
    pallas_call x1, Pallas kernels, norm(): pl.pallas_call(norm_kernel, out_shape=jax.ShapeDtypeStruct((rows, width +...  1.1 us
  transfers between devices with their start and end apart: 20, of which 5 were waited for; matrix products, arithmetic and copies ran while one was open for 0% of the time, Pallas kernels for 22%

profile of v5, /device:TPU:0, one launch (start us, length us, event | category | flops | bytes accessed | tf_op | source)
XLA Modules:
  0.0 50.7 jit_solution(10549048826120089179)
XLA Ops:
  0.0 1.1 %norm.1.refs_1_.refs_0_ = bf16[16,3712]{1,0:T(8,128)(2,1)S(1)} custom-call(bf16[16,3584]{1,0:T(8,128)(2,1)} %refs_0_.1, f32[3584]{0:T(1024)} %refs_1_.1, s32[8,16]{1,0:T(8,128)} %bitcast.4, bf16[8,16]{1,0:T(8,128)(2,1)} %bitcast.5), custom_call_target="tpu_custom_call" | custom-call | tf_op jit(solution)/shard_map/norm/pallas_call | solution.py:57
  1.1 3.0 %collective-permute-start.1 = (bf16[16,3712]{1,0:T(8,128)(2,1)S(1)}, bf16[16,3712]{1,0:T(8,128)(2,1)S(1)}, u32[]{:S(2)}, u32[]{:S(2)}) collective-permute-start(bf16[16,3712]{1,0:T(8,128)(2,1)S(1)} %norm.1.refs_1_.refs_0_), channel_id=1, source_target_pairs={{0,2},{1,3},{2,0},{3,1},{4,6},{5,7},{6,4},{7,5},{8,10},{9,11},{10,... | collective-permute-start | bytes 356360 | tf_op jit(solution)/shard_map/ppermute | solution.py:519
  4.1 3.6 %collective-permute-start = (bf16[16,3712]{1,0:T(8,128)(2,1)S(1)}, bf16[16,3712]{1,0:T(8,128)(2,1)S(1)}, u32[]{:S(2)}, u32[]{:S(2)}) collective-permute-start(bf16[16,3712]{1,0:T(8,128)(2,1)S(1)} %norm.1.refs_1_.refs_0_), channel_id=1, source_target_pairs={{0,12},{1,13},{2,14},{3,15},{4,8},{5,9},{6,10},{7,11},{8,4},{9,5},... | collective-permute-start | bytes 356360 | tf_op jit(solution)/shard_map/ppermute | solution.py:519
  7.7 3.6 %unpack.2 = (bf16[3584,1024]{1,0:T(8,128)(2,1)S(1)}, f32[8,128]{1,0:T(8,128)S(1)}) custom-call(bf16[1,3584,2,1024]{3,2,1,0:T(2,128)(2,1)} %packed_ref.3), custom_call_target="tpu_custom_call" | custom-call | bytes 16777216 | tf_op jit(solution)/shard_map/unpack/pallas_call | solution.py:104
  11.4 0.1 collective-permute-start.3
  11.5 0.6 %collective-permute-start.2 = (bf16[16,3712]{1,0:T(8,128)(2,1)S(1)}, bf16[16,3712]{1,0:T(8,128)(2,1)S(1)}, u32[]{:S(2)}, u32[]{:S(2)}) collective-permute-start(bf16[16,3712]{1,0:T(8,128)(2,1)S(1)} %get-tuple-element.32), channel_id=1, source_target_pairs={{0,2},{1,3},{2,0},{3,1},{4,6},{5,7},{6,4},{7,5},{8,10},{9,11},{10,... | collective-permute-start | bytes 356360 | tf_op jit(solution)/shard_map/ppermute | solution.py:519
  12.1 2.4 %collective-permute-start.5 = (bf16[16,3712]{1,0:T(8,128)(2,1)S(1)}, bf16[16,3712]{1,0:T(8,128)(2,1)S(1)}, u32[]{:S(2)}, u32[]{:S(2)}) collective-permute-start(bf16[16,3712]{1,0:T(8,128)(2,1)S(1)} %join.5.refs_0_), channel_id=1, source_target_pairs={{0,6},{1,7},{2,4},{3,5},{4,2},{5,3},{6,0},{7,1},{8,14},{9,15},{10,... | collective-permute-start | bytes 356360 | tf_op jit(solution)/shard_map/ppermute | solution.py:519
  14.5 0.5 %collective-permute-start.4 = (bf16[16,3712]{1,0:T(8,128)(2,1)S(1)}, bf16[16,3712]{1,0:T(8,128)(2,1)S(1)}, u32[]{:S(2)}, u32[]{:S(2)}) collective-permute-start(bf16[16,3712]{1,0:T(8,128)(2,1)S(1)} %join.5.refs_0_), channel_id=1, source_target_pairs={{0,4},{1,5},{2,6},{3,7},{4,0},{5,1},{6,2},{7,3},{8,12},{9,13},{10,... | collective-permute-start | bytes 356360 | tf_op jit(solution)/shard_map/ppermute | solution.py:519
  15.1 3.7 %unpack.3 = (bf16[3584,1024]{1,0:T(8,128)(2,1)S(1)}, f32[8,128]{1,0:T(8,128)S(1)}) custom-call(bf16[1,3584,2,1024]{3,2,1,0:T(2,128)(2,1)} %packed_ref.3, bf16[16,3712]{1,0:T(8,128)(2,1)S(1)} %join.5.refs_0_), custom_call_target="tpu_custom_call" | custom-call | bytes 16777216 | tf_op jit(solution)/shard_map/unpack/pallas_call | solution.py:104
  18.9 0.6 %collective-permute-start.8 = (bf16[16,3712]{1,0:T(8,128)(2,1)S(1)}, bf16[16,3712]{1,0:T(8,128)(2,1)S(1)}, u32[]{:S(2)}, u32[]{:S(2)}) collective-permute-start(bf16[16,3712]{1,0:T(8,128)(2,1)S(1)} %get-tuple-element.40), channel_id=1, source_target_pairs={{0,2},{1,3},{2,0},{3,1},{4,6},{5,7},{6,4},{7,5},{8,10},{9,11},{10,... | collective-permute-start | bytes 356360 | tf_op jit(solution)/shard_map/ppermute | solution.py:519
  19.4 0.5 collective-permute-start.7
  19.9 0.8 %collective-permute-done.5.refs_3_.refs_2_ = bf16[16,3712]{1,0:T(8,128)(2,1)S(1)} collective-permute-done((bf16[16,3712]{1,0:T(8,128)(2,1)S(1)}, bf16[16,3712]{1,0:T(8,128)(2,1)S(1)}, u32[]{:S(2)}, u32[]{:S(2)}) %collective-permute-start.5) | collective-permute-done | bytes 118816 | tf_op jit(solution)/shard_map/ppermute | solution.py:519
  20.8 1.4 %collective-permute-done.4.refs_2_.refs_1_ = bf16[16,3712]{1,0:T(8,128)(2,1)S(1)} collective-permute-done((bf16[16,3712]{1,0:T(8,128)(2,1)S(1)}, bf16[16,3712]{1,0:T(8,128)(2,1)S(1)}, u32[]{:S(2)}, u32[]{:S(2)}) %collective-permute-start.4) | collective-permute-done | bytes 118816 | tf_op jit(solution)/shard_map/ppermute | solution.py:519
  22.1 2.4 %hidden.1 = (bf16[112,1024]{1,0:T(8,128)(2,1)S(1)}, f32[112,128]{1,0:T(8,128)S(1)}) custom-call(bf16[48,3712]{1,0:T(8,128)(2,1)S(1)} %get-tuple-element.31.refs_0_, bf16[32,3712]{1,0:T(8,128)(2,1)S(1)} %get-tuple-element.35.refs_1_, bf16[16,3712]{1,0:T(8,128)(2,1)S(1)} %collective-permute-done.4.refs_2_.refs_1_, ...), custom_call_target="tpu_custom_call" | custom-call | tf_op jit(solution)/shard_map/hidden/pallas_call | solution.py:392
  24.6 0.1 collective-permute-start.9
  24.6 0.5 collective-permute-start.10
  25.1 1.2 %collective-permute-done.10.refs_6_ = bf16[16,3712]{1,0:T(8,128)(2,1)S(1)} collective-permute-done((bf16[16,3712]{1,0:T(8,128)(2,1)S(1)}, bf16[16,3712]{1,0:T(8,128)(2,1)S(1)}, u32[]{:S(2)}, u32[]{:S(2)}) %collective-permute-start.10) | collective-permute-done | bytes 118816 | tf_op jit(solution)/shard_map/ppermute | solution.py:519
  26.3 3.4 %away.1 = (bf16[128,3584]{1,0:T(8,128)(2,1)S(1)}, bf16[128,1024]{1,0:T(8,128)(2,1)S(1)}, f32[128,128]{1,0:T(8,128)S(1)}) custom-call(bf16[1,1024,3584]{2,1,0:T(8,128)(2,1)S(1)} %bitcast.3, bf16[112,1024]{1,0:T(8,128)(2,1)S(1)} %get-tuple-element.38.refs_0_, f32[112,128]{1,0:T(8,128)S(1)} %get-tuple-element.39.refs_3_.refs_1_, ...), custom_call_target="tpu_custom_call" | custom-call | flops 2818572288 | tf_op jit(solution)/shard_map/away/pallas_call | solution.py:455
  29.8 0.2 collective-permute-start.11
  30.0 1.1 %here.1.here_ref = bf16[128,3584]{1,0:T(8,128)(2,1)S(1)} custom-call(bf16[1,1024,3584]{2,1,0:T(8,128)(2,1)S(1)} %bitcast.3, bf16[128,1024]{1,0:T(8,128)(2,1)S(1)} %get-tuple-element.44.hidden_ref, f32[128,128]{1,0:T(8,128)S(1)} %get-tuple-element.45.share_ref), custom_call_target="tpu_custom_call" | custom-call | flops 939524096 | tf_op jit(solution)/shard_map/here/pallas_call | solution.py:476
  31.2 1.1 %collective-permute-done.11.got_ref = bf16[128,3584]{1,0:T(8,128)(2,1)S(1)} collective-permute-done((bf16[128,3584]{1,0:T(8,128)(2,1)S(1)}, bf16[128,3584]{1,0:T(8,128)(2,1)S(1)}, u32[]{:S(2)}, u32[]{:S(2)}) %collective-permute-start.11) | collective-permute-done | bytes 917536 | tf_op jit(solution)/shard_map/ppermute | solution.py:519
  32.3 0.2 add.43
  32.5 0.5 %collective-permute-start.14 = (bf16[16,4864]{1,0:T(8,128)(2,1)S(1)}, bf16[16,4864]{1,0:T(8,128)(2,1)S(1)}, u32[]{:S(2)}, u32[]{:S(2)}) collective-permute-start(bf16[16,4864]{1,0:T(8,128)(2,1)S(1)} %get-tuple-element.49), channel_id=1, source_target_pairs={{0,2},{1,3},{2,0},{3,1},{4,6},{5,7},{6,4},{7,5},{8,10},{9,11},{10,... | collective-permute-start | bytes 466952 | tf_op jit(solution)/shard_map/ppermute | solution.py:519
  33.0 2.4 %collective-permute-start.18 = (bf16[16,2304]{1,0:T(8,128)(2,1)S(1)}, bf16[16,2304]{1,0:T(8,128)(2,1)S(1)}, u32[]{:S(2)}, u32[]{:S(2)}) collective-permute-start(bf16[16,2304]{1,0:T(8,128)(2,1)S(1)} %get-tuple-element.55), channel_id=1, source_target_pairs={{0,8},{1,9},{2,10},{3,11},{4,12},{5,13},{6,14},{7,15},{8,0},{9,1},... | collective-permute-start | bytes 221192 | tf_op jit(solution)/shard_map/ppermute | solution.py:519
  35.4 1.5 %collective-permute-start.19 = (bf16[16,2304]{1,0:T(8,128)(2,1)S(1)}, bf16[16,2304]{1,0:T(8,128)(2,1)S(1)}, u32[]{:S(2)}, u32[]{:S(2)}) collective-permute-start(bf16[16,2304]{1,0:T(8,128)(2,1)S(1)} %get-tuple-element.56), channel_id=1, source_target_pairs={{0,10},{1,11},{2,8},{3,9},{4,14},{5,15},{6,12},{7,13},{8,2},{9,3},... | collective-permute-start | bytes 221192 | tf_op jit(solution)/shard_map/ppermute | solution.py:519
  37.0 0.7 %collective-permute-start.12 = (bf16[16,3584]{1,0:T(8,128)(2,1)S(1)}, bf16[16,3584]{1,0:T(8,128)(2,1)S(1)}, u32[]{:S(2)}, u32[]{:S(2)}) collective-permute-start(bf16[16,3584]{1,0:T(8,128)(2,1)S(1)} %get-tuple-element.47), channel_id=1, source_target_pairs={{0,4},{1,5},{2,6},{3,7},{4,0},{5,1},{6,2},{7,3},{8,12},{9,13},{10,... | collective-permute-start | bytes 344072 | tf_op jit(solution)/shard_map/ppermute | solution.py:519
  37.7 1.2 %collective-permute-start.13 = (bf16[16,3584]{1,0:T(8,128)(2,1)S(1)}, bf16[16,3584]{1,0:T(8,128)(2,1)S(1)}, u32[]{:S(2)}, u32[]{:S(2)}) collective-permute-start(bf16[16,3584]{1,0:T(8,128)(2,1)S(1)} %get-tuple-element.48), channel_id=1, source_target_pairs={{0,6},{1,7},{2,4},{3,5},{4,2},{5,3},{6,0},{7,1},{8,14},{9,15},{10,... | collective-permute-start | bytes 344072 | tf_op jit(solution)/shard_map/ppermute | solution.py:519
  38.9 2.8 %collective-permute-start.17 = (bf16[16,1280]{1,0:T(8,128)(2,1)S(1)}, bf16[16,1280]{1,0:T(8,128)(2,1)S(1)}, u32[]{:S(2)}, u32[]{:S(2)}) collective-permute-start(bf16[16,1280]{1,0:T(8,128)(2,1)S(1)} %get-tuple-element.54), channel_id=1, source_target_pairs={{0,8},{1,9},{2,10},{3,11},{4,12},{5,13},{6,14},{7,15},{8,0},{9,1},... | collective-permute-start | bytes 122888 | tf_op jit(solution)/shard_map/ppermute | solution.py:519
  41.7 2.8 %collective-permute-start.15 = (bf16[16,3584]{1,0:T(8,128)(2,1)S(1)}, bf16[16,3584]{1,0:T(8,128)(2,1)S(1)}, u32[]{:S(2)}, u32[]{:S(2)}) collective-permute-start(bf16[16,3584]{1,0:T(8,128)(2,1)S(1)} %get-tuple-element.52), channel_id=1, source_target_pairs={{0,12},{1,13},{2,14},{3,15},{4,8},{5,9},{6,10},{7,11},{8,4},{9,5},... | collective-permute-start | bytes 344072 | tf_op jit(solution)/shard_map/ppermute | solution.py:519
  44.5 1.6 %collective-permute-start.16 = (bf16[16,3584]{1,0:T(8,128)(2,1)S(1)}, bf16[16,3584]{1,0:T(8,128)(2,1)S(1)}, u32[]{:S(2)}, u32[]{:S(2)}) collective-permute-start(bf16[16,3584]{1,0:T(8,128)(2,1)S(1)} %get-tuple-element.53), channel_id=1, source_target_pairs={{0,2},{1,3},{2,0},{3,1},{4,6},{5,7},{6,4},{7,5},{8,10},{9,11},{10,... | collective-permute-start | bytes 344072 | tf_op jit(solution)/shard_map/ppermute | solution.py:519
  46.2 3.8 %collective-permute-done.13 = bf16[16,3584]{1,0:T(8,128)(2,1)S(1)} collective-permute-done((bf16[16,3584]{1,0:T(8,128)(2,1)S(1)}, bf16[16,3584]{1,0:T(8,128)(2,1)S(1)}, u32[]{:S(2)}, u32[]{:S(2)}) %collective-permute-start.13) | collective-permute-done | bytes 114720 | tf_op jit(solution)/shard_map/ppermute | solution.py:519
  50.0 0.8 %fusion.1 = bf16[16,3584]{1,0:T(8,128)(2,1)} fusion(f32[16,2304]{1,0:T(8,128)S(1)} %convert_add_fusion, f32[16,1280]{1,0:T(8,128)S(1)} %convert_element_type.36, bf16[16,3584]{1,0:T(8,128)(2,1)S(1)} %collective-permute-done.16, bf16[16,3584]{1,0:T(8,128)(2,1)S(1)} %collective-permute-done.15, bf16[16,3584]{1,0:T(8,128)(2,1)S(1)} %collective-permute-done.13, ...), kind=kLoop, calls=%fused_computation.2 | loop fusion | flops 802816 | bytes 1032192 | tf_op jit(solution)/shard_map/convert_element_type | solution.py:592
  (30 shorter events, 0.2 us)
Async XLA Ops:
  1.1 10.3 %collective-permute-start.1 = (bf16[16,3712]{1,0:T(8,128)(2,1)S(1)}, bf16[16,3712]{1,0:T(8,128)(2,1)S(1)}, u32[]{:S(2)}, u32[]{:S(2)}) collective-permute-start(bf16[16,3712]{1,0:T(8,128)(2,1)S(1)} %norm.1.refs_1_.refs_0_), channel_id=1, source_target_pairs={{0,2},{1,3},{2,0},{3,1},{4,6},{5,7},{6,4},{7,5},{8,10},{9,11},{10,... | collective-permute-start | bytes 356360 | tf_op jit(solution)/shard_map/ppermute | solution.py:519
  4.1 7.3 %collective-permute-start = (bf16[16,3712]{1,0:T(8,128)(2,1)S(1)}, bf16[16,3712]{1,0:T(8,128)(2,1)S(1)}, u32[]{:S(2)}, u32[]{:S(2)}) collective-permute-start(bf16[16,3712]{1,0:T(8,128)(2,1)S(1)} %norm.1.refs_1_.refs_0_), channel_id=1, source_target_pairs={{0,12},{1,13},{2,14},{3,15},{4,8},{5,9},{6,10},{7,11},{8,4},{9,5},... | collective-permute-start | bytes 356360 | tf_op jit(solution)/shard_map/ppermute | solution.py:519
  11.4 7.4 %collective-permute-start.3 = (bf16[16,3712]{1,0:T(8,128)(2,1)S(1)}, bf16[16,3712]{1,0:T(8,128)(2,1)S(1)}, u32[]{:S(2)}, u32[]{:S(2)}) collective-permute-start(bf16[16,3712]{1,0:T(8,128)(2,1)S(1)} %join.5.refs_0_), channel_id=1, source_target_pairs={{0,8},{1,9},{2,10},{3,11},{4,12},{5,13},{6,14},{7,15},{8,0},{9,1},... | collective-permute-start | bytes 356360 | tf_op jit(solution)/shard_map/ppermute | solution.py:519
  11.5 7.3 %collective-permute-start.2 = (bf16[16,3712]{1,0:T(8,128)(2,1)S(1)}, bf16[16,3712]{1,0:T(8,128)(2,1)S(1)}, u32[]{:S(2)}, u32[]{:S(2)}) collective-permute-start(bf16[16,3712]{1,0:T(8,128)(2,1)S(1)} %get-tuple-element.32), channel_id=1, source_target_pairs={{0,2},{1,3},{2,0},{3,1},{4,6},{5,7},{6,4},{7,5},{8,10},{9,11},{10,... | collective-permute-start | bytes 356360 | tf_op jit(solution)/shard_map/ppermute | solution.py:519
  12.1 8.7 %collective-permute-start.5 = (bf16[16,3712]{1,0:T(8,128)(2,1)S(1)}, bf16[16,3712]{1,0:T(8,128)(2,1)S(1)}, u32[]{:S(2)}, u32[]{:S(2)}) collective-permute-start(bf16[16,3712]{1,0:T(8,128)(2,1)S(1)} %join.5.refs_0_), channel_id=1, source_target_pairs={{0,6},{1,7},{2,4},{3,5},{4,2},{5,3},{6,0},{7,1},{8,14},{9,15},{10,... | collective-permute-start | bytes 356360 | tf_op jit(solution)/shard_map/ppermute | solution.py:519
  14.5 7.6 %collective-permute-start.4 = (bf16[16,3712]{1,0:T(8,128)(2,1)S(1)}, bf16[16,3712]{1,0:T(8,128)(2,1)S(1)}, u32[]{:S(2)}, u32[]{:S(2)}) collective-permute-start(bf16[16,3712]{1,0:T(8,128)(2,1)S(1)} %join.5.refs_0_), channel_id=1, source_target_pairs={{0,4},{1,5},{2,6},{3,7},{4,0},{5,1},{6,2},{7,3},{8,12},{9,13},{10,... | collective-permute-start | bytes 356360 | tf_op jit(solution)/shard_map/ppermute | solution.py:519
  15.1 11.2 %slice-start = ((s8[7340032]{0:T(1024)(128)(4,1)}), s8[4194304]{0:T(1024)(128)(4,1)S(1)}, s32[]{:S(2)}) async-start(s8[7340032]{0:T(1024)(128)(4,1)} %bitcast.2), calls=%async_computation | async-start | bytes 8388608
  18.9 5.7 %collective-permute-start.8 = (bf16[16,3712]{1,0:T(8,128)(2,1)S(1)}, bf16[16,3712]{1,0:T(8,128)(2,1)S(1)}, u32[]{:S(2)}, u32[]{:S(2)}) collective-permute-start(bf16[16,3712]{1,0:T(8,128)(2,1)S(1)} %get-tuple-element.40), channel_id=1, source_target_pairs={{0,2},{1,3},{2,0},{3,1},{4,6},{5,7},{6,4},{7,5},{8,10},{9,11},{10,... | collective-permute-start | bytes 356360 | tf_op jit(solution)/shard_map/ppermute | solution.py:519
  19.4 5.7 %collective-permute-start.6 = (bf16[48,3712]{1,0:T(8,128)(2,1)S(1)}, bf16[48,3712]{1,0:T(8,128)(2,1)S(1)}, u32[]{:S(2)}, u32[]{:S(2)}) collective-permute-start(bf16[48,3712]{1,0:T(8,128)(2,1)S(1)} %get-tuple-element.31.refs_0_), channel_id=1, source_target_pairs={{0,1},{1,0},{2,3},{3,2},{4,5},{5,4},{6,7},{7,6},{8,9},{9,8},{10,11... | collective-permute-start | bytes 1069064 | tf_op jit(solution)/shard_map/ppermute | solution.py:519
  19.4 6.9 %collective-permute-start.7 = (bf16[32,3712]{1,0:T(8,128)(2,1)S(1)}, bf16[32,3712]{1,0:T(8,128)(2,1)S(1)}, u32[]{:S(2)}, u32[]{:S(2)}) collective-permute-start(bf16[32,3712]{1,0:T(8,128)(2,1)S(1)} %get-tuple-element.35.refs_1_), channel_id=1, source_target_pairs={{0,1},{1,0},{2,3},{3,2},{4,5},{5,4},{6,7},{7,6},{8,9},{9,8},{10,11... | collective-permute-start | bytes 712712 | tf_op jit(solution)/shard_map/ppermute | solution.py:519
  22.1 4.2 %slice-start.1 = ((s8[7340032]{0:T(1024)(128)(4,1)}), s8[3145728]{0:T(1024)(128)(4,1)S(1)}, s32[]{:S(2)}) async-start(s8[7340032]{0:T(1024)(128)(4,1)} %bitcast.2), calls=%async_computation.1 | async-start | bytes 6291456
  24.6 1.7 %collective-permute-start.9 = (bf16[32,3712]{1,0:T(8,128)(2,1)S(1)}, bf16[32,3712]{1,0:T(8,128)(2,1)S(1)}, u32[]{:S(2)}, u32[]{:S(2)}) collective-permute-start(bf16[32,3712]{1,0:T(8,128)(2,1)S(1)} %get-tuple-element.41), channel_id=1, source_target_pairs={{0,1},{1,0},{2,3},{3,2},{4,5},{5,4},{6,7},{7,6},{8,9},{9,8},{10,11... | collective-permute-start | bytes 712712 | tf_op jit(solution)/shard_map/ppermute | solution.py:519
  24.6 1.7 %collective-permute-start.10 = (bf16[16,3712]{1,0:T(8,128)(2,1)S(1)}, bf16[16,3712]{1,0:T(8,128)(2,1)S(1)}, u32[]{:S(2)}, u32[]{:S(2)}) collective-permute-start(bf16[16,3712]{1,0:T(8,128)(2,1)S(1)} %get-tuple-element.42.refs_5_), channel_id=1, source_target_pairs={{0,1},{1,0},{2,3},{3,2},{4,5},{5,4},{6,7},{7,6},{8,9},{9,8},{10,11... | collective-permute-start | bytes 356360 | tf_op jit(solution)/shard_map/ppermute | solution.py:519
  29.7 20.2 %copy-start = (bf16[16,3584]{1,0:T(8,128)(2,1)S(1)}, bf16[16,3584]{1,0:T(8,128)(2,1)}, u32[]{:S(2)}) copy-start(bf16[16,3584]{1,0:T(8,128)(2,1)} %refs_0_.1) | copy-start | bytes 344068
  29.8 2.5 %collective-permute-start.11 = (bf16[128,3584]{1,0:T(8,128)(2,1)S(1)}, bf16[128,3584]{1,0:T(8,128)(2,1)S(1)}, u32[]{:S(2)}, u32[]{:S(2)}) collective-permute-start(bf16[128,3584]{1,0:T(8,128)(2,1)S(1)} %get-tuple-element.43), channel_id=1, source_target_pairs={{0,1},{1,0},{2,3},{3,2},{4,5},{5,4},{6,7},{7,6},{8,9},{9,8},{10,11... | collective-permute-start | bytes 2752520 | tf_op jit(solution)/shard_map/ppermute | solution.py:519
  32.5 6.4 %collective-permute-start.14 = (bf16[16,4864]{1,0:T(8,128)(2,1)S(1)}, bf16[16,4864]{1,0:T(8,128)(2,1)S(1)}, u32[]{:S(2)}, u32[]{:S(2)}) collective-permute-start(bf16[16,4864]{1,0:T(8,128)(2,1)S(1)} %get-tuple-element.49), channel_id=1, source_target_pairs={{0,2},{1,3},{2,0},{3,1},{4,6},{5,7},{6,4},{7,5},{8,10},{9,11},{10,... | collective-permute-start | bytes 466952 | tf_op jit(solution)/shard_map/ppermute | solution.py:519
  33.0 8.7 %collective-permute-start.18 = (bf16[16,2304]{1,0:T(8,128)(2,1)S(1)}, bf16[16,2304]{1,0:T(8,128)(2,1)S(1)}, u32[]{:S(2)}, u32[]{:S(2)}) collective-permute-start(bf16[16,2304]{1,0:T(8,128)(2,1)S(1)} %get-tuple-element.55), channel_id=1, source_target_pairs={{0,8},{1,9},{2,10},{3,11},{4,12},{5,13},{6,14},{7,15},{8,0},{9,1},... | collective-permute-start | bytes 221192 | tf_op jit(solution)/shard_map/ppermute | solution.py:519
  35.4 9.1 %collective-permute-start.19 = (bf16[16,2304]{1,0:T(8,128)(2,1)S(1)}, bf16[16,2304]{1,0:T(8,128)(2,1)S(1)}, u32[]{:S(2)}, u32[]{:S(2)}) collective-permute-start(bf16[16,2304]{1,0:T(8,128)(2,1)S(1)} %get-tuple-element.56), channel_id=1, source_target_pairs={{0,10},{1,11},{2,8},{3,9},{4,14},{5,15},{6,12},{7,13},{8,2},{9,3},... | collective-permute-start | bytes 221192 | tf_op jit(solution)/shard_map/ppermute | solution.py:519
  37.0 9.2 %collective-permute-start.12 = (bf16[16,3584]{1,0:T(8,128)(2,1)S(1)}, bf16[16,3584]{1,0:T(8,128)(2,1)S(1)}, u32[]{:S(2)}, u32[]{:S(2)}) collective-permute-start(bf16[16,3584]{1,0:T(8,128)(2,1)S(1)} %get-tuple-element.47), channel_id=1, source_target_pairs={{0,4},{1,5},{2,6},{3,7},{4,0},{5,1},{6,2},{7,3},{8,12},{9,13},{10,... | collective-permute-start | bytes 344072 | tf_op jit(solution)/shard_map/ppermute | solution.py:519
  37.7 12.3 %collective-permute-start.13 = (bf16[16,3584]{1,0:T(8,128)(2,1)S(1)}, bf16[16,3584]{1,0:T(8,128)(2,1)S(1)}, u32[]{:S(2)}, u32[]{:S(2)}) collective-permute-start(bf16[16,3584]{1,0:T(8,128)(2,1)S(1)} %get-tuple-element.48), channel_id=1, source_target_pairs={{0,6},{1,7},{2,4},{3,5},{4,2},{5,3},{6,0},{7,1},{8,14},{9,15},{10,... | collective-permute-start | bytes 344072 | tf_op jit(solution)/shard_map/ppermute | solution.py:519
  38.9 7.2 %collective-permute-start.17 = (bf16[16,1280]{1,0:T(8,128)(2,1)S(1)}, bf16[16,1280]{1,0:T(8,128)(2,1)S(1)}, u32[]{:S(2)}, u32[]{:S(2)}) collective-permute-start(bf16[16,1280]{1,0:T(8,128)(2,1)S(1)} %get-tuple-element.54), channel_id=1, source_target_pairs={{0,8},{1,9},{2,10},{3,11},{4,12},{5,13},{6,14},{7,15},{8,0},{9,1},... | collective-permute-start | bytes 122888 | tf_op jit(solution)/shard_map/ppermute | solution.py:519
  41.7 8.2 %collective-permute-start.15 = (bf16[16,3584]{1,0:T(8,128)(2,1)S(1)}, bf16[16,3584]{1,0:T(8,128)(2,1)S(1)}, u32[]{:S(2)}, u32[]{:S(2)}) collective-permute-start(bf16[16,3584]{1,0:T(8,128)(2,1)S(1)} %get-tuple-element.52), channel_id=1, source_target_pairs={{0,12},{1,13},{2,14},{3,15},{4,8},{5,9},{6,10},{7,11},{8,4},{9,5},... | collective-permute-start | bytes 344072 | tf_op jit(solution)/shard_map/ppermute | solution.py:519
  44.5 5.5 %collective-permute-start.16 = (bf16[16,3584]{1,0:T(8,128)(2,1)S(1)}, bf16[16,3584]{1,0:T(8,128)(2,1)S(1)}, u32[]{:S(2)}, u32[]{:S(2)}) collective-permute-start(bf16[16,3584]{1,0:T(8,128)(2,1)S(1)} %get-tuple-element.53), channel_id=1, source_target_pairs={{0,2},{1,3},{2,0},{3,1},{4,6},{5,7},{6,4},{7,5},{8,10},{9,11},{10,... | collective-permute-start | bytes 344072 | tf_op jit(solution)/shard_map/ppermute | solution.py:519

commit v6 on v5

--- a/solution.py
+++ b/solution.py
@@ -72,31 +72,40 @@
     width = packed_ref.shape[1]
     groups = buffer.shape[0]
     inner = groups * lane
-    copies = [
-        pltpu.make_async_copy(
-            packed_ref.at[0, :, :, (first + c) * lane : (first + c + 1) * lane],
-            buffer.at[c],
-            sems.at[c],
+    cuts = sems.shape[1]
+    depth = width // cuts
+    copies = {
+        (c, part): pltpu.make_async_copy(
+            packed_ref.at[
+                0,
+                part * depth : (part + 1) * depth,
+                :,
+                (first + c) * lane : (first + c + 1) * lane,
+            ],
+            buffer.at[c, part * depth : (part + 1) * depth],
+            sems.at[c, part],
         )
         for c in range(groups)
-    ]
-    for copy in copies:
+        for part in range(cuts)
+    }
+    for copy in copies.values():
         copy.start()
     tile = 128
-    for c in range(groups):
-        copies[c].wait()
+    for (c, part), copy in copies.items():
+        copy.wait()
         rows = buffer.at[c].reshape(2 * width, lane)
 
         def step(i, _):
-            both = rows.at[pl.ds(pl.multiple_of(i * 2 * tile, 2 * tile), 2 * tile), :]
-            to = pl.ds(pl.multiple_of(i * tile, tile), tile)
+            at = part * depth + i * tile
+            both = rows.at[pl.ds(pl.multiple_of(2 * at, 2 * tile), 2 * tile), :]
+            to = pl.ds(pl.multiple_of(at, tile), tile)
             out_ref[to, c * lane : (c + 1) * lane] = both[pl.ds(0, tile, stride=2), :]
             out_ref[to, inner + c * lane : inner + (c + 1) * lane] = both[
                 pl.ds(1, tile, stride=2), :
             ]
             return 0
 
-        lax.fori_loop(0, width // tile, step, 0, unroll=2)
+        lax.fori_loop(0, depth // tile, step, 0, unroll=7)
 
 
 def unpack(packed, first, groups, after, cost=0):
@@ -111,7 +120,7 @@
         out_specs=[VMEM, VMEM],
         scratch_shapes=[
             pltpu.VMEM((groups, width, 2, lane), jnp.bfloat16),
-            pltpu.SemaphoreType.DMA((groups,)),
+            pltpu.SemaphoreType.DMA((groups, 4)),
         ],
         compiler_params=limit(9),
         cost_estimate=pl.CostEstimate(flops=0, bytes_accessed=cost, transcendentals=0),
@@ -319,206 +328,6 @@
     return lax.ppermute(block, "ep", [(i, i ^ offset) for i in range(count)])
 
 
-def join_kernel(sizes, *refs):
-    sources, out_refs = refs[: sum(sizes)], refs[-len(sizes) :]
-    at = 0
-    for size, out_ref in zip(sizes, out_refs):
-        to = 0
-        for source in sources[at : at + size]:
-            rows = source.shape[0]
-            out_ref[to : to + rows, :] = source[...]
-            to += rows
-        at += size
-
-
-def join(groups, after):
-    blocks = [block for group in groups for block in group]
-    shapes = [(sum(b.shape[0] for b in group), group[0].shape[1]) for group in groups]
-    return pl.pallas_call(
-        functools.partial(join_kernel, tuple(len(group) for group in groups)),
-        out_shape=[jax.ShapeDtypeStruct(shape, jnp.bfloat16) for shape in shapes],
-        in_specs=[VMEM] * len(blocks) + [ANY] * len(after),
-        out_specs=[VMEM] * len(groups),
-        compiler_params=limit(4 if len(blocks) < 8 else 12),
-        name="join",
-    )(*blocks, *after)
-
-
-def hidden_rows(rows_ref, gu_refs, hidden, at, tile):
-    to = 0
-    rows = rows_ref[at : at + tile, : gu_refs[0].shape[0]]
-    for gu_ref in gu_refs:
-        half = gu_ref.shape[1] // 2
-        step = min(256, half)
-        for n in range(0, half, step):
-            gate = jnp.dot(rows, gu_ref[:, n : n + step], preferred_element_type=jnp.float32)
-            up = jnp.dot(
-                rows, gu_ref[:, half + n : half + n + step], preferred_element_type=jnp.float32
-            )
-            hidden[at : at + tile, to : to + step] = (jax.nn.silu(gate) * up).astype(jnp.bfloat16)
-            to += step
-
-
-def fill(rows_ref, block_refs):
-    to = 0
-    for block_ref in block_refs:
-        rows = block_ref.shape[0]
-        rows_ref[to : to + rows, :] = block_ref[...]
-        to += rows
-
-
-def hidden_and_share(rows_ref, gu_refs, hidden, share_ref):
-    rows = rows_ref.shape[0]
-    width = gu_refs[0].shape[0]
-    tile = min(256, rows)
-    for at in range(0, rows, tile):
-        hidden_rows(rows_ref, gu_refs, hidden, at, min(tile, rows - at))
-    shares = rows_ref[:, width:].astype(jnp.float32)
-    lanes = lax.broadcasted_iota(jnp.int32, shares.shape, 1)
-    mine = jnp.where(lanes == lax.axis_index("ep"), shares, 0.0)
-    share_ref[...] = jnp.broadcast_to(jnp.sum(mine, axis=1, keepdims=True), shares.shape)
-
-
-def hidden_kernel(count, after, *refs):
-    block_refs, gu_refs = refs[:count], refs[count : -3 - after]
-    hidden, share_ref, rows_ref = refs[-3:]
-    fill(rows_ref, block_refs)
-    hidden_and_share(rows_ref, gu_refs, hidden, share_ref)
-
-
-def hidden_of(blocks, halves, after):
-    count, wide = sum(b.shape[0] for b in blocks), blocks[0].shape[1]
-    width, inner = halves[0].shape[0], sum(h.shape[1] // 2 for h in halves)
-    return pl.pallas_call(
-        functools.partial(hidden_kernel, len(blocks), len(after)),
-        out_shape=[
-            jax.ShapeDtypeStruct((count, inner), jnp.bfloat16),
-            jax.ShapeDtypeStruct((count, lane), jnp.float32),
-        ],
-        in_specs=[VMEM] * (len(blocks) + len(halves)) + [ANY] * len(after),
-        out_specs=[VMEM, VMEM],
-        scratch_shapes=[pltpu.VMEM((count, wide), jnp.bfloat16)],
-        compiler_params=limit(6 if count <= 256 else 16),
-        cost_estimate=pl.CostEstimate(flops=0, bytes_accessed=0, transcendentals=0),
-        name="hidden",
-    )(*blocks, *halves, *after)
-
-
-def down_rows(hidden, share, down_ref, out_ref):
-    count, width = out_ref.shape
-    tile = min(256, count)
-    step = 512
-    for at in range(0, count, tile):
-        for n in range(0, width, step):
-            piece = jnp.dot(
-                hidden[at : at + tile, :],
-                down_ref[0, :, n : n + step],
-                preferred_element_type=jnp.float32,
-            )
-            piece = piece.astype(jnp.bfloat16).astype(jnp.float32)
-            terms = (share[at : at + tile, :1] * piece).astype(jnp.bfloat16)
-            out_ref[at : at + tile, n : n + step] = terms
-
-
-def away_kernel(sets, count, places, down_ref, *refs):
-    hidden_refs, share_refs, refs = refs[:sets], refs[sets : 2 * sets], refs[2 * sets :]
-    block_refs, gu_refs = refs[:count], refs[count:-7]
-    away_ref, here_hidden, here_share, last_rows, last_hidden, last_share, hidden = refs[-7:]
-    half = away_ref.shape[0]
-    size = 2 * half // len(places)
-    fill(last_rows, block_refs)
-    hidden_and_share(last_rows, gu_refs, last_hidden, last_share)
-    hidden_refs = (*hidden_refs, last_hidden)
-    share_refs = (*share_refs, last_share)
-    shares = []
-    for to, (which, at) in enumerate(places):
-        part = slice(at, at + size)
-        place = slice(to * size % half, to * size % half + size)
-        if to * size < half:
-            hidden[place, :] = hidden_refs[which][part, :]
-            shares.append(share_refs[which][part, :])
-        else:
-            here_hidden[place, :] = hidden_refs[which][part, :]
-            here_share[place, :] = share_refs[which][part, :]
-    down_rows(hidden, jnp.concatenate(shares, axis=0), down_ref, away_ref)
-
-
-def here_kernel(down_ref, hidden_ref, share_ref, out_ref):
-    down_rows(hidden_ref, share_ref, down_ref, out_ref)
-
-
-def expert(down, hidden, shares, last, halves, places, rows):
-    half = rows * len(places) // 2
-    last_count = sum(b.shape[0] for b in last)
-    _, inner, width = down.shape
-    shape = jax.ShapeDtypeStruct
-    away, here_hidden, here_share = pl.pallas_call(
-        functools.partial(away_kernel, len(hidden), len(last), tuple(places)),
-        out_shape=[
-            shape((half, width), jnp.bfloat16),
-            shape((half, inner), jnp.bfloat16),
-            shape((half, lane), jnp.float32),
-        ],
-        in_specs=[VMEM] * (1 + 2 * len(hidden) + len(last) + len(halves)),
-        out_specs=[VMEM] * 3,
-        scratch_shapes=[
-            pltpu.VMEM((last_count, width + lane), jnp.bfloat16),
-            pltpu.VMEM((last_count, inner), jnp.bfloat16),
-            pltpu.VMEM((last_count, lane), jnp.float32),
-            pltpu.VMEM((half, inner), jnp.bfloat16),
-        ],
-        compiler_params=limit(8 if half <= 128 else 24),
-        cost_estimate=pl.CostEstimate(
-            flops=6 * half * width * inner, bytes_accessed=0, transcendentals=half * inner
-        ),
-        name="away",
-    )(down, *hidden, *shares, *last, *halves)
-    here = pl.pallas_call(
-        here_kernel,
-        out_shape=shape((half, width), jnp.bfloat16),
-        in_specs=[VMEM] * 3,
-        out_specs=VMEM,
-        compiler_params=limit(4 if half <= 128 else 8),
-        cost_estimate=pl.CostEstimate(
-            flops=2 * half * width * inner, bytes_accessed=0, transcendentals=0
-        ),
-        name="here",
-    )(down, here_hidden, here_share)
-    return away, here
-
-
-def add_kernel(pieces, got_ref, here_ref, *refs):
-    later = (len(refs) - len(pieces)) // 2
-    for piece, out_ref in zip(pieces, refs[later:]):
-        to = 0
-        for rows, columns in piece:
-            here = here_ref[slice(*rows), slice(*columns)].astype(jnp.float32)
-            got = got_ref[slice(*rows), slice(*columns)].astype(jnp.float32)
-            end = to + columns[1] - columns[0]
-            out_ref[:, to:end] = (got + here).astype(jnp.bfloat16)
-            to = end
-    for source, out_ref in zip(refs, refs[len(refs) - later :]):
-        out_ref[...] = source[...]
-
-
-def add(got, here, pieces, later=()):
-    shapes = [(piece[0][0][1] - piece[0][0][0], sum(c[1] - c[0] for _, c in piece)) for piece in pieces]
-    shapes += [array.shape for array in later]
-    return pl.pallas_call(
-        functools.partial(add_kernel, tuple(tuple(piece) for piece in pieces)),
-        out_shape=[jax.ShapeDtypeStruct(shape, jnp.bfloat16) for shape in shapes],
-        in_specs=[VMEM] * (2 + len(later)),
-        out_specs=[VMEM] * len(shapes),
-        compiler_params=limit(2 if got.shape[0] <= 16 else 6 if got.shape[0] <= 128 else 16),
-        name="add",
-    )(got, here, *later)
-
-
-def swap(block, offset):
-    count = lax.axis_size("ep")
-    return lax.ppermute(block, "ep", [(i, i ^ offset) for i in range(count)])
-
-
 def gather_blocks(block, far, gate_up):
     groups = gate_up.shape[3] // lane // 2
     lead, *late = far[:0:-1]
@@ -527,7 +336,7 @@
     first, token = unpack(gate_up, 0, groups, [], 1 << 24)
     (again,) = join([[block]], [token])
     others = {offset: swap(again, offset) for offset in (*late, close, close ^ 2)}
-    along, early = join([[along], [block, beside, along]], [beside])
+    (early,) = join([[block, beside, along]], [])
     across = swap(along, 2)
     second, token = unpack(gate_up, groups, gate_up.shape[3] // lane - groups, [again], 1 << 24)
     halves = [first, second]
@@ -560,7 +369,7 @@
     lead, *late = far[:0:-1]
     close = far[0]
     width = away.shape[1]
-    cut = width // lane * 3 // 8 * lane
+    cut = width // lane * 4 // 8 * lane
     keys = [o for o in order if o & 3 == 0]
     half = len(keys) * rows
     away_rows = {o: (at * rows, at * rows + rows) for at, o in enumerate(keys)}

time: 50.9 us -> 49.5 us (0.972)
  starting transfers between devices: 25.7 us -> 22.5 us
  waiting for transfers between devices: 8.33 us -> 10.9 us
  Pallas kernels: 15.7 us -> 14.9 us
    ppermute x20, starting transfers between devices: 25.7 us -> 22.5 us  [swap(): return lax.ppermute(block, 'ep', [(i, i ^ offset) for i in range(count)])]
    ppermute x20, waiting for transfers between devices: 8.33 us -> 10.9 us  [swap(): return lax.ppermute(block, 'ep', [(i, i ^ offset) for i in range(count)])]
    pallas_call x2, Pallas kernels: 7.32 us -> 6.6 us  [unpack(): pl.pallas_call(functools.partial(unpack_kernel, first), out_shape=[jax.Sh...]
  transfers between devices with their start and end apart: 20 -> 20, of which waited for: 5 -> 8; matrix products, arithmetic and copies ran while one was open for 0% -> 0% of each run, Pallas kernels for 22% -> 21%
where the time goes in v6:
time: 49.5 us; the launch traced here: 49.4 us
  starting transfers between devices  22.5 us (45%)
  Pallas kernels  14.9 us (30%)
  waiting for transfers between devices  10.9 us (22%)
  other arithmetic  0.78 us (2%)
    ppermute x20, starting transfers between devices, swap(): return lax.ppermute(block, 'ep', [(i, i ^ offset) for i in range(count)])  22.5 us
    ppermute x20, waiting for transfers between devices, swap(): return lax.ppermute(block, 'ep', [(i, i ^ offset) for i in range(count)])  10.9 us
    pallas_call x2, Pallas kernels, unpack(): pl.pallas_call(functools.partial(unpack_kernel, first), out_shape=[jax.Sh...  6.6 us
    pallas_call x1, Pallas kernels, expert(): pl.pallas_call(functools.partial(away_kernel, len(hidden), len(last), tup...  3.42 us
    pallas_call x1, Pallas kernels, hidden_of(): pl.pallas_call(functools.partial(hidden_kernel, len(blocks), len(after)),...  2.35 us
    pallas_call x1, Pallas kernels, expert(): pl.pallas_call(here_kernel, out_shape=shape((half, width), jnp.bfloat16),...  1.14 us
    pallas_call x1, Pallas kernels, norm(): pl.pallas_call(norm_kernel, out_shape=jax.ShapeDtypeStruct((rows, width +...  1.1 us
  transfers between devices with their start and end apart: 20, of which 8 were waited for; matrix products, arithmetic and copies ran while one was open for 0% of the time, Pallas kernels for 21%

profile of v6, /device:TPU:0, one launch (start us, length us, event | category | flops | bytes accessed | tf_op | source)
XLA Modules:
  0.0 49.4 jit_solution(7668617571573243167)
XLA Ops:
  0.0 1.1 %norm.1.refs_0_ = bf16[16,3712]{1,0:T(8,128)(2,1)S(1)} custom-call(bf16[16,3584]{1,0:T(8,128)(2,1)} %refs_0_.1, f32[3584]{0:T(1024)} %refs_1_.1, s32[8,16]{1,0:T(8,128)} %bitcast.4, bf16[8,16]{1,0:T(8,128)(2,1)} %bitcast.5), custom_call_target="tpu_custom_call" | custom-call | tf_op jit(solution)/shard_map/norm/pallas_call | solution.py:57
  1.1 5.1 %collective-permute-start.1 = (bf16[16,3712]{1,0:T(8,128)(2,1)S(1)}, bf16[16,3712]{1,0:T(8,128)(2,1)S(1)}, u32[]{:S(2)}, u32[]{:S(2)}) collective-permute-start(bf16[16,3712]{1,0:T(8,128)(2,1)S(1)} %norm.1.refs_0_), channel_id=1, source_target_pairs={{0,12},{1,13},{2,14},{3,15},{4,8},{5,9},{6,10},{7,11},{8,4},{9,5},... | collective-permute-start | bytes 356360 | tf_op jit(solution)/shard_map/ppermute | solution.py:328
  6.2 1.5 %collective-permute-start = (bf16[16,3712]{1,0:T(8,128)(2,1)S(1)}, bf16[16,3712]{1,0:T(8,128)(2,1)S(1)}, u32[]{:S(2)}, u32[]{:S(2)}) collective-permute-start(bf16[16,3712]{1,0:T(8,128)(2,1)S(1)} %norm.1.refs_0_), channel_id=1, source_target_pairs={{0,2},{1,3},{2,0},{3,1},{4,6},{5,7},{6,4},{7,5},{8,10},{9,11},{10,... | collective-permute-start | bytes 356360 | tf_op jit(solution)/shard_map/ppermute | solution.py:328
  7.7 3.3 %unpack.2 = (bf16[3584,1024]{1,0:T(8,128)(2,1)S(1)}, f32[8,128]{1,0:T(8,128)S(1)}) custom-call(bf16[1,3584,2,1024]{3,2,1,0:T(2,128)(2,1)} %packed_ref.3), custom_call_target="tpu_custom_call" | custom-call | bytes 16777216 | tf_op jit(solution)/shard_map/unpack/pallas_call | solution.py:113
  11.2 0.6 %collective-permute-start.2 = (bf16[16,3712]{1,0:T(8,128)(2,1)S(1)}, bf16[16,3712]{1,0:T(8,128)(2,1)S(1)}, u32[]{:S(2)}, u32[]{:S(2)}) collective-permute-start(bf16[16,3712]{1,0:T(8,128)(2,1)S(1)} %collective-permute-done.1.refs_2_), channel_id=1, source_target_pairs={{0,2},{1,3},{2,0},{3,1},{4,6},{5,7},{6,4},{7,5},{8,10},{9,11},{10,... | collective-permute-start | bytes 356360 | tf_op jit(solution)/shard_map/ppermute | solution.py:328
  11.7 1.7 %collective-permute-start.5 = (bf16[16,3712]{1,0:T(8,128)(2,1)S(1)}, bf16[16,3712]{1,0:T(8,128)(2,1)S(1)}, u32[]{:S(2)}, u32[]{:S(2)}) collective-permute-start(bf16[16,3712]{1,0:T(8,128)(2,1)S(1)} %join.5.refs_0_), channel_id=1, source_target_pairs={{0,6},{1,7},{2,4},{3,5},{4,2},{5,3},{6,0},{7,1},{8,14},{9,15},{10,... | collective-permute-start | bytes 356360 | tf_op jit(solution)/shard_map/ppermute | solution.py:328
  13.4 1.3 %collective-permute-start.4 = (bf16[16,3712]{1,0:T(8,128)(2,1)S(1)}, bf16[16,3712]{1,0:T(8,128)(2,1)S(1)}, u32[]{:S(2)}, u32[]{:S(2)}) collective-permute-start(bf16[16,3712]{1,0:T(8,128)(2,1)S(1)} %join.5.refs_0_), channel_id=1, source_target_pairs={{0,4},{1,5},{2,6},{3,7},{4,0},{5,1},{6,2},{7,3},{8,12},{9,13},{10,... | collective-permute-start | bytes 356360 | tf_op jit(solution)/shard_map/ppermute | solution.py:328
  14.7 3.3 %unpack.3 = (bf16[3584,1024]{1,0:T(8,128)(2,1)S(1)}, f32[8,128]{1,0:T(8,128)S(1)}) custom-call(bf16[1,3584,2,1024]{3,2,1,0:T(2,128)(2,1)} %packed_ref.3, bf16[16,3712]{1,0:T(8,128)(2,1)S(1)} %join.5.refs_0_), custom_call_target="tpu_custom_call" | custom-call | bytes 16777216 | tf_op jit(solution)/shard_map/unpack/pallas_call | solution.py:113
  18.1 0.6 %collective-permute-start.8 = (bf16[16,3712]{1,0:T(8,128)(2,1)S(1)}, bf16[16,3712]{1,0:T(8,128)(2,1)S(1)}, u32[]{:S(2)}, u32[]{:S(2)}) collective-permute-start(bf16[16,3712]{1,0:T(8,128)(2,1)S(1)} %get-tuple-element.36), channel_id=1, source_target_pairs={{0,2},{1,3},{2,0},{3,1},{4,6},{5,7},{6,4},{7,5},{8,10},{9,11},{10,... | collective-permute-start | bytes 356360 | tf_op jit(solution)/shard_map/ppermute | solution.py:328
  18.7 0.5 %collective-permute-start.7 = (bf16[32,3712]{1,0:T(8,128)(2,1)S(1)}, bf16[32,3712]{1,0:T(8,128)(2,1)S(1)}, u32[]{:S(2)}, u32[]{:S(2)}) collective-permute-start(bf16[32,3712]{1,0:T(8,128)(2,1)S(1)} %get-tuple-element.31.refs_1_), channel_id=1, source_target_pairs={{0,1},{1,0},{2,3},{3,2},{4,5},{5,4},{6,7},{7,6},{8,9},{9,8},{10,11... | collective-permute-start | bytes 712712 | tf_op jit(solution)/shard_map/ppermute | solution.py:328
  19.2 1.3 %collective-permute-done.5.refs_3_.refs_2_ = bf16[16,3712]{1,0:T(8,128)(2,1)S(1)} collective-permute-done((bf16[16,3712]{1,0:T(8,128)(2,1)S(1)}, bf16[16,3712]{1,0:T(8,128)(2,1)S(1)}, u32[]{:S(2)}, u32[]{:S(2)}) %collective-permute-start.5) | collective-permute-done | bytes 118816 | tf_op jit(solution)/shard_map/ppermute | solution.py:328
  20.5 1.4 %collective-permute-done.4.refs_2_.refs_1_ = bf16[16,3712]{1,0:T(8,128)(2,1)S(1)} collective-permute-done((bf16[16,3712]{1,0:T(8,128)(2,1)S(1)}, bf16[16,3712]{1,0:T(8,128)(2,1)S(1)}, u32[]{:S(2)}, u32[]{:S(2)}) %collective-permute-start.4) | collective-permute-done | bytes 118816 | tf_op jit(solution)/shard_map/ppermute | solution.py:328
  21.8 2.3 %hidden.1 = (bf16[112,1024]{1,0:T(8,128)(2,1)S(1)}, f32[112,128]{1,0:T(8,128)S(1)}) custom-call(bf16[48,3712]{1,0:T(8,128)(2,1)S(1)} %join.4.refs_0_, bf16[32,3712]{1,0:T(8,128)(2,1)S(1)} %get-tuple-element.31.refs_1_, bf16[16,3712]{1,0:T(8,128)(2,1)S(1)} %collective-permute-done.4.refs_2_.refs_1_, ...), custom_call_target="tpu_custom_call" | custom-call | tf_op jit(solution)/shard_map/hidden/pallas_call | solution.py:201
  24.3 0.5 %collective-permute-start.10 = (bf16[16,3712]{1,0:T(8,128)(2,1)S(1)}, bf16[16,3712]{1,0:T(8,128)(2,1)S(1)}, u32[]{:S(2)}, u32[]{:S(2)}) collective-permute-start(bf16[16,3712]{1,0:T(8,128)(2,1)S(1)} %get-tuple-element.38.refs_5_), channel_id=1, source_target_pairs={{0,1},{1,0},{2,3},{3,2},{4,5},{5,4},{6,7},{7,6},{8,9},{9,8},{10,11... | collective-permute-start | bytes 356360 | tf_op jit(solution)/shard_map/ppermute | solution.py:328
  24.8 1.2 %collective-permute-done.10.refs_6_ = bf16[16,3712]{1,0:T(8,128)(2,1)S(1)} collective-permute-done((bf16[16,3712]{1,0:T(8,128)(2,1)S(1)}, bf16[16,3712]{1,0:T(8,128)(2,1)S(1)}, u32[]{:S(2)}, u32[]{:S(2)}) %collective-permute-start.10) | collective-permute-done | bytes 118816 | tf_op jit(solution)/shard_map/ppermute | solution.py:328
  26.0 3.4 %away.1 = (bf16[128,3584]{1,0:T(8,128)(2,1)S(1)}, bf16[128,1024]{1,0:T(8,128)(2,1)S(1)}, f32[128,128]{1,0:T(8,128)S(1)}) custom-call(bf16[1,1024,3584]{2,1,0:T(8,128)(2,1)S(1)} %bitcast.3, bf16[112,1024]{1,0:T(8,128)(2,1)S(1)} %get-tuple-element.34.refs_0_, f32[112,128]{1,0:T(8,128)S(1)} %get-tuple-element.35.refs_3_.refs_1_, ...), custom_call_target="tpu_custom_call" | custom-call | flops 2818572288 | tf_op jit(solution)/shard_map/away/pallas_call | solution.py:264
  29.5 0.2 collective-permute-start.11
  29.7 1.1 %here.1.here_ref = bf16[128,3584]{1,0:T(8,128)(2,1)S(1)} custom-call(bf16[1,1024,3584]{2,1,0:T(8,128)(2,1)S(1)} %bitcast.3, bf16[128,1024]{1,0:T(8,128)(2,1)S(1)} %get-tuple-element.40.hidden_ref, f32[128,128]{1,0:T(8,128)S(1)} %get-tuple-element.41.share_ref), custom_call_target="tpu_custom_call" | custom-call | flops 939524096 | tf_op jit(solution)/shard_map/here/pallas_call | solution.py:285
  30.8 1.2 %collective-permute-done.11.got_ref = bf16[128,3584]{1,0:T(8,128)(2,1)S(1)} collective-permute-done((bf16[128,3584]{1,0:T(8,128)(2,1)S(1)}, bf16[128,3584]{1,0:T(8,128)(2,1)S(1)}, u32[]{:S(2)}, u32[]{:S(2)}) %collective-permute-start.11) | collective-permute-done | bytes 917536 | tf_op jit(solution)/shard_map/ppermute | solution.py:328
  32.0 0.2 add.43
  32.2 0.5 %collective-permute-start.14 = (bf16[16,5376]{1,0:T(8,128)(2,1)S(1)}, bf16[16,5376]{1,0:T(8,128)(2,1)S(1)}, u32[]{:S(2)}, u32[]{:S(2)}) collective-permute-start(bf16[16,5376]{1,0:T(8,128)(2,1)S(1)} %get-tuple-element.45), channel_id=1, source_target_pairs={{0,2},{1,3},{2,0},{3,1},{4,6},{5,7},{6,4},{7,5},{8,10},{9,11},{10,... | collective-permute-start | bytes 516104 | tf_op jit(solution)/shard_map/ppermute | solution.py:328
  32.7 1.7 %collective-permute-start.18 = (bf16[16,1792]{1,0:T(8,128)(2,1)S(1)}, bf16[16,1792]{1,0:T(8,128)(2,1)S(1)}, u32[]{:S(2)}, u32[]{:S(2)}) collective-permute-start(bf16[16,1792]{1,0:T(8,128)(2,1)S(1)} %get-tuple-element.51), channel_id=1, source_target_pairs={{0,8},{1,9},{2,10},{3,11},{4,12},{5,13},{6,14},{7,15},{8,0},{9,1},... | collective-permute-start | bytes 172040 | tf_op jit(solution)/shard_map/ppermute | solution.py:328
  34.4 2.2 %collective-permute-start.19 = (bf16[16,1792]{1,0:T(8,128)(2,1)S(1)}, bf16[16,1792]{1,0:T(8,128)(2,1)S(1)}, u32[]{:S(2)}, u32[]{:S(2)}) collective-permute-start(bf16[16,1792]{1,0:T(8,128)(2,1)S(1)} %get-tuple-element.52), channel_id=1, source_target_pairs={{0,10},{1,11},{2,8},{3,9},{4,14},{5,15},{6,12},{7,13},{8,2},{9,3},... | collective-permute-start | bytes 172040 | tf_op jit(solution)/shard_map/ppermute | solution.py:328
  36.7 1.9 %collective-permute-start.13 = (bf16[16,3584]{1,0:T(8,128)(2,1)S(1)}, bf16[16,3584]{1,0:T(8,128)(2,1)S(1)}, u32[]{:S(2)}, u32[]{:S(2)}) collective-permute-start(bf16[16,3584]{1,0:T(8,128)(2,1)S(1)} %get-tuple-element.44), channel_id=1, source_target_pairs={{0,6},{1,7},{2,4},{3,5},{4,2},{5,3},{6,0},{7,1},{8,14},{9,15},{10,... | collective-permute-start | bytes 344072 | tf_op jit(solution)/shard_map/ppermute | solution.py:328
  38.6 0.3 collective-permute-done.14.got_ref
  39.0 2.1 %collective-permute-start.17 = (bf16[16,1792]{1,0:T(8,128)(2,1)S(1)}, bf16[16,1792]{1,0:T(8,128)(2,1)S(1)}, u32[]{:S(2)}, u32[]{:S(2)}) collective-permute-start(bf16[16,1792]{1,0:T(8,128)(2,1)S(1)} %get-tuple-element.50), channel_id=1, source_target_pairs={{0,8},{1,9},{2,10},{3,11},{4,12},{5,13},{6,14},{7,15},{8,0},{9,1},... | collective-permute-start | bytes 172040 | tf_op jit(solution)/shard_map/ppermute | solution.py:328
  41.1 0.9 %collective-permute-start.15 = (bf16[16,3584]{1,0:T(8,128)(2,1)S(1)}, bf16[16,3584]{1,0:T(8,128)(2,1)S(1)}, u32[]{:S(2)}, u32[]{:S(2)}) collective-permute-start(bf16[16,3584]{1,0:T(8,128)(2,1)S(1)} %get-tuple-element.48), channel_id=1, source_target_pairs={{0,12},{1,13},{2,14},{3,15},{4,8},{5,9},{6,10},{7,11},{8,4},{9,5},... | collective-permute-start | bytes 344072 | tf_op jit(solution)/shard_map/ppermute | solution.py:328
  42.0 1.0 %collective-permute-start.16 = (bf16[16,3584]{1,0:T(8,128)(2,1)S(1)}, bf16[16,3584]{1,0:T(8,128)(2,1)S(1)}, u32[]{:S(2)}, u32[]{:S(2)}) collective-permute-start(bf16[16,3584]{1,0:T(8,128)(2,1)S(1)} %get-tuple-element.49), channel_id=1, source_target_pairs={{0,2},{1,3},{2,0},{3,1},{4,6},{5,7},{6,4},{7,5},{8,10},{9,11},{10,... | collective-permute-start | bytes 344072 | tf_op jit(solution)/shard_map/ppermute | solution.py:328
  43.0 2.1 %collective-permute-done.17 = bf16[16,1792]{1,0:T(8,128)(2,1)S(1)} collective-permute-done((bf16[16,1792]{1,0:T(8,128)(2,1)S(1)}, bf16[16,1792]{1,0:T(8,128)(2,1)S(1)}, u32[]{:S(2)}, u32[]{:S(2)}) %collective-permute-start.17) | collective-permute-done | bytes 57376 | tf_op jit(solution)/shard_map/ppermute | solution.py:328
  45.1 2.2 %collective-permute-done.13 = bf16[16,3584]{1,0:T(8,128)(2,1)S(1)} collective-permute-done((bf16[16,3584]{1,0:T(8,128)(2,1)S(1)}, bf16[16,3584]{1,0:T(8,128)(2,1)S(1)}, u32[]{:S(2)}, u32[]{:S(2)}) %collective-permute-start.13) | collective-permute-done | bytes 114720 | tf_op jit(solution)/shard_map/ppermute | solution.py:328
  47.3 1.3 %collective-permute-done.15 = bf16[16,3584]{1,0:T(8,128)(2,1)S(1)} collective-permute-done((bf16[16,3584]{1,0:T(8,128)(2,1)S(1)}, bf16[16,3584]{1,0:T(8,128)(2,1)S(1)}, u32[]{:S(2)}, u32[]{:S(2)}) %collective-permute-start.15) | collective-permute-done | bytes 114720 | tf_op jit(solution)/shard_map/ppermute | solution.py:328
  48.6 0.8 %fusion.1 = bf16[16,3584]{1,0:T(8,128)(2,1)} fusion(f32[16,1792]{1,0:T(8,128)S(1)} %convert_add_fusion, f32[16,1792]{1,0:T(8,128)S(1)} %convert_element_type.36, bf16[16,3584]{1,0:T(8,128)(2,1)S(1)} %collective-permute-done.16, bf16[16,3584]{1,0:T(8,128)(2,1)S(1)} %collective-permute-done.15, bf16[16,3584]{1,0:T(8,128)(2,1)S(1)} %collective-permute-done.13, ...), kind=kLoop, calls=%fused_computation.2 | loop fusion | flops 802816 | bytes 1032192 | tf_op jit(solution)/shard_map/convert_element_type | solution.py:401
  (30 shorter events, 0.4 us)
Async XLA Ops:
  1.1 10.0 %collective-permute-start.1 = (bf16[16,3712]{1,0:T(8,128)(2,1)S(1)}, bf16[16,3712]{1,0:T(8,128)(2,1)S(1)}, u32[]{:S(2)}, u32[]{:S(2)}) collective-permute-start(bf16[16,3712]{1,0:T(8,128)(2,1)S(1)} %norm.1.refs_0_), channel_id=1, source_target_pairs={{0,12},{1,13},{2,14},{3,15},{4,8},{5,9},{6,10},{7,11},{8,4},{9,5},... | collective-permute-start | bytes 356360 | tf_op jit(solution)/shard_map/ppermute | solution.py:328
  6.2 11.8 %collective-permute-start = (bf16[16,3712]{1,0:T(8,128)(2,1)S(1)}, bf16[16,3712]{1,0:T(8,128)(2,1)S(1)}, u32[]{:S(2)}, u32[]{:S(2)}) collective-permute-start(bf16[16,3712]{1,0:T(8,128)(2,1)S(1)} %norm.1.refs_0_), channel_id=1, source_target_pairs={{0,2},{1,3},{2,0},{3,1},{4,6},{5,7},{6,4},{7,5},{8,10},{9,11},{10,... | collective-permute-start | bytes 356360 | tf_op jit(solution)/shard_map/ppermute | solution.py:328
  11.1 7.0 %collective-permute-start.3 = (bf16[16,3712]{1,0:T(8,128)(2,1)S(1)}, bf16[16,3712]{1,0:T(8,128)(2,1)S(1)}, u32[]{:S(2)}, u32[]{:S(2)}) collective-permute-start(bf16[16,3712]{1,0:T(8,128)(2,1)S(1)} %join.5.refs_0_), channel_id=1, source_target_pairs={{0,8},{1,9},{2,10},{3,11},{4,12},{5,13},{6,14},{7,15},{8,0},{9,1},... | collective-permute-start | bytes 356360 | tf_op jit(solution)/shard_map/ppermute | solution.py:328
  11.2 6.9 %collective-permute-start.2 = (bf16[16,3712]{1,0:T(8,128)(2,1)S(1)}, bf16[16,3712]{1,0:T(8,128)(2,1)S(1)}, u32[]{:S(2)}, u32[]{:S(2)}) collective-permute-start(bf16[16,3712]{1,0:T(8,128)(2,1)S(1)} %collective-permute-done.1.refs_2_), channel_id=1, source_target_pairs={{0,2},{1,3},{2,0},{3,1},{4,6},{5,7},{6,4},{7,5},{8,10},{9,11},{10,... | collective-permute-start | bytes 356360 | tf_op jit(solution)/shard_map/ppermute | solution.py:328
  11.7 8.7 %collective-permute-start.5 = (bf16[16,3712]{1,0:T(8,128)(2,1)S(1)}, bf16[16,3712]{1,0:T(8,128)(2,1)S(1)}, u32[]{:S(2)}, u32[]{:S(2)}) collective-permute-start(bf16[16,3712]{1,0:T(8,128)(2,1)S(1)} %join.5.refs_0_), channel_id=1, source_target_pairs={{0,6},{1,7},{2,4},{3,5},{4,2},{5,3},{6,0},{7,1},{8,14},{9,15},{10,... | collective-permute-start | bytes 356360 | tf_op jit(solution)/shard_map/ppermute | solution.py:328
  13.4 8.5 %collective-permute-start.4 = (bf16[16,3712]{1,0:T(8,128)(2,1)S(1)}, bf16[16,3712]{1,0:T(8,128)(2,1)S(1)}, u32[]{:S(2)}, u32[]{:S(2)}) collective-permute-start(bf16[16,3712]{1,0:T(8,128)(2,1)S(1)} %join.5.refs_0_), channel_id=1, source_target_pairs={{0,4},{1,5},{2,6},{3,7},{4,0},{5,1},{6,2},{7,3},{8,12},{9,13},{10,... | collective-permute-start | bytes 356360 | tf_op jit(solution)/shard_map/ppermute | solution.py:328
  18.0 8.0 %slice-start = ((s8[7340032]{0:T(1024)(128)(4,1)}), s8[4194304]{0:T(1024)(128)(4,1)S(1)}, s32[]{:S(2)}) async-start(s8[7340032]{0:T(1024)(128)(4,1)} %bitcast.2), calls=%async_computation | async-start | bytes 8388608
  18.1 6.1 %collective-permute-start.8 = (bf16[16,3712]{1,0:T(8,128)(2,1)S(1)}, bf16[16,3712]{1,0:T(8,128)(2,1)S(1)}, u32[]{:S(2)}, u32[]{:S(2)}) collective-permute-start(bf16[16,3712]{1,0:T(8,128)(2,1)S(1)} %get-tuple-element.36), channel_id=1, source_target_pairs={{0,2},{1,3},{2,0},{3,1},{4,6},{5,7},{6,4},{7,5},{8,10},{9,11},{10,... | collective-permute-start | bytes 356360 | tf_op jit(solution)/shard_map/ppermute | solution.py:328
  18.7 6.1 %collective-permute-start.6 = (bf16[48,3712]{1,0:T(8,128)(2,1)S(1)}, bf16[48,3712]{1,0:T(8,128)(2,1)S(1)}, u32[]{:S(2)}, u32[]{:S(2)}) collective-permute-start(bf16[48,3712]{1,0:T(8,128)(2,1)S(1)} %join.4.refs_0_), channel_id=1, source_target_pairs={{0,1},{1,0},{2,3},{3,2},{4,5},{5,4},{6,7},{7,6},{8,9},{9,8},{10,11... | collective-permute-start | bytes 1069064 | tf_op jit(solution)/shard_map/ppermute | solution.py:328
  18.7 7.3 %collective-permute-start.7 = (bf16[32,3712]{1,0:T(8,128)(2,1)S(1)}, bf16[32,3712]{1,0:T(8,128)(2,1)S(1)}, u32[]{:S(2)}, u32[]{:S(2)}) collective-permute-start(bf16[32,3712]{1,0:T(8,128)(2,1)S(1)} %get-tuple-element.31.refs_1_), channel_id=1, source_target_pairs={{0,1},{1,0},{2,3},{3,2},{4,5},{5,4},{6,7},{7,6},{8,9},{9,8},{10,11... | collective-permute-start | bytes 712712 | tf_op jit(solution)/shard_map/ppermute | solution.py:328
  21.8 4.2 %slice-start.1 = ((s8[7340032]{0:T(1024)(128)(4,1)}), s8[3145728]{0:T(1024)(128)(4,1)S(1)}, s32[]{:S(2)}) async-start(s8[7340032]{0:T(1024)(128)(4,1)} %bitcast.2), calls=%async_computation.1 | async-start | bytes 6291456
  24.2 1.7 %collective-permute-start.9 = (bf16[32,3712]{1,0:T(8,128)(2,1)S(1)}, bf16[32,3712]{1,0:T(8,128)(2,1)S(1)}, u32[]{:S(2)}, u32[]{:S(2)}) collective-permute-start(bf16[32,3712]{1,0:T(8,128)(2,1)S(1)} %get-tuple-element.37), channel_id=1, source_target_pairs={{0,1},{1,0},{2,3},{3,2},{4,5},{5,4},{6,7},{7,6},{8,9},{9,8},{10,11... | collective-permute-start | bytes 712712 | tf_op jit(solution)/shard_map/ppermute | solution.py:328
  24.3 1.7 %collective-permute-start.10 = (bf16[16,3712]{1,0:T(8,128)(2,1)S(1)}, bf16[16,3712]{1,0:T(8,128)(2,1)S(1)}, u32[]{:S(2)}, u32[]{:S(2)}) collective-permute-start(bf16[16,3712]{1,0:T(8,128)(2,1)S(1)} %get-tuple-element.38.refs_5_), channel_id=1, source_target_pairs={{0,1},{1,0},{2,3},{3,2},{4,5},{5,4},{6,7},{7,6},{8,9},{9,8},{10,11... | collective-permute-start | bytes 356360 | tf_op jit(solution)/shard_map/ppermute | solution.py:328
  29.4 19.2 %copy-start = (bf16[16,3584]{1,0:T(8,128)(2,1)S(1)}, bf16[16,3584]{1,0:T(8,128)(2,1)}, u32[]{:S(2)}) copy-start(bf16[16,3584]{1,0:T(8,128)(2,1)} %refs_0_.1) | copy-start | bytes 344068
  29.5 2.5 %collective-permute-start.11 = (bf16[128,3584]{1,0:T(8,128)(2,1)S(1)}, bf16[128,3584]{1,0:T(8,128)(2,1)S(1)}, u32[]{:S(2)}, u32[]{:S(2)}) collective-permute-start(bf16[128,3584]{1,0:T(8,128)(2,1)S(1)} %get-tuple-element.39), channel_id=1, source_target_pairs={{0,1},{1,0},{2,3},{3,2},{4,5},{5,4},{6,7},{7,6},{8,9},{9,8},{10,11... | collective-permute-start | bytes 2752520 | tf_op jit(solution)/shard_map/ppermute | solution.py:328
  32.2 6.7 %collective-permute-start.14 = (bf16[16,5376]{1,0:T(8,128)(2,1)S(1)}, bf16[16,5376]{1,0:T(8,128)(2,1)S(1)}, u32[]{:S(2)}, u32[]{:S(2)}) collective-permute-start(bf16[16,5376]{1,0:T(8,128)(2,1)S(1)} %get-tuple-element.45), channel_id=1, source_target_pairs={{0,2},{1,3},{2,0},{3,1},{4,6},{5,7},{6,4},{7,5},{8,10},{9,11},{10,... | collective-permute-start | bytes 516104 | tf_op jit(solution)/shard_map/ppermute | solution.py:328
  32.7 8.4 %collective-permute-start.18 = (bf16[16,1792]{1,0:T(8,128)(2,1)S(1)}, bf16[16,1792]{1,0:T(8,128)(2,1)S(1)}, u32[]{:S(2)}, u32[]{:S(2)}) collective-permute-start(bf16[16,1792]{1,0:T(8,128)(2,1)S(1)} %get-tuple-element.51), channel_id=1, source_target_pairs={{0,8},{1,9},{2,10},{3,11},{4,12},{5,13},{6,14},{7,15},{8,0},{9,1},... | collective-permute-start | bytes 172040 | tf_op jit(solution)/shard_map/ppermute | solution.py:328
  34.4 7.6 %collective-permute-start.19 = (bf16[16,1792]{1,0:T(8,128)(2,1)S(1)}, bf16[16,1792]{1,0:T(8,128)(2,1)S(1)}, u32[]{:S(2)}, u32[]{:S(2)}) collective-permute-start(bf16[16,1792]{1,0:T(8,128)(2,1)S(1)} %get-tuple-element.52), channel_id=1, source_target_pairs={{0,10},{1,11},{2,8},{3,9},{4,14},{5,15},{6,12},{7,13},{8,2},{9,3},... | collective-permute-start | bytes 172040 | tf_op jit(solution)/shard_map/ppermute | solution.py:328
  36.7 8.4 %collective-permute-start.12 = (bf16[16,3584]{1,0:T(8,128)(2,1)S(1)}, bf16[16,3584]{1,0:T(8,128)(2,1)S(1)}, u32[]{:S(2)}, u32[]{:S(2)}) collective-permute-start(bf16[16,3584]{1,0:T(8,128)(2,1)S(1)} %get-tuple-element.43), channel_id=1, source_target_pairs={{0,4},{1,5},{2,6},{3,7},{4,0},{5,1},{6,2},{7,3},{8,12},{9,13},{10,... | collective-permute-start | bytes 344072 | tf_op jit(solution)/shard_map/ppermute | solution.py:328
  36.7 10.6 %collective-permute-start.13 = (bf16[16,3584]{1,0:T(8,128)(2,1)S(1)}, bf16[16,3584]{1,0:T(8,128)(2,1)S(1)}, u32[]{:S(2)}, u32[]{:S(2)}) collective-permute-start(bf16[16,3584]{1,0:T(8,128)(2,1)S(1)} %get-tuple-element.44), channel_id=1, source_target_pairs={{0,6},{1,7},{2,4},{3,5},{4,2},{5,3},{6,0},{7,1},{8,14},{9,15},{10,... | collective-permute-start | bytes 344072 | tf_op jit(solution)/shard_map/ppermute | solution.py:328
  39.0 6.1 %collective-permute-start.17 = (bf16[16,1792]{1,0:T(8,128)(2,1)S(1)}, bf16[16,1792]{1,0:T(8,128)(2,1)S(1)}, u32[]{:S(2)}, u32[]{:S(2)}) collective-permute-start(bf16[16,1792]{1,0:T(8,128)(2,1)S(1)} %get-tuple-element.50), channel_id=1, source_target_pairs={{0,8},{1,9},{2,10},{3,11},{4,12},{5,13},{6,14},{7,15},{8,0},{9,1},... | collective-permute-start | bytes 172040 | tf_op jit(solution)/shard_map/ppermute | solution.py:328
  41.1 7.5 %collective-permute-start.15 = (bf16[16,3584]{1,0:T(8,128)(2,1)S(1)}, bf16[16,3584]{1,0:T(8,128)(2,1)S(1)}, u32[]{:S(2)}, u32[]{:S(2)}) collective-permute-start(bf16[16,3584]{1,0:T(8,128)(2,1)S(1)} %get-tuple-element.48), channel_id=1, source_target_pairs={{0,12},{1,13},{2,14},{3,15},{4,8},{5,9},{6,10},{7,11},{8,4},{9,5},... | collective-permute-start | bytes 344072 | tf_op jit(solution)/shard_map/ppermute | solution.py:328
  42.0 6.6 %collective-permute-start.16 = (bf16[16,3584]{1,0:T(8,128)(2,1)S(1)}, bf16[16,3584]{1,0:T(8,128)(2,1)S(1)}, u32[]{:S(2)}, u32[]{:S(2)}) collective-permute-start(bf16[16,3584]{1,0:T(8,128)(2,1)S(1)} %get-tuple-element.49), channel_id=1, source_target_pairs={{0,2},{1,3},{2,0},{3,1},{4,6},{5,7},{6,4},{7,5},{8,10},{9,11},{10,... | collective-permute-start | bytes 344072 | tf_op jit(solution)/shard_map/ppermute | solution.py:328

commit v7 on v6

--- a/solution.py
+++ b/solution.py
@@ -386,10 +386,11 @@
     direct += [swap(sums["away", o], o ^ 2) for o in late]
     whole = [sums["here", 0], swap(sums["here", close], close)]
     whole.append(swap(sums["away", close], close ^ 2))
-    later = [sums["away", 0]]
+    own = sums["away", 0]
+    later = []
     ends = [width + at * cut for at in range(len(late) + 1)]
     parts = [full, *zip(ends, ends[1:])]
-    total, *lows, own = add(got, sums["here"], [[((0, rows), part)] for part in parts], later)
+    total, *lows = add(got, sums["here"], [[((0, rows), part)] for part in parts], later)
     whole.append(swap(total, lead))
     summed = [swap(array, o) for o, array in zip(late, lows)]
     whole.append(swap(own, 2))

time: 49.5 us -> 49.5 us (level)
  starting transfers between devices: 22.5 us -> 23.3 us
  waiting for transfers between devices: 10.9 us -> 10.1 us
    ppermute x20, waiting for transfers between devices: 10.9 us -> 10.1 us  [swap(): return lax.ppermute(block, 'ep', [(i, i ^ offset) for i in range(count)])]
    ppermute x20, starting transfers between devices: 22.5 us -> 23.3 us  [swap(): return lax.ppermute(block, 'ep', [(i, i ^ offset) for i in range(count)])]
where the time goes in v7:
time: 49.5 us; the launch traced here: 49.4 us
  starting transfers between devices  23.3 us (47%)
  Pallas kernels  14.9 us (30%)
  waiting for transfers between devices  10.1 us (20%)
  other arithmetic  0.77 us (2%)
    ppermute x20, starting transfers between devices, swap(): return lax.ppermute(block, 'ep', [(i, i ^ offset) for i in range(count)])  23.3 us
    ppermute x20, waiting for transfers between devices, swap(): return lax.ppermute(block, 'ep', [(i, i ^ offset) for i in range(count)])  10.1 us
    pallas_call x2, Pallas kernels, unpack(): pl.pallas_call(functools.partial(unpack_kernel, first), out_shape=[jax.Sh...  6.6 us
    pallas_call x1, Pallas kernels, expert(): pl.pallas_call(functools.partial(away_kernel, len(hidden), len(last), tup...  3.42 us
    pallas_call x1, Pallas kernels, hidden_of(): pl.pallas_call(functools.partial(hidden_kernel, len(blocks), len(after)),...  2.35 us
    pallas_call x1, Pallas kernels, expert(): pl.pallas_call(here_kernel, out_shape=shape((half, width), jnp.bfloat16),...  1.14 us
    pallas_call x1, Pallas kernels, norm(): pl.pallas_call(norm_kernel, out_shape=jax.ShapeDtypeStruct((rows, width +...  1.1 us
  transfers between devices with their start and end apart: 20, of which 8 were waited for; matrix products, arithmetic and copies ran while one was open for 0% of the time, Pallas kernels for 21%

profile of v7, /device:TPU:0, one launch (start us, length us, event | category | flops | bytes accessed | tf_op | source)
XLA Modules:
  0.0 49.4 jit_solution(6448985191866279067)
XLA Ops:
  0.0 1.1 %norm.1.refs_0_ = bf16[16,3712]{1,0:T(8,128)(2,1)S(1)} custom-call(bf16[16,3584]{1,0:T(8,128)(2,1)} %refs_0_.1, f32[3584]{0:T(1024)} %refs_1_.1, s32[8,16]{1,0:T(8,128)} %bitcast.4, bf16[8,16]{1,0:T(8,128)(2,1)} %bitcast.5), custom_call_target="tpu_custom_call" | custom-call | tf_op jit(solution)/shard_map/norm/pallas_call | solution.py:57
  1.1 5.1 %collective-permute-start.1 = (bf16[16,3712]{1,0:T(8,128)(2,1)S(1)}, bf16[16,3712]{1,0:T(8,128)(2,1)S(1)}, u32[]{:S(2)}, u32[]{:S(2)}) collective-permute-start(bf16[16,3712]{1,0:T(8,128)(2,1)S(1)} %norm.1.refs_0_), channel_id=1, source_target_pairs={{0,12},{1,13},{2,14},{3,15},{4,8},{5,9},{6,10},{7,11},{8,4},{9,5},... | collective-permute-start | bytes 356360 | tf_op jit(solution)/shard_map/ppermute | solution.py:328
  6.2 1.5 %collective-permute-start = (bf16[16,3712]{1,0:T(8,128)(2,1)S(1)}, bf16[16,3712]{1,0:T(8,128)(2,1)S(1)}, u32[]{:S(2)}, u32[]{:S(2)}) collective-permute-start(bf16[16,3712]{1,0:T(8,128)(2,1)S(1)} %norm.1.refs_0_), channel_id=1, source_target_pairs={{0,2},{1,3},{2,0},{3,1},{4,6},{5,7},{6,4},{7,5},{8,10},{9,11},{10,... | collective-permute-start | bytes 356360 | tf_op jit(solution)/shard_map/ppermute | solution.py:328
  7.7 3.3 %unpack.2 = (bf16[3584,1024]{1,0:T(8,128)(2,1)S(1)}, f32[8,128]{1,0:T(8,128)S(1)}) custom-call(bf16[1,3584,2,1024]{3,2,1,0:T(2,128)(2,1)} %packed_ref.3), custom_call_target="tpu_custom_call" | custom-call | bytes 16777216 | tf_op jit(solution)/shard_map/unpack/pallas_call | solution.py:113
  11.2 0.6 %collective-permute-start.2 = (bf16[16,3712]{1,0:T(8,128)(2,1)S(1)}, bf16[16,3712]{1,0:T(8,128)(2,1)S(1)}, u32[]{:S(2)}, u32[]{:S(2)}) collective-permute-start(bf16[16,3712]{1,0:T(8,128)(2,1)S(1)} %collective-permute-done.1.refs_2_), channel_id=1, source_target_pairs={{0,2},{1,3},{2,0},{3,1},{4,6},{5,7},{6,4},{7,5},{8,10},{9,11},{10,... | collective-permute-start | bytes 356360 | tf_op jit(solution)/shard_map/ppermute | solution.py:328
  11.7 1.7 %collective-permute-start.5 = (bf16[16,3712]{1,0:T(8,128)(2,1)S(1)}, bf16[16,3712]{1,0:T(8,128)(2,1)S(1)}, u32[]{:S(2)}, u32[]{:S(2)}) collective-permute-start(bf16[16,3712]{1,0:T(8,128)(2,1)S(1)} %join.5.refs_0_), channel_id=1, source_target_pairs={{0,6},{1,7},{2,4},{3,5},{4,2},{5,3},{6,0},{7,1},{8,14},{9,15},{10,... | collective-permute-start | bytes 356360 | tf_op jit(solution)/shard_map/ppermute | solution.py:328
  13.4 1.3 %collective-permute-start.4 = (bf16[16,3712]{1,0:T(8,128)(2,1)S(1)}, bf16[16,3712]{1,0:T(8,128)(2,1)S(1)}, u32[]{:S(2)}, u32[]{:S(2)}) collective-permute-start(bf16[16,3712]{1,0:T(8,128)(2,1)S(1)} %join.5.refs_0_), channel_id=1, source_target_pairs={{0,4},{1,5},{2,6},{3,7},{4,0},{5,1},{6,2},{7,3},{8,12},{9,13},{10,... | collective-permute-start | bytes 356360 | tf_op jit(solution)/shard_map/ppermute | solution.py:328
  14.7 3.3 %unpack.3 = (bf16[3584,1024]{1,0:T(8,128)(2,1)S(1)}, f32[8,128]{1,0:T(8,128)S(1)}) custom-call(bf16[1,3584,2,1024]{3,2,1,0:T(2,128)(2,1)} %packed_ref.3, bf16[16,3712]{1,0:T(8,128)(2,1)S(1)} %join.5.refs_0_), custom_call_target="tpu_custom_call" | custom-call | bytes 16777216 | tf_op jit(solution)/shard_map/unpack/pallas_call | solution.py:113
  18.1 0.6 %collective-permute-start.8 = (bf16[16,3712]{1,0:T(8,128)(2,1)S(1)}, bf16[16,3712]{1,0:T(8,128)(2,1)S(1)}, u32[]{:S(2)}, u32[]{:S(2)}) collective-permute-start(bf16[16,3712]{1,0:T(8,128)(2,1)S(1)} %get-tuple-element.35), channel_id=1, source_target_pairs={{0,2},{1,3},{2,0},{3,1},{4,6},{5,7},{6,4},{7,5},{8,10},{9,11},{10,... | collective-permute-start | bytes 356360 | tf_op jit(solution)/shard_map/ppermute | solution.py:328
  18.7 0.5 %collective-permute-start.7 = (bf16[32,3712]{1,0:T(8,128)(2,1)S(1)}, bf16[32,3712]{1,0:T(8,128)(2,1)S(1)}, u32[]{:S(2)}, u32[]{:S(2)}) collective-permute-start(bf16[32,3712]{1,0:T(8,128)(2,1)S(1)} %get-tuple-element.30.refs_1_), channel_id=1, source_target_pairs={{0,1},{1,0},{2,3},{3,2},{4,5},{5,4},{6,7},{7,6},{8,9},{9,8},{10,11... | collective-permute-start | bytes 712712 | tf_op jit(solution)/shard_map/ppermute | solution.py:328
  19.2 1.3 %collective-permute-done.5.refs_3_.refs_2_ = bf16[16,3712]{1,0:T(8,128)(2,1)S(1)} collective-permute-done((bf16[16,3712]{1,0:T(8,128)(2,1)S(1)}, bf16[16,3712]{1,0:T(8,128)(2,1)S(1)}, u32[]{:S(2)}, u32[]{:S(2)}) %collective-permute-start.5) | collective-permute-done | bytes 118816 | tf_op jit(solution)/shard_map/ppermute | solution.py:328
  20.5 1.4 %collective-permute-done.4.refs_2_.refs_1_ = bf16[16,3712]{1,0:T(8,128)(2,1)S(1)} collective-permute-done((bf16[16,3712]{1,0:T(8,128)(2,1)S(1)}, bf16[16,3712]{1,0:T(8,128)(2,1)S(1)}, u32[]{:S(2)}, u32[]{:S(2)}) %collective-permute-start.4) | collective-permute-done | bytes 118816 | tf_op jit(solution)/shard_map/ppermute | solution.py:328
  21.8 2.3 %hidden.1 = (bf16[112,1024]{1,0:T(8,128)(2,1)S(1)}, f32[112,128]{1,0:T(8,128)S(1)}) custom-call(bf16[48,3712]{1,0:T(8,128)(2,1)S(1)} %join.4.refs_0_, bf16[32,3712]{1,0:T(8,128)(2,1)S(1)} %get-tuple-element.30.refs_1_, bf16[16,3712]{1,0:T(8,128)(2,1)S(1)} %collective-permute-done.4.refs_2_.refs_1_, ...), custom_call_target="tpu_custom_call" | custom-call | tf_op jit(solution)/shard_map/hidden/pallas_call | solution.py:201
  24.3 0.5 %collective-permute-start.10 = (bf16[16,3712]{1,0:T(8,128)(2,1)S(1)}, bf16[16,3712]{1,0:T(8,128)(2,1)S(1)}, u32[]{:S(2)}, u32[]{:S(2)}) collective-permute-start(bf16[16,3712]{1,0:T(8,128)(2,1)S(1)} %get-tuple-element.37.refs_5_), channel_id=1, source_target_pairs={{0,1},{1,0},{2,3},{3,2},{4,5},{5,4},{6,7},{7,6},{8,9},{9,8},{10,11... | collective-permute-start | bytes 356360 | tf_op jit(solution)/shard_map/ppermute | solution.py:328
  24.8 1.2 %collective-permute-done.10.refs_6_ = bf16[16,3712]{1,0:T(8,128)(2,1)S(1)} collective-permute-done((bf16[16,3712]{1,0:T(8,128)(2,1)S(1)}, bf16[16,3712]{1,0:T(8,128)(2,1)S(1)}, u32[]{:S(2)}, u32[]{:S(2)}) %collective-permute-start.10) | collective-permute-done | bytes 118816 | tf_op jit(solution)/shard_map/ppermute | solution.py:328
  26.0 3.4 %away.1 = (bf16[128,3584]{1,0:T(8,128)(2,1)S(1)}, bf16[128,1024]{1,0:T(8,128)(2,1)S(1)}, f32[128,128]{1,0:T(8,128)S(1)}) custom-call(bf16[1,1024,3584]{2,1,0:T(8,128)(2,1)S(1)} %bitcast.3, bf16[112,1024]{1,0:T(8,128)(2,1)S(1)} %get-tuple-element.33.refs_0_, f32[112,128]{1,0:T(8,128)S(1)} %get-tuple-element.34.refs_3_.refs_1_, ...), custom_call_target="tpu_custom_call" | custom-call | flops 2818572288 | tf_op jit(solution)/shard_map/away/pallas_call | solution.py:264
  29.5 0.2 collective-permute-start.11
  29.7 1.1 %here.1.here_ref = bf16[128,3584]{1,0:T(8,128)(2,1)S(1)} custom-call(bf16[1,1024,3584]{2,1,0:T(8,128)(2,1)S(1)} %bitcast.3, bf16[128,1024]{1,0:T(8,128)(2,1)S(1)} %get-tuple-element.39.hidden_ref, f32[128,128]{1,0:T(8,128)S(1)} %get-tuple-element.40.share_ref), custom_call_target="tpu_custom_call" | custom-call | flops 939524096 | tf_op jit(solution)/shard_map/here/pallas_call | solution.py:285
  30.8 1.2 %collective-permute-done.11.got_ref = bf16[128,3584]{1,0:T(8,128)(2,1)S(1)} collective-permute-done((bf16[128,3584]{1,0:T(8,128)(2,1)S(1)}, bf16[128,3584]{1,0:T(8,128)(2,1)S(1)}, u32[]{:S(2)}, u32[]{:S(2)}) %collective-permute-start.11) | collective-permute-done | bytes 917536 | tf_op jit(solution)/shard_map/ppermute | solution.py:328
  32.0 0.2 add.43
  32.2 0.5 %collective-permute-start.14 = (bf16[16,5376]{1,0:T(8,128)(2,1)S(1)}, bf16[16,5376]{1,0:T(8,128)(2,1)S(1)}, u32[]{:S(2)}, u32[]{:S(2)}) collective-permute-start(bf16[16,5376]{1,0:T(8,128)(2,1)S(1)} %get-tuple-element.44), channel_id=1, source_target_pairs={{0,2},{1,3},{2,0},{3,1},{4,6},{5,7},{6,4},{7,5},{8,10},{9,11},{10,... | collective-permute-start | bytes 516104 | tf_op jit(solution)/shard_map/ppermute | solution.py:328
  32.7 1.7 %collective-permute-start.18 = (bf16[16,1792]{1,0:T(8,128)(2,1)S(1)}, bf16[16,1792]{1,0:T(8,128)(2,1)S(1)}, u32[]{:S(2)}, u32[]{:S(2)}) collective-permute-start(bf16[16,1792]{1,0:T(8,128)(2,1)S(1)} %get-tuple-element.49), channel_id=1, source_target_pairs={{0,8},{1,9},{2,10},{3,11},{4,12},{5,13},{6,14},{7,15},{8,0},{9,1},... | collective-permute-start | bytes 172040 | tf_op jit(solution)/shard_map/ppermute | solution.py:328
  34.4 2.2 %collective-permute-start.19 = (bf16[16,1792]{1,0:T(8,128)(2,1)S(1)}, bf16[16,1792]{1,0:T(8,128)(2,1)S(1)}, u32[]{:S(2)}, u32[]{:S(2)}) collective-permute-start(bf16[16,1792]{1,0:T(8,128)(2,1)S(1)} %get-tuple-element.50), channel_id=1, source_target_pairs={{0,10},{1,11},{2,8},{3,9},{4,14},{5,15},{6,12},{7,13},{8,2},{9,3},... | collective-permute-start | bytes 172040 | tf_op jit(solution)/shard_map/ppermute | solution.py:328
  36.7 1.9 %collective-permute-start.13 = (bf16[16,3584]{1,0:T(8,128)(2,1)S(1)}, bf16[16,3584]{1,0:T(8,128)(2,1)S(1)}, u32[]{:S(2)}, u32[]{:S(2)}) collective-permute-start(bf16[16,3584]{1,0:T(8,128)(2,1)S(1)} %get-tuple-element.43), channel_id=1, source_target_pairs={{0,6},{1,7},{2,4},{3,5},{4,2},{5,3},{6,0},{7,1},{8,14},{9,15},{10,... | collective-permute-start | bytes 344072 | tf_op jit(solution)/shard_map/ppermute | solution.py:328
  38.6 0.3 collective-permute-done.14.got_ref
  38.9 1.2 %collective-permute-start.16 = (bf16[16,3584]{1,0:T(8,128)(2,1)S(1)}, bf16[16,3584]{1,0:T(8,128)(2,1)S(1)}, u32[]{:S(2)}, u32[]{:S(2)}) collective-permute-start(bf16[16,3584]{1,0:T(8,128)(2,1)S(1)} %get-tuple-element.47), channel_id=1, source_target_pairs={{0,2},{1,3},{2,0},{3,1},{4,6},{5,7},{6,4},{7,5},{8,10},{9,11},{10,... | collective-permute-start | bytes 344072 | tf_op jit(solution)/shard_map/ppermute | solution.py:328
  40.2 1.7 %collective-permute-start.17 = (bf16[16,1792]{1,0:T(8,128)(2,1)S(1)}, bf16[16,1792]{1,0:T(8,128)(2,1)S(1)}, u32[]{:S(2)}, u32[]{:S(2)}) collective-permute-start(bf16[16,1792]{1,0:T(8,128)(2,1)S(1)} %get-tuple-element.48), channel_id=1, source_target_pairs={{0,8},{1,9},{2,10},{3,11},{4,12},{5,13},{6,14},{7,15},{8,0},{9,1},... | collective-permute-start | bytes 172040 | tf_op jit(solution)/shard_map/ppermute | solution.py:328
  41.9 1.8 %collective-permute-start.15 = (bf16[16,3584]{1,0:T(8,128)(2,1)S(1)}, bf16[16,3584]{1,0:T(8,128)(2,1)S(1)}, u32[]{:S(2)}, u32[]{:S(2)}) collective-permute-start(bf16[16,3584]{1,0:T(8,128)(2,1)S(1)} %get-tuple-element.46), channel_id=1, source_target_pairs={{0,12},{1,13},{2,14},{3,15},{4,8},{5,9},{6,10},{7,11},{8,4},{9,5},... | collective-permute-start | bytes 344072 | tf_op jit(solution)/shard_map/ppermute | solution.py:328
  43.7 1.9 %collective-permute-done.17 = bf16[16,1792]{1,0:T(8,128)(2,1)S(1)} collective-permute-done((bf16[16,1792]{1,0:T(8,128)(2,1)S(1)}, bf16[16,1792]{1,0:T(8,128)(2,1)S(1)}, u32[]{:S(2)}, u32[]{:S(2)}) %collective-permute-start.17) | collective-permute-done | bytes 57376 | tf_op jit(solution)/shard_map/ppermute | solution.py:328
  45.7 1.0 %collective-permute-done.13 = bf16[16,3584]{1,0:T(8,128)(2,1)S(1)} collective-permute-done((bf16[16,3584]{1,0:T(8,128)(2,1)S(1)}, bf16[16,3584]{1,0:T(8,128)(2,1)S(1)}, u32[]{:S(2)}, u32[]{:S(2)}) %collective-permute-start.13) | collective-permute-done | bytes 114720 | tf_op jit(solution)/shard_map/ppermute | solution.py:328
  46.7 1.9 %collective-permute-done.15 = bf16[16,3584]{1,0:T(8,128)(2,1)S(1)} collective-permute-done((bf16[16,3584]{1,0:T(8,128)(2,1)S(1)}, bf16[16,3584]{1,0:T(8,128)(2,1)S(1)}, u32[]{:S(2)}, u32[]{:S(2)}) %collective-permute-start.15) | collective-permute-done | bytes 114720 | tf_op jit(solution)/shard_map/ppermute | solution.py:328
  48.6 0.8 %fusion.1 = bf16[16,3584]{1,0:T(8,128)(2,1)} fusion(f32[16,1792]{1,0:T(8,128)S(1)} %convert_add_fusion, f32[16,1792]{1,0:T(8,128)S(1)} %convert_element_type.36, bf16[16,3584]{1,0:T(8,128)(2,1)S(1)} %collective-permute-done.16, bf16[16,3584]{1,0:T(8,128)(2,1)S(1)} %collective-permute-done.15, bf16[16,3584]{1,0:T(8,128)(2,1)S(1)} %collective-permute-done.13, ...), kind=kLoop, calls=%fused_computation.2 | loop fusion | flops 802816 | bytes 1032192 | tf_op jit(solution)/shard_map/convert_element_type | solution.py:402
  (30 shorter events, 0.4 us)
Async XLA Ops:
  1.1 10.0 %collective-permute-start.1 = (bf16[16,3712]{1,0:T(8,128)(2,1)S(1)}, bf16[16,3712]{1,0:T(8,128)(2,1)S(1)}, u32[]{:S(2)}, u32[]{:S(2)}) collective-permute-start(bf16[16,3712]{1,0:T(8,128)(2,1)S(1)} %norm.1.refs_0_), channel_id=1, source_target_pairs={{0,12},{1,13},{2,14},{3,15},{4,8},{5,9},{6,10},{7,11},{8,4},{9,5},... | collective-permute-start | bytes 356360 | tf_op jit(solution)/shard_map/ppermute | solution.py:328
  6.2 11.8 %collective-permute-start = (bf16[16,3712]{1,0:T(8,128)(2,1)S(1)}, bf16[16,3712]{1,0:T(8,128)(2,1)S(1)}, u32[]{:S(2)}, u32[]{:S(2)}) collective-permute-start(bf16[16,3712]{1,0:T(8,128)(2,1)S(1)} %norm.1.refs_0_), channel_id=1, source_target_pairs={{0,2},{1,3},{2,0},{3,1},{4,6},{5,7},{6,4},{7,5},{8,10},{9,11},{10,... | collective-permute-start | bytes 356360 | tf_op jit(solution)/shard_map/ppermute | solution.py:328
  11.1 7.0 %collective-permute-start.3 = (bf16[16,3712]{1,0:T(8,128)(2,1)S(1)}, bf16[16,3712]{1,0:T(8,128)(2,1)S(1)}, u32[]{:S(2)}, u32[]{:S(2)}) collective-permute-start(bf16[16,3712]{1,0:T(8,128)(2,1)S(1)} %join.5.refs_0_), channel_id=1, source_target_pairs={{0,8},{1,9},{2,10},{3,11},{4,12},{5,13},{6,14},{7,15},{8,0},{9,1},... | collective-permute-start | bytes 356360 | tf_op jit(solution)/shard_map/ppermute | solution.py:328
  11.2 6.9 %collective-permute-start.2 = (bf16[16,3712]{1,0:T(8,128)(2,1)S(1)}, bf16[16,3712]{1,0:T(8,128)(2,1)S(1)}, u32[]{:S(2)}, u32[]{:S(2)}) collective-permute-start(bf16[16,3712]{1,0:T(8,128)(2,1)S(1)} %collective-permute-done.1.refs_2_), channel_id=1, source_target_pairs={{0,2},{1,3},{2,0},{3,1},{4,6},{5,7},{6,4},{7,5},{8,10},{9,11},{10,... | collective-permute-start | bytes 356360 | tf_op jit(solution)/shard_map/ppermute | solution.py:328
  11.7 8.7 %collective-permute-start.5 = (bf16[16,3712]{1,0:T(8,128)(2,1)S(1)}, bf16[16,3712]{1,0:T(8,128)(2,1)S(1)}, u32[]{:S(2)}, u32[]{:S(2)}) collective-permute-start(bf16[16,3712]{1,0:T(8,128)(2,1)S(1)} %join.5.refs_0_), channel_id=1, source_target_pairs={{0,6},{1,7},{2,4},{3,5},{4,2},{5,3},{6,0},{7,1},{8,14},{9,15},{10,... | collective-permute-start | bytes 356360 | tf_op jit(solution)/shard_map/ppermute | solution.py:328
  13.4 8.5 %collective-permute-start.4 = (bf16[16,3712]{1,0:T(8,128)(2,1)S(1)}, bf16[16,3712]{1,0:T(8,128)(2,1)S(1)}, u32[]{:S(2)}, u32[]{:S(2)}) collective-permute-start(bf16[16,3712]{1,0:T(8,128)(2,1)S(1)} %join.5.refs_0_), channel_id=1, source_target_pairs={{0,4},{1,5},{2,6},{3,7},{4,0},{5,1},{6,2},{7,3},{8,12},{9,13},{10,... | collective-permute-start | bytes 356360 | tf_op jit(solution)/shard_map/ppermute | solution.py:328
  18.0 8.0 %slice-start = ((s8[7340032]{0:T(1024)(128)(4,1)}), s8[4194304]{0:T(1024)(128)(4,1)S(1)}, s32[]{:S(2)}) async-start(s8[7340032]{0:T(1024)(128)(4,1)} %bitcast.2), calls=%async_computation | async-start | bytes 8388608
  18.1 6.1 %collective-permute-start.8 = (bf16[16,3712]{1,0:T(8,128)(2,1)S(1)}, bf16[16,3712]{1,0:T(8,128)(2,1)S(1)}, u32[]{:S(2)}, u32[]{:S(2)}) collective-permute-start(bf16[16,3712]{1,0:T(8,128)(2,1)S(1)} %get-tuple-element.35), channel_id=1, source_target_pairs={{0,2},{1,3},{2,0},{3,1},{4,6},{5,7},{6,4},{7,5},{8,10},{9,11},{10,... | collective-permute-start | bytes 356360 | tf_op jit(solution)/shard_map/ppermute | solution.py:328
  18.7 6.1 %collective-permute-start.6 = (bf16[48,3712]{1,0:T(8,128)(2,1)S(1)}, bf16[48,3712]{1,0:T(8,128)(2,1)S(1)}, u32[]{:S(2)}, u32[]{:S(2)}) collective-permute-start(bf16[48,3712]{1,0:T(8,128)(2,1)S(1)} %join.4.refs_0_), channel_id=1, source_target_pairs={{0,1},{1,0},{2,3},{3,2},{4,5},{5,4},{6,7},{7,6},{8,9},{9,8},{10,11... | collective-permute-start | bytes 1069064 | tf_op jit(solution)/shard_map/ppermute | solution.py:328
  18.7 7.3 %collective-permute-start.7 = (bf16[32,3712]{1,0:T(8,128)(2,1)S(1)}, bf16[32,3712]{1,0:T(8,128)(2,1)S(1)}, u32[]{:S(2)}, u32[]{:S(2)}) collective-permute-start(bf16[32,3712]{1,0:T(8,128)(2,1)S(1)} %get-tuple-element.30.refs_1_), channel_id=1, source_target_pairs={{0,1},{1,0},{2,3},{3,2},{4,5},{5,4},{6,7},{7,6},{8,9},{9,8},{10,11... | collective-permute-start | bytes 712712 | tf_op jit(solution)/shard_map/ppermute | solution.py:328
  21.8 4.2 %slice-start.1 = ((s8[7340032]{0:T(1024)(128)(4,1)}), s8[3145728]{0:T(1024)(128)(4,1)S(1)}, s32[]{:S(2)}) async-start(s8[7340032]{0:T(1024)(128)(4,1)} %bitcast.2), calls=%async_computation.1 | async-start | bytes 6291456
  24.2 1.7 %collective-permute-start.9 = (bf16[32,3712]{1,0:T(8,128)(2,1)S(1)}, bf16[32,3712]{1,0:T(8,128)(2,1)S(1)}, u32[]{:S(2)}, u32[]{:S(2)}) collective-permute-start(bf16[32,3712]{1,0:T(8,128)(2,1)S(1)} %get-tuple-element.36), channel_id=1, source_target_pairs={{0,1},{1,0},{2,3},{3,2},{4,5},{5,4},{6,7},{7,6},{8,9},{9,8},{10,11... | collective-permute-start | bytes 712712 | tf_op jit(solution)/shard_map/ppermute | solution.py:328
  24.3 1.7 %collective-permute-start.10 = (bf16[16,3712]{1,0:T(8,128)(2,1)S(1)}, bf16[16,3712]{1,0:T(8,128)(2,1)S(1)}, u32[]{:S(2)}, u32[]{:S(2)}) collective-permute-start(bf16[16,3712]{1,0:T(8,128)(2,1)S(1)} %get-tuple-element.37.refs_5_), channel_id=1, source_target_pairs={{0,1},{1,0},{2,3},{3,2},{4,5},{5,4},{6,7},{7,6},{8,9},{9,8},{10,11... | collective-permute-start | bytes 356360 | tf_op jit(solution)/shard_map/ppermute | solution.py:328
  29.4 19.2 %copy-start = (bf16[16,3584]{1,0:T(8,128)(2,1)S(1)}, bf16[16,3584]{1,0:T(8,128)(2,1)}, u32[]{:S(2)}) copy-start(bf16[16,3584]{1,0:T(8,128)(2,1)} %refs_0_.1) | copy-start | bytes 344068
  29.5 2.5 %collective-permute-start.11 = (bf16[128,3584]{1,0:T(8,128)(2,1)S(1)}, bf16[128,3584]{1,0:T(8,128)(2,1)S(1)}, u32[]{:S(2)}, u32[]{:S(2)}) collective-permute-start(bf16[128,3584]{1,0:T(8,128)(2,1)S(1)} %get-tuple-element.38), channel_id=1, source_target_pairs={{0,1},{1,0},{2,3},{3,2},{4,5},{5,4},{6,7},{7,6},{8,9},{9,8},{10,11... | collective-permute-start | bytes 2752520 | tf_op jit(solution)/shard_map/ppermute | solution.py:328
  32.2 6.7 %collective-permute-start.14 = (bf16[16,5376]{1,0:T(8,128)(2,1)S(1)}, bf16[16,5376]{1,0:T(8,128)(2,1)S(1)}, u32[]{:S(2)}, u32[]{:S(2)}) collective-permute-start(bf16[16,5376]{1,0:T(8,128)(2,1)S(1)} %get-tuple-element.44), channel_id=1, source_target_pairs={{0,2},{1,3},{2,0},{3,1},{4,6},{5,7},{6,4},{7,5},{8,10},{9,11},{10,... | collective-permute-start | bytes 516104 | tf_op jit(solution)/shard_map/ppermute | solution.py:328
  32.7 7.5 %collective-permute-start.18 = (bf16[16,1792]{1,0:T(8,128)(2,1)S(1)}, bf16[16,1792]{1,0:T(8,128)(2,1)S(1)}, u32[]{:S(2)}, u32[]{:S(2)}) collective-permute-start(bf16[16,1792]{1,0:T(8,128)(2,1)S(1)} %get-tuple-element.49), channel_id=1, source_target_pairs={{0,8},{1,9},{2,10},{3,11},{4,12},{5,13},{6,14},{7,15},{8,0},{9,1},... | collective-permute-start | bytes 172040 | tf_op jit(solution)/shard_map/ppermute | solution.py:328
  34.4 7.5 %collective-permute-start.19 = (bf16[16,1792]{1,0:T(8,128)(2,1)S(1)}, bf16[16,1792]{1,0:T(8,128)(2,1)S(1)}, u32[]{:S(2)}, u32[]{:S(2)}) collective-permute-start(bf16[16,1792]{1,0:T(8,128)(2,1)S(1)} %get-tuple-element.50), channel_id=1, source_target_pairs={{0,10},{1,11},{2,8},{3,9},{4,14},{5,15},{6,12},{7,13},{8,2},{9,3},... | collective-permute-start | bytes 172040 | tf_op jit(solution)/shard_map/ppermute | solution.py:328
  36.7 9.0 %collective-permute-start.12 = (bf16[16,3584]{1,0:T(8,128)(2,1)S(1)}, bf16[16,3584]{1,0:T(8,128)(2,1)S(1)}, u32[]{:S(2)}, u32[]{:S(2)}) collective-permute-start(bf16[16,3584]{1,0:T(8,128)(2,1)S(1)} %get-tuple-element.42), channel_id=1, source_target_pairs={{0,4},{1,5},{2,6},{3,7},{4,0},{5,1},{6,2},{7,3},{8,12},{9,13},{10,... | collective-permute-start | bytes 344072 | tf_op jit(solution)/shard_map/ppermute | solution.py:328
  36.7 10.0 %collective-permute-start.13 = (bf16[16,3584]{1,0:T(8,128)(2,1)S(1)}, bf16[16,3584]{1,0:T(8,128)(2,1)S(1)}, u32[]{:S(2)}, u32[]{:S(2)}) collective-permute-start(bf16[16,3584]{1,0:T(8,128)(2,1)S(1)} %get-tuple-element.43), channel_id=1, source_target_pairs={{0,6},{1,7},{2,4},{3,5},{4,2},{5,3},{6,0},{7,1},{8,14},{9,15},{10,... | collective-permute-start | bytes 344072 | tf_op jit(solution)/shard_map/ppermute | solution.py:328
  38.9 7.8 %collective-permute-start.16 = (bf16[16,3584]{1,0:T(8,128)(2,1)S(1)}, bf16[16,3584]{1,0:T(8,128)(2,1)S(1)}, u32[]{:S(2)}, u32[]{:S(2)}) collective-permute-start(bf16[16,3584]{1,0:T(8,128)(2,1)S(1)} %get-tuple-element.47), channel_id=1, source_target_pairs={{0,2},{1,3},{2,0},{3,1},{4,6},{5,7},{6,4},{7,5},{8,10},{9,11},{10,... | collective-permute-start | bytes 344072 | tf_op jit(solution)/shard_map/ppermute | solution.py:328
  40.2 5.5 %collective-permute-start.17 = (bf16[16,1792]{1,0:T(8,128)(2,1)S(1)}, bf16[16,1792]{1,0:T(8,128)(2,1)S(1)}, u32[]{:S(2)}, u32[]{:S(2)}) collective-permute-start(bf16[16,1792]{1,0:T(8,128)(2,1)S(1)} %get-tuple-element.48), channel_id=1, source_target_pairs={{0,8},{1,9},{2,10},{3,11},{4,12},{5,13},{6,14},{7,15},{8,0},{9,1},... | collective-permute-start | bytes 172040 | tf_op jit(solution)/shard_map/ppermute | solution.py:328
  41.9 6.7 %collective-permute-start.15 = (bf16[16,3584]{1,0:T(8,128)(2,1)S(1)}, bf16[16,3584]{1,0:T(8,128)(2,1)S(1)}, u32[]{:S(2)}, u32[]{:S(2)}) collective-permute-start(bf16[16,3584]{1,0:T(8,128)(2,1)S(1)} %get-tuple-element.46), channel_id=1, source_target_pairs={{0,12},{1,13},{2,14},{3,15},{4,8},{5,9},{6,10},{7,11},{8,4},{9,5},... | collective-permute-start | bytes 344072 | tf_op jit(solution)/shard_map/ppermute | solution.py:328

commit v8 on v7

--- a/solution.py
+++ b/solution.py
@@ -191,12 +191,15 @@
 def hidden_kernel(count, after, *refs):
     block_refs, gu_refs = refs[:count], refs[count : -3 - after]
     hidden, share_ref, rows_ref = refs[-3:]
+    used = sum(ref.shape[0] for ref in block_refs)
     fill(rows_ref, block_refs)
+    rows_ref[used:, :] = jnp.zeros_like(rows_ref[used:, :])
     hidden_and_share(rows_ref, gu_refs, hidden, share_ref)
 
 
 def hidden_of(blocks, halves, after):
     count, wide = sum(b.shape[0] for b in blocks), blocks[0].shape[1]
+    count += -count % lane
     width, inner = halves[0].shape[0], sum(h.shape[1] // 2 for h in halves)
     return pl.pallas_call(
         functools.partial(hidden_kernel, len(blocks), len(after)),

time: 49.5 us -> 49.5 us (level)
  transfers between devices with their start and end apart: 20 -> 20, of which waited for: 8 -> 8; matrix products, arithmetic and copies ran while one was open for 0% -> 0% of each run, Pallas kernels for 21% -> 20%
where the time goes in v8:
time: 49.5 us; the launch traced here: 49.4 us
  starting transfers between devices  23.6 us (48%)
  Pallas kernels  14.8 us (30%)
  waiting for transfers between devices  10 us (20%)
  other arithmetic  0.77 us (2%)
    ppermute x20, starting transfers between devices, swap(): return lax.ppermute(block, 'ep', [(i, i ^ offset) for i in range(count)])  23.6 us
    ppermute x20, waiting for transfers between devices, swap(): return lax.ppermute(block, 'ep', [(i, i ^ offset) for i in range(count)])  10 us
    pallas_call x2, Pallas kernels, unpack(): pl.pallas_call(functools.partial(unpack_kernel, first), out_shape=[jax.Sh...  6.6 us
    pallas_call x1, Pallas kernels, expert(): pl.pallas_call(functools.partial(away_kernel, len(hidden), len(last), tup...  3.42 us
    pallas_call x1, Pallas kernels, hidden_of(): pl.pallas_call(functools.partial(hidden_kernel, len(blocks), len(after)),...  2.15 us
    pallas_call x1, Pallas kernels, expert(): pl.pallas_call(here_kernel, out_shape=shape((half, width), jnp.bfloat16),...  1.14 us
    pallas_call x1, Pallas kernels, norm(): pl.pallas_call(norm_kernel, out_shape=jax.ShapeDtypeStruct((rows, width +...  1.1 us
  transfers between devices with their start and end apart: 20, of which 8 were waited for; matrix products, arithmetic and copies ran while one was open for 0% of the time, Pallas kernels for 20%

profile of v8, /device:TPU:0, one launch (start us, length us, event | category | flops | bytes accessed | tf_op | source)
XLA Modules:
  0.0 49.4 jit_solution(6644799765159091779)
XLA Ops:
  0.0 1.1 %norm.1.refs_0_ = bf16[16,3712]{1,0:T(8,128)(2,1)S(1)} custom-call(bf16[16,3584]{1,0:T(8,128)(2,1)} %refs_0_.1, f32[3584]{0:T(1024)} %refs_1_.1, s32[8,16]{1,0:T(8,128)} %bitcast.4, bf16[8,16]{1,0:T(8,128)(2,1)} %bitcast.5), custom_call_target="tpu_custom_call" | custom-call | tf_op jit(solution)/shard_map/norm/pallas_call | solution.py:57
  1.1 5.1 %collective-permute-start.1 = (bf16[16,3712]{1,0:T(8,128)(2,1)S(1)}, bf16[16,3712]{1,0:T(8,128)(2,1)S(1)}, u32[]{:S(2)}, u32[]{:S(2)}) collective-permute-start(bf16[16,3712]{1,0:T(8,128)(2,1)S(1)} %norm.1.refs_0_), channel_id=1, source_target_pairs={{0,12},{1,13},{2,14},{3,15},{4,8},{5,9},{6,10},{7,11},{8,4},{9,5},... | collective-permute-start | bytes 356360 | tf_op jit(solution)/shard_map/ppermute | solution.py:331
  6.2 1.5 %collective-permute-start = (bf16[16,3712]{1,0:T(8,128)(2,1)S(1)}, bf16[16,3712]{1,0:T(8,128)(2,1)S(1)}, u32[]{:S(2)}, u32[]{:S(2)}) collective-permute-start(bf16[16,3712]{1,0:T(8,128)(2,1)S(1)} %norm.1.refs_0_), channel_id=1, source_target_pairs={{0,2},{1,3},{2,0},{3,1},{4,6},{5,7},{6,4},{7,5},{8,10},{9,11},{10,... | collective-permute-start | bytes 356360 | tf_op jit(solution)/shard_map/ppermute | solution.py:331
  7.7 3.3 %unpack.2 = (bf16[3584,1024]{1,0:T(8,128)(2,1)S(1)}, f32[8,128]{1,0:T(8,128)S(1)}) custom-call(bf16[1,3584,2,1024]{3,2,1,0:T(2,128)(2,1)} %packed_ref.3), custom_call_target="tpu_custom_call" | custom-call | bytes 16777216 | tf_op jit(solution)/shard_map/unpack/pallas_call | solution.py:113
  11.2 0.6 %collective-permute-start.2 = (bf16[16,3712]{1,0:T(8,128)(2,1)S(1)}, bf16[16,3712]{1,0:T(8,128)(2,1)S(1)}, u32[]{:S(2)}, u32[]{:S(2)}) collective-permute-start(bf16[16,3712]{1,0:T(8,128)(2,1)S(1)} %collective-permute-done.1.refs_2_), channel_id=1, source_target_pairs={{0,2},{1,3},{2,0},{3,1},{4,6},{5,7},{6,4},{7,5},{8,10},{9,11},{10,... | collective-permute-start | bytes 356360 | tf_op jit(solution)/shard_map/ppermute | solution.py:331
  11.7 1.7 %collective-permute-start.5 = (bf16[16,3712]{1,0:T(8,128)(2,1)S(1)}, bf16[16,3712]{1,0:T(8,128)(2,1)S(1)}, u32[]{:S(2)}, u32[]{:S(2)}) collective-permute-start(bf16[16,3712]{1,0:T(8,128)(2,1)S(1)} %join.5.refs_0_), channel_id=1, source_target_pairs={{0,6},{1,7},{2,4},{3,5},{4,2},{5,3},{6,0},{7,1},{8,14},{9,15},{10,... | collective-permute-start | bytes 356360 | tf_op jit(solution)/shard_map/ppermute | solution.py:331
  13.4 1.3 %collective-permute-start.4 = (bf16[16,3712]{1,0:T(8,128)(2,1)S(1)}, bf16[16,3712]{1,0:T(8,128)(2,1)S(1)}, u32[]{:S(2)}, u32[]{:S(2)}) collective-permute-start(bf16[16,3712]{1,0:T(8,128)(2,1)S(1)} %join.5.refs_0_), channel_id=1, source_target_pairs={{0,4},{1,5},{2,6},{3,7},{4,0},{5,1},{6,2},{7,3},{8,12},{9,13},{10,... | collective-permute-start | bytes 356360 | tf_op jit(solution)/shard_map/ppermute | solution.py:331
  14.7 3.3 %unpack.3 = (bf16[3584,1024]{1,0:T(8,128)(2,1)S(1)}, f32[8,128]{1,0:T(8,128)S(1)}) custom-call(bf16[1,3584,2,1024]{3,2,1,0:T(2,128)(2,1)} %packed_ref.3, bf16[16,3712]{1,0:T(8,128)(2,1)S(1)} %join.5.refs_0_), custom_call_target="tpu_custom_call" | custom-call | bytes 16777216 | tf_op jit(solution)/shard_map/unpack/pallas_call | solution.py:113
  18.1 0.6 %collective-permute-start.8 = (bf16[16,3712]{1,0:T(8,128)(2,1)S(1)}, bf16[16,3712]{1,0:T(8,128)(2,1)S(1)}, u32[]{:S(2)}, u32[]{:S(2)}) collective-permute-start(bf16[16,3712]{1,0:T(8,128)(2,1)S(1)} %get-tuple-element.35), channel_id=1, source_target_pairs={{0,2},{1,3},{2,0},{3,1},{4,6},{5,7},{6,4},{7,5},{8,10},{9,11},{10,... | collective-permute-start | bytes 356360 | tf_op jit(solution)/shard_map/ppermute | solution.py:331
  18.7 0.5 %collective-permute-start.7 = (bf16[32,3712]{1,0:T(8,128)(2,1)S(1)}, bf16[32,3712]{1,0:T(8,128)(2,1)S(1)}, u32[]{:S(2)}, u32[]{:S(2)}) collective-permute-start(bf16[32,3712]{1,0:T(8,128)(2,1)S(1)} %get-tuple-element.30.refs_1_), channel_id=1, source_target_pairs={{0,1},{1,0},{2,3},{3,2},{4,5},{5,4},{6,7},{7,6},{8,9},{9,8},{10,11... | collective-permute-start | bytes 712712 | tf_op jit(solution)/shard_map/ppermute | solution.py:331
  19.2 1.3 %collective-permute-done.5.refs_3_.refs_2_ = bf16[16,3712]{1,0:T(8,128)(2,1)S(1)} collective-permute-done((bf16[16,3712]{1,0:T(8,128)(2,1)S(1)}, bf16[16,3712]{1,0:T(8,128)(2,1)S(1)}, u32[]{:S(2)}, u32[]{:S(2)}) %collective-permute-start.5) | collective-permute-done | bytes 118816 | tf_op jit(solution)/shard_map/ppermute | solution.py:331
  20.5 1.4 %collective-permute-done.4.refs_2_.refs_1_ = bf16[16,3712]{1,0:T(8,128)(2,1)S(1)} collective-permute-done((bf16[16,3712]{1,0:T(8,128)(2,1)S(1)}, bf16[16,3712]{1,0:T(8,128)(2,1)S(1)}, u32[]{:S(2)}, u32[]{:S(2)}) %collective-permute-start.4) | collective-permute-done | bytes 118816 | tf_op jit(solution)/shard_map/ppermute | solution.py:331
  21.8 2.2 %hidden.1 = (bf16[128,1024]{1,0:T(8,128)(2,1)S(1)}, f32[128,128]{1,0:T(8,128)S(1)}) custom-call(bf16[48,3712]{1,0:T(8,128)(2,1)S(1)} %join.4.refs_0_, bf16[32,3712]{1,0:T(8,128)(2,1)S(1)} %get-tuple-element.30.refs_1_, bf16[16,3712]{1,0:T(8,128)(2,1)S(1)} %collective-permute-done.4.refs_2_.refs_1_, ...), custom_call_target="tpu_custom_call" | custom-call | tf_op jit(solution)/shard_map/hidden/pallas_call | solution.py:204
  24.1 0.5 %collective-permute-start.10 = (bf16[16,3712]{1,0:T(8,128)(2,1)S(1)}, bf16[16,3712]{1,0:T(8,128)(2,1)S(1)}, u32[]{:S(2)}, u32[]{:S(2)}) collective-permute-start(bf16[16,3712]{1,0:T(8,128)(2,1)S(1)} %get-tuple-element.37.refs_5_), channel_id=1, source_target_pairs={{0,1},{1,0},{2,3},{3,2},{4,5},{5,4},{6,7},{7,6},{8,9},{9,8},{10,11... | collective-permute-start | bytes 356360 | tf_op jit(solution)/shard_map/ppermute | solution.py:331
  24.6 1.2 %collective-permute-done.10.refs_6_ = bf16[16,3712]{1,0:T(8,128)(2,1)S(1)} collective-permute-done((bf16[16,3712]{1,0:T(8,128)(2,1)S(1)}, bf16[16,3712]{1,0:T(8,128)(2,1)S(1)}, u32[]{:S(2)}, u32[]{:S(2)}) %collective-permute-start.10) | collective-permute-done | bytes 118816 | tf_op jit(solution)/shard_map/ppermute | solution.py:331
  25.8 3.4 %away.1 = (bf16[128,3584]{1,0:T(8,128)(2,1)S(1)}, bf16[128,1024]{1,0:T(8,128)(2,1)S(1)}, f32[128,128]{1,0:T(8,128)S(1)}) custom-call(bf16[1,1024,3584]{2,1,0:T(8,128)(2,1)S(1)} %bitcast.3, bf16[128,1024]{1,0:T(8,128)(2,1)S(1)} %get-tuple-element.33.refs_0_, f32[128,128]{1,0:T(8,128)S(1)} %get-tuple-element.34.refs_3_.refs_1_, ...), custom_call_target="tpu_custom_call" | custom-call | flops 2818572288 | tf_op jit(solution)/shard_map/away/pallas_call | solution.py:267
  29.3 0.2 collective-permute-start.11
  29.5 1.1 %here.1.here_ref = bf16[128,3584]{1,0:T(8,128)(2,1)S(1)} custom-call(bf16[1,1024,3584]{2,1,0:T(8,128)(2,1)S(1)} %bitcast.3, bf16[128,1024]{1,0:T(8,128)(2,1)S(1)} %get-tuple-element.39.hidden_ref, f32[128,128]{1,0:T(8,128)S(1)} %get-tuple-element.40.share_ref), custom_call_target="tpu_custom_call" | custom-call | flops 939524096 | tf_op jit(solution)/shard_map/here/pallas_call | solution.py:288
  30.7 1.1 %collective-permute-done.11.got_ref = bf16[128,3584]{1,0:T(8,128)(2,1)S(1)} collective-permute-done((bf16[128,3584]{1,0:T(8,128)(2,1)S(1)}, bf16[128,3584]{1,0:T(8,128)(2,1)S(1)}, u32[]{:S(2)}, u32[]{:S(2)}) %collective-permute-start.11) | collective-permute-done | bytes 917536 | tf_op jit(solution)/shard_map/ppermute | solution.py:331
  31.8 0.2 add.43
  32.0 0.5 %collective-permute-start.14 = (bf16[16,5376]{1,0:T(8,128)(2,1)S(1)}, bf16[16,5376]{1,0:T(8,128)(2,1)S(1)}, u32[]{:S(2)}, u32[]{:S(2)}) collective-permute-start(bf16[16,5376]{1,0:T(8,128)(2,1)S(1)} %get-tuple-element.44), channel_id=1, source_target_pairs={{0,2},{1,3},{2,0},{3,1},{4,6},{5,7},{6,4},{7,5},{8,10},{9,11},{10,... | collective-permute-start | bytes 516104 | tf_op jit(solution)/shard_map/ppermute | solution.py:331
  32.5 1.9 %collective-permute-start.18 = (bf16[16,1792]{1,0:T(8,128)(2,1)S(1)}, bf16[16,1792]{1,0:T(8,128)(2,1)S(1)}, u32[]{:S(2)}, u32[]{:S(2)}) collective-permute-start(bf16[16,1792]{1,0:T(8,128)(2,1)S(1)} %get-tuple-element.49), channel_id=1, source_target_pairs={{0,8},{1,9},{2,10},{3,11},{4,12},{5,13},{6,14},{7,15},{8,0},{9,1},... | collective-permute-start | bytes 172040 | tf_op jit(solution)/shard_map/ppermute | solution.py:331
  34.4 2.0 %collective-permute-start.19 = (bf16[16,1792]{1,0:T(8,128)(2,1)S(1)}, bf16[16,1792]{1,0:T(8,128)(2,1)S(1)}, u32[]{:S(2)}, u32[]{:S(2)}) collective-permute-start(bf16[16,1792]{1,0:T(8,128)(2,1)S(1)} %get-tuple-element.50), channel_id=1, source_target_pairs={{0,10},{1,11},{2,8},{3,9},{4,14},{5,15},{6,12},{7,13},{8,2},{9,3},... | collective-permute-start | bytes 172040 | tf_op jit(solution)/shard_map/ppermute | solution.py:331
  36.5 1.9 %collective-permute-start.13 = (bf16[16,3584]{1,0:T(8,128)(2,1)S(1)}, bf16[16,3584]{1,0:T(8,128)(2,1)S(1)}, u32[]{:S(2)}, u32[]{:S(2)}) collective-permute-start(bf16[16,3584]{1,0:T(8,128)(2,1)S(1)} %get-tuple-element.43), channel_id=1, source_target_pairs={{0,6},{1,7},{2,4},{3,5},{4,2},{5,3},{6,0},{7,1},{8,14},{9,15},{10,... | collective-permute-start | bytes 344072 | tf_op jit(solution)/shard_map/ppermute | solution.py:331
  38.4 0.2 collective-permute-done.14.got_ref
  38.6 1.4 %collective-permute-start.16 = (bf16[16,3584]{1,0:T(8,128)(2,1)S(1)}, bf16[16,3584]{1,0:T(8,128)(2,1)S(1)}, u32[]{:S(2)}, u32[]{:S(2)}) collective-permute-start(bf16[16,3584]{1,0:T(8,128)(2,1)S(1)} %get-tuple-element.47), channel_id=1, source_target_pairs={{0,2},{1,3},{2,0},{3,1},{4,6},{5,7},{6,4},{7,5},{8,10},{9,11},{10,... | collective-permute-start | bytes 344072 | tf_op jit(solution)/shard_map/ppermute | solution.py:331
  40.0 1.9 %collective-permute-start.17 = (bf16[16,1792]{1,0:T(8,128)(2,1)S(1)}, bf16[16,1792]{1,0:T(8,128)(2,1)S(1)}, u32[]{:S(2)}, u32[]{:S(2)}) collective-permute-start(bf16[16,1792]{1,0:T(8,128)(2,1)S(1)} %get-tuple-element.48), channel_id=1, source_target_pairs={{0,8},{1,9},{2,10},{3,11},{4,12},{5,13},{6,14},{7,15},{8,0},{9,1},... | collective-permute-start | bytes 172040 | tf_op jit(solution)/shard_map/ppermute | solution.py:331
  41.9 1.8 %collective-permute-start.15 = (bf16[16,3584]{1,0:T(8,128)(2,1)S(1)}, bf16[16,3584]{1,0:T(8,128)(2,1)S(1)}, u32[]{:S(2)}, u32[]{:S(2)}) collective-permute-start(bf16[16,3584]{1,0:T(8,128)(2,1)S(1)} %get-tuple-element.46), channel_id=1, source_target_pairs={{0,12},{1,13},{2,14},{3,15},{4,8},{5,9},{6,10},{7,11},{8,4},{9,5},... | collective-permute-start | bytes 344072 | tf_op jit(solution)/shard_map/ppermute | solution.py:331
  43.8 1.7 %collective-permute-done.17 = bf16[16,1792]{1,0:T(8,128)(2,1)S(1)} collective-permute-done((bf16[16,1792]{1,0:T(8,128)(2,1)S(1)}, bf16[16,1792]{1,0:T(8,128)(2,1)S(1)}, u32[]{:S(2)}, u32[]{:S(2)}) %collective-permute-start.17) | collective-permute-done | bytes 57376 | tf_op jit(solution)/shard_map/ppermute | solution.py:331
  45.5 1.0 %collective-permute-done.13 = bf16[16,3584]{1,0:T(8,128)(2,1)S(1)} collective-permute-done((bf16[16,3584]{1,0:T(8,128)(2,1)S(1)}, bf16[16,3584]{1,0:T(8,128)(2,1)S(1)}, u32[]{:S(2)}, u32[]{:S(2)}) %collective-permute-start.13) | collective-permute-done | bytes 114720 | tf_op jit(solution)/shard_map/ppermute | solution.py:331
  46.5 2.1 %collective-permute-done.15 = bf16[16,3584]{1,0:T(8,128)(2,1)S(1)} collective-permute-done((bf16[16,3584]{1,0:T(8,128)(2,1)S(1)}, bf16[16,3584]{1,0:T(8,128)(2,1)S(1)}, u32[]{:S(2)}, u32[]{:S(2)}) %collective-permute-start.15) | collective-permute-done | bytes 114720 | tf_op jit(solution)/shard_map/ppermute | solution.py:331
  48.6 0.7 %fusion.1 = bf16[16,3584]{1,0:T(8,128)(2,1)} fusion(f32[16,1792]{1,0:T(8,128)S(1)} %convert_add_fusion, f32[16,1792]{1,0:T(8,128)S(1)} %convert_element_type.36, bf16[16,3584]{1,0:T(8,128)(2,1)S(1)} %collective-permute-done.16, bf16[16,3584]{1,0:T(8,128)(2,1)S(1)} %collective-permute-done.15, bf16[16,3584]{1,0:T(8,128)(2,1)S(1)} %collective-permute-done.13, ...), kind=kLoop, calls=%fused_computation.2 | loop fusion | flops 802816 | bytes 1032192 | tf_op jit(solution)/shard_map/convert_element_type | solution.py:405
  (30 shorter events, 0.4 us)
Async XLA Ops:
  1.1 10.0 %collective-permute-start.1 = (bf16[16,3712]{1,0:T(8,128)(2,1)S(1)}, bf16[16,3712]{1,0:T(8,128)(2,1)S(1)}, u32[]{:S(2)}, u32[]{:S(2)}) collective-permute-start(bf16[16,3712]{1,0:T(8,128)(2,1)S(1)} %norm.1.refs_0_), channel_id=1, source_target_pairs={{0,12},{1,13},{2,14},{3,15},{4,8},{5,9},{6,10},{7,11},{8,4},{9,5},... | collective-permute-start | bytes 356360 | tf_op jit(solution)/shard_map/ppermute | solution.py:331
  6.2 11.8 %collective-permute-start = (bf16[16,3712]{1,0:T(8,128)(2,1)S(1)}, bf16[16,3712]{1,0:T(8,128)(2,1)S(1)}, u32[]{:S(2)}, u32[]{:S(2)}) collective-permute-start(bf16[16,3712]{1,0:T(8,128)(2,1)S(1)} %norm.1.refs_0_), channel_id=1, source_target_pairs={{0,2},{1,3},{2,0},{3,1},{4,6},{5,7},{6,4},{7,5},{8,10},{9,11},{10,... | collective-permute-start | bytes 356360 | tf_op jit(solution)/shard_map/ppermute | solution.py:331
  11.1 7.0 %collective-permute-start.3 = (bf16[16,3712]{1,0:T(8,128)(2,1)S(1)}, bf16[16,3712]{1,0:T(8,128)(2,1)S(1)}, u32[]{:S(2)}, u32[]{:S(2)}) collective-permute-start(bf16[16,3712]{1,0:T(8,128)(2,1)S(1)} %join.5.refs_0_), channel_id=1, source_target_pairs={{0,8},{1,9},{2,10},{3,11},{4,12},{5,13},{6,14},{7,15},{8,0},{9,1},... | collective-permute-start | bytes 356360 | tf_op jit(solution)/shard_map/ppermute | solution.py:331
  11.2 6.9 %collective-permute-start.2 = (bf16[16,3712]{1,0:T(8,128)(2,1)S(1)}, bf16[16,3712]{1,0:T(8,128)(2,1)S(1)}, u32[]{:S(2)}, u32[]{:S(2)}) collective-permute-start(bf16[16,3712]{1,0:T(8,128)(2,1)S(1)} %collective-permute-done.1.refs_2_), channel_id=1, source_target_pairs={{0,2},{1,3},{2,0},{3,1},{4,6},{5,7},{6,4},{7,5},{8,10},{9,11},{10,... | collective-permute-start | bytes 356360 | tf_op jit(solution)/shard_map/ppermute | solution.py:331
  11.7 8.7 %collective-permute-start.5 = (bf16[16,3712]{1,0:T(8,128)(2,1)S(1)}, bf16[16,3712]{1,0:T(8,128)(2,1)S(1)}, u32[]{:S(2)}, u32[]{:S(2)}) collective-permute-start(bf16[16,3712]{1,0:T(8,128)(2,1)S(1)} %join.5.refs_0_), channel_id=1, source_target_pairs={{0,6},{1,7},{2,4},{3,5},{4,2},{5,3},{6,0},{7,1},{8,14},{9,15},{10,... | collective-permute-start | bytes 356360 | tf_op jit(solution)/shard_map/ppermute | solution.py:331
  13.4 8.5 %collective-permute-start.4 = (bf16[16,3712]{1,0:T(8,128)(2,1)S(1)}, bf16[16,3712]{1,0:T(8,128)(2,1)S(1)}, u32[]{:S(2)}, u32[]{:S(2)}) collective-permute-start(bf16[16,3712]{1,0:T(8,128)(2,1)S(1)} %join.5.refs_0_), channel_id=1, source_target_pairs={{0,4},{1,5},{2,6},{3,7},{4,0},{5,1},{6,2},{7,3},{8,12},{9,13},{10,... | collective-permute-start | bytes 356360 | tf_op jit(solution)/shard_map/ppermute | solution.py:331
  18.0 7.8 %slice-start = ((s8[7340032]{0:T(1024)(128)(4,1)}), s8[4194304]{0:T(1024)(128)(4,1)S(1)}, s32[]{:S(2)}) async-start(s8[7340032]{0:T(1024)(128)(4,1)} %bitcast.2), calls=%async_computation | async-start | bytes 8388608
  18.1 5.9 %collective-permute-start.8 = (bf16[16,3712]{1,0:T(8,128)(2,1)S(1)}, bf16[16,3712]{1,0:T(8,128)(2,1)S(1)}, u32[]{:S(2)}, u32[]{:S(2)}) collective-permute-start(bf16[16,3712]{1,0:T(8,128)(2,1)S(1)} %get-tuple-element.35), channel_id=1, source_target_pairs={{0,2},{1,3},{2,0},{3,1},{4,6},{5,7},{6,4},{7,5},{8,10},{9,11},{10,... | collective-permute-start | bytes 356360 | tf_op jit(solution)/shard_map/ppermute | solution.py:331
  18.7 5.9 %collective-permute-start.6 = (bf16[48,3712]{1,0:T(8,128)(2,1)S(1)}, bf16[48,3712]{1,0:T(8,128)(2,1)S(1)}, u32[]{:S(2)}, u32[]{:S(2)}) collective-permute-start(bf16[48,3712]{1,0:T(8,128)(2,1)S(1)} %join.4.refs_0_), channel_id=1, source_target_pairs={{0,1},{1,0},{2,3},{3,2},{4,5},{5,4},{6,7},{7,6},{8,9},{9,8},{10,11... | collective-permute-start | bytes 1069064 | tf_op jit(solution)/shard_map/ppermute | solution.py:331
  18.7 7.1 %collective-permute-start.7 = (bf16[32,3712]{1,0:T(8,128)(2,1)S(1)}, bf16[32,3712]{1,0:T(8,128)(2,1)S(1)}, u32[]{:S(2)}, u32[]{:S(2)}) collective-permute-start(bf16[32,3712]{1,0:T(8,128)(2,1)S(1)} %get-tuple-element.30.refs_1_), channel_id=1, source_target_pairs={{0,1},{1,0},{2,3},{3,2},{4,5},{5,4},{6,7},{7,6},{8,9},{9,8},{10,11... | collective-permute-start | bytes 712712 | tf_op jit(solution)/shard_map/ppermute | solution.py:331
  21.8 4.0 %slice-start.1 = ((s8[7340032]{0:T(1024)(128)(4,1)}), s8[3145728]{0:T(1024)(128)(4,1)S(1)}, s32[]{:S(2)}) async-start(s8[7340032]{0:T(1024)(128)(4,1)} %bitcast.2), calls=%async_computation.1 | async-start | bytes 6291456
  24.1 1.7 %collective-permute-start.9 = (bf16[32,3712]{1,0:T(8,128)(2,1)S(1)}, bf16[32,3712]{1,0:T(8,128)(2,1)S(1)}, u32[]{:S(2)}, u32[]{:S(2)}) collective-permute-start(bf16[32,3712]{1,0:T(8,128)(2,1)S(1)} %get-tuple-element.36), channel_id=1, source_target_pairs={{0,1},{1,0},{2,3},{3,2},{4,5},{5,4},{6,7},{7,6},{8,9},{9,8},{10,11... | collective-permute-start | bytes 712712 | tf_op jit(solution)/shard_map/ppermute | solution.py:331
  24.1 1.7 %collective-permute-start.10 = (bf16[16,3712]{1,0:T(8,128)(2,1)S(1)}, bf16[16,3712]{1,0:T(8,128)(2,1)S(1)}, u32[]{:S(2)}, u32[]{:S(2)}) collective-permute-start(bf16[16,3712]{1,0:T(8,128)(2,1)S(1)} %get-tuple-element.37.refs_5_), channel_id=1, source_target_pairs={{0,1},{1,0},{2,3},{3,2},{4,5},{5,4},{6,7},{7,6},{8,9},{9,8},{10,11... | collective-permute-start | bytes 356360 | tf_op jit(solution)/shard_map/ppermute | solution.py:331
  29.3 19.4 %copy-start = (bf16[16,3584]{1,0:T(8,128)(2,1)S(1)}, bf16[16,3584]{1,0:T(8,128)(2,1)}, u32[]{:S(2)}) copy-start(bf16[16,3584]{1,0:T(8,128)(2,1)} %refs_0_.1) | copy-start | bytes 344068
  29.3 2.5 %collective-permute-start.11 = (bf16[128,3584]{1,0:T(8,128)(2,1)S(1)}, bf16[128,3584]{1,0:T(8,128)(2,1)S(1)}, u32[]{:S(2)}, u32[]{:S(2)}) collective-permute-start(bf16[128,3584]{1,0:T(8,128)(2,1)S(1)} %get-tuple-element.38), channel_id=1, source_target_pairs={{0,1},{1,0},{2,3},{3,2},{4,5},{5,4},{6,7},{7,6},{8,9},{9,8},{10,11... | collective-permute-start | bytes 2752520 | tf_op jit(solution)/shard_map/ppermute | solution.py:331
  32.0 6.6 %collective-permute-start.14 = (bf16[16,5376]{1,0:T(8,128)(2,1)S(1)}, bf16[16,5376]{1,0:T(8,128)(2,1)S(1)}, u32[]{:S(2)}, u32[]{:S(2)}) collective-permute-start(bf16[16,5376]{1,0:T(8,128)(2,1)S(1)} %get-tuple-element.44), channel_id=1, source_target_pairs={{0,2},{1,3},{2,0},{3,1},{4,6},{5,7},{6,4},{7,5},{8,10},{9,11},{10,... | collective-permute-start | bytes 516104 | tf_op jit(solution)/shard_map/ppermute | solution.py:331
  32.5 7.5 %collective-permute-start.18 = (bf16[16,1792]{1,0:T(8,128)(2,1)S(1)}, bf16[16,1792]{1,0:T(8,128)(2,1)S(1)}, u32[]{:S(2)}, u32[]{:S(2)}) collective-permute-start(bf16[16,1792]{1,0:T(8,128)(2,1)S(1)} %get-tuple-element.49), channel_id=1, source_target_pairs={{0,8},{1,9},{2,10},{3,11},{4,12},{5,13},{6,14},{7,15},{8,0},{9,1},... | collective-permute-start | bytes 172040 | tf_op jit(solution)/shard_map/ppermute | solution.py:331
  34.4 7.5 %collective-permute-start.19 = (bf16[16,1792]{1,0:T(8,128)(2,1)S(1)}, bf16[16,1792]{1,0:T(8,128)(2,1)S(1)}, u32[]{:S(2)}, u32[]{:S(2)}) collective-permute-start(bf16[16,1792]{1,0:T(8,128)(2,1)S(1)} %get-tuple-element.50), channel_id=1, source_target_pairs={{0,10},{1,11},{2,8},{3,9},{4,14},{5,15},{6,12},{7,13},{8,2},{9,3},... | collective-permute-start | bytes 172040 | tf_op jit(solution)/shard_map/ppermute | solution.py:331
  36.5 9.0 %collective-permute-start.12 = (bf16[16,3584]{1,0:T(8,128)(2,1)S(1)}, bf16[16,3584]{1,0:T(8,128)(2,1)S(1)}, u32[]{:S(2)}, u32[]{:S(2)}) collective-permute-start(bf16[16,3584]{1,0:T(8,128)(2,1)S(1)} %get-tuple-element.42), channel_id=1, source_target_pairs={{0,4},{1,5},{2,6},{3,7},{4,0},{5,1},{6,2},{7,3},{8,12},{9,13},{10,... | collective-permute-start | bytes 344072 | tf_op jit(solution)/shard_map/ppermute | solution.py:331
  36.5 10.0 %collective-permute-start.13 = (bf16[16,3584]{1,0:T(8,128)(2,1)S(1)}, bf16[16,3584]{1,0:T(8,128)(2,1)S(1)}, u32[]{:S(2)}, u32[]{:S(2)}) collective-permute-start(bf16[16,3584]{1,0:T(8,128)(2,1)S(1)} %get-tuple-element.43), channel_id=1, source_target_pairs={{0,6},{1,7},{2,4},{3,5},{4,2},{5,3},{6,0},{7,1},{8,14},{9,15},{10,... | collective-permute-start | bytes 344072 | tf_op jit(solution)/shard_map/ppermute | solution.py:331
  38.6 7.9 %collective-permute-start.16 = (bf16[16,3584]{1,0:T(8,128)(2,1)S(1)}, bf16[16,3584]{1,0:T(8,128)(2,1)S(1)}, u32[]{:S(2)}, u32[]{:S(2)}) collective-permute-start(bf16[16,3584]{1,0:T(8,128)(2,1)S(1)} %get-tuple-element.47), channel_id=1, source_target_pairs={{0,2},{1,3},{2,0},{3,1},{4,6},{5,7},{6,4},{7,5},{8,10},{9,11},{10,... | collective-permute-start | bytes 344072 | tf_op jit(solution)/shard_map/ppermute | solution.py:331
  40.0 5.5 %collective-permute-start.17 = (bf16[16,1792]{1,0:T(8,128)(2,1)S(1)}, bf16[16,1792]{1,0:T(8,128)(2,1)S(1)}, u32[]{:S(2)}, u32[]{:S(2)}) collective-permute-start(bf16[16,1792]{1,0:T(8,128)(2,1)S(1)} %get-tuple-element.48), channel_id=1, source_target_pairs={{0,8},{1,9},{2,10},{3,11},{4,12},{5,13},{6,14},{7,15},{8,0},{9,1},... | collective-permute-start | bytes 172040 | tf_op jit(solution)/shard_map/ppermute | solution.py:331
  41.9 6.7 %collective-permute-start.15 = (bf16[16,3584]{1,0:T(8,128)(2,1)S(1)}, bf16[16,3584]{1,0:T(8,128)(2,1)S(1)}, u32[]{:S(2)}, u32[]{:S(2)}) collective-permute-start(bf16[16,3584]{1,0:T(8,128)(2,1)S(1)} %get-tuple-element.46), channel_id=1, source_target_pairs={{0,12},{1,13},{2,14},{3,15},{4,8},{5,9},{6,10},{7,11},{8,4},{9,5},... | collective-permute-start | bytes 344072 | tf_op jit(solution)/shard_map/ppermute | solution.py:331
